TPU v7x, 32 devices: a whole 2x2x4 slice. The times are simulated.
32 devices in a mesh: region: 2 (over y), user: 4 (over x, core), item: 4 (over z).
Axes of the slice: x: 2, y: 2, z: 4, core: 2. Of those that a mesh axis runs over, the one named last changes fastest.
Arguments:
- user_emb: bfloat16 [65536, 128], P(('region', 'user')), parts along dimension 0, may hold values from -1.05 to 1.05
- item_emb: bfloat16 [65536, 128], P(('region', 'item')), parts along dimension 0, may hold values from -1.05 to 1.05
- user_count: int32 [65536], P(('region', 'user')), parts along dimension 0, may hold values from 1 to 60, as said below
- item_count: int32 [65536], P(('region', 'item')), parts along dimension 0, may hold values from 1 to 60, as said below
- tiles: int32 [8, 4, 5, 2], P(('region', 'user'), 'item'), parts along dimension 0, may hold values from 0 to 15, as said below
- tile_count: int32 [8, 4], P(('region', 'user'), 'item'), parts along dimension 0, may hold values from 4 to 5, as said below
Outputs:
- user_potential: float32 [65536], P(('region', 'user')), parts along dimension 0
- item_potential: float32 [65536], P(('region', 'item')), parts along dimension 0
There are 2 independent parts, one for each index of `region`. A program takes and returns all parts, laid end to end along the dimension named above; each array names one. Nothing has to cross between parts.
Inputs may be any that keep to these rules, and one draw needn't show every extreme that they name: `tiles`: on the device in user row p and item column q, slot j names a user cluster of that device's user shard and an item cluster of its item shard by local numbers; no pair stands twice on a device. For j < 4 the slot pairs user cluster (q * 4 + j) mod 16 with item cluster (p * 4 + j) mod 16. `tile_count`: the slots in use are the leading ones; the first device uses all 5. `user_count`: positive counts. `item_count`: positive counts.
All inputs are finite; a program needn't handle non-finite values.
Results may differ from a plain program's by a relative error of at most 0.0003.
Values sent between devices are 32-bit elements; how exact they have to be, the bound alone decides.
No kernel may reach another device: no remote copies, remote signals or barrier semaphores. Data moves between devices by JAX's collectives and lax.ppermute only.
A program may use at most 64 MiB of HBM per device.

v0:
```python
import jax
import jax.numpy as jnp
from jax import lax
from jax.sharding import PartitionSpec as P

CLUSTER = 512
ITERS = 3


entropy = 0.25
lowest = -1e30


def visit(update, carry, filled, total_slots):
    for position in range(total_slots):
        renewed = update(carry, position)
        carry = jnp.where(position < filled, renewed, carry)
    return carry


def visit_keep(update, top_state, stack, filled, total_slots):
    for position in range(total_slots):
        renewed, stack = update(top_state, stack, position)
        top_state = jnp.where(position < filled, renewed, top_state)
    return (top_state, stack)


def block_scores(row_table, col_table, col_values, row_groups, col_groups, position):
    row_start = row_groups[position] * CLUSTER
    col_start = col_groups[position] * CLUSTER
    row_block = lax.dynamic_slice_in_dim(row_table, row_start, CLUSTER, 0)
    col_block = lax.dynamic_slice_in_dim(col_table, col_start, CLUSTER, 0)
    shifts = lax.dynamic_slice_in_dim(col_values, col_start, CLUSTER, 0)
    products = lax.dot_general(
        row_block, col_block, (((1,), (1,)), ((), ())), preferred_element_type=jnp.float32
    )
    return (row_start, (products + shifts[None, :]) / entropy)


def potential(
    row_table, col_table, col_values, row_groups, col_groups, filled, log_share, along_items
):
    rows_here = row_table.shape[0]
    total_slots = row_groups.shape[0]

    def raise_top(top_state, stack, position):
        row_start, scores = block_scores(
            row_table, col_table, col_values, row_groups, col_groups, position
        )
        old_top = lax.dynamic_slice_in_dim(top_state, row_start, CLUSTER, 0)
        top_state = lax.dynamic_update_slice_in_dim(
            top_state, jnp.maximum(old_top, jnp.max(scores, axis=1)), row_start, 0
        )
        stack = lax.dynamic_update_index_in_dim(stack, scores, position, 0)
        return (top_state, stack)

    empty_stack = jnp.zeros((total_slots, CLUSTER, CLUSTER), jnp.float32)
    top_local, kept = visit_keep(
        raise_top, jnp.full((rows_here,), lowest, jnp.float32), empty_stack, filled, total_slots
    )
    if along_items:
        top_rows = lax.pmax(top_local, "item")
    else:
        top_rows = lax.pmax(top_local, "user")

    def add_mass(mass_state, position):
        row_start = row_groups[position] * CLUSTER
        scores = lax.dynamic_index_in_dim(kept, position, 0, keepdims=False)
        anchor = lax.dynamic_slice_in_dim(top_rows, row_start, CLUSTER, 0)
        old_mass = lax.dynamic_slice_in_dim(mass_state, row_start, CLUSTER, 0)
        fresh_mass = old_mass + jnp.sum(jnp.exp(scores - anchor[:, None]), axis=1)
        return lax.dynamic_update_slice_in_dim(mass_state, fresh_mass, row_start, 0)

    mass_local = visit(add_mass, jnp.zeros((rows_here,), jnp.float32), filled, total_slots)
    if along_items:
        mass_rows = lax.psum(mass_local, "item")
    else:
        mass_rows = lax.psum(mass_local, "user")
    return entropy * (log_share - (top_rows + jnp.log(mass_rows)))


def body(user_emb, item_emb, user_count, item_count, tiles, tile_count):
    user_counts = user_count.astype(jnp.float32)
    item_counts = item_count.astype(jnp.float32)
    user_total = lax.psum(jnp.sum(user_counts), "user")
    item_total = lax.psum(jnp.sum(item_counts), "item")
    log_users = jnp.log(user_counts / user_total)
    log_items = jnp.log(item_counts / item_total)
    slot_table = tiles[0, 0]
    user_groups = slot_table[:, 0]
    item_groups = slot_table[:, 1]
    filled = tile_count[0, 0]
    item_values = jnp.zeros((item_emb.shape[0],), jnp.float32)
    user_values = jnp.zeros((user_emb.shape[0],), jnp.float32)
    for iteration in range(ITERS):
        user_values = potential(
            user_emb, item_emb, item_values, user_groups, item_groups, filled, log_users, True
        )
        item_values = potential(
            item_emb, user_emb, user_values, item_groups, user_groups, filled, log_items, False
        )
    return (user_values, item_values)


def solution(mesh):
    in_specs = (
        P(("region", "user"), None),
        P(("region", "item"), None),
        P(("region", "user")),
        P(("region", "item")),
        P(("region", "user"), "item", None, None),
        P(("region", "user"), "item"),
    )
    out_specs = (P(("region", "user")), P(("region", "item")))
    return jax.shard_map(body, mesh=mesh, in_specs=in_specs, out_specs=out_specs, check_vma=False)
```

profile of v0, /device:TPU:0, one launch (start us, length us, event | category | flops | bytes accessed | tf_op | source)
XLA Modules:
  0.0 260.5 jit_solution(10496632806128311927)
XLA Ops:
  0.6 1.7 fusion.124
  3.7 1.2 multiply_reduce_fusion.4
  7.0 2.2 multiply_reduce_fusion.3
  10.6 2.2 multiply_reduce_fusion.2
  14.2 2.2 multiply_reduce_fusion.1
  17.9 2.2 multiply_reduce_fusion
  20.2 20.7 %pmax.42 = f32[8192]{0:T(1024)S(1)} all-reduce(f32[8192]{0:T(1024)S(1)} %fusion.68), channel_id=1, replica_groups=mesh['region'=2,'user'=4,'item'=4] {'item'}, use_global_device_ids=true, to_apply=%region_9.10 | all-reduce | flops 8192 | bytes 65536 | tf_op jit(solution)/shard_map/pmax | solution.py:62
  41.1 2.0 exponential_reduce_fusion.25
  45.1 17.2 %all-reduce = (f32[8192]{0:T(1024)S(1)}, f32[]{:T(128)}) all-reduce(f32[8192]{0:T(1024)S(1)} %fusion.72, f32[]{:T(128)} %convert_reduce_fusion), channel_id=1, replica_groups=mesh['region'=2,'user'=4,'item'=4] {'item'}, use_global_device_ids=true, to_apply=%region_15.16 | all-reduce | flops 8193 | bytes 65544 | tf_op jit(solution)/shard_map/psum | solution.py:76
  63.0 6.3 %psum.56 = f32[]{:T(128)} all-reduce(f32[]{:T(128)} %convert_reduce_fusion.1), channel_id=1, replica_groups=mesh['region'=2,'user'=4,'item'=4] {'user'}, use_global_device_ids=true, to_apply=%region_1.0 | all-reduce | flops 1 | bytes 8 | tf_op jit(solution)/shard_map/psum | solution.py:85
  70.0 2.2 fusion
  72.3 2.2 fusion.1
  74.7 2.2 fusion.2
  77.0 2.2 fusion.3
  79.4 2.3 fusion.4
  81.9 11.1 %pmax.43 = f32[8192]{0:T(1024)S(1)} all-reduce(f32[8192]{0:T(1024)S(1)} %fusion.76), channel_id=1, replica_groups=mesh['region'=2,'user'=4,'item'=4] {'user'}, use_global_device_ids=true, to_apply=%region_21.22 | all-reduce | flops 8192 | bytes 65536 | tf_op jit(solution)/shard_map/pmax | solution.py:64
  93.1 1.7 exponential_reduce_fusion.20
  94.8 1.5 exponential_reduce_fusion.21
  98.0 10.3 %psum.59 = f32[8192]{0:T(1024)S(1)} all-reduce(f32[8192]{0:T(1024)S(1)} %fusion.80), channel_id=1, replica_groups=mesh['region'=2,'user'=4,'item'=4] {'user'}, use_global_device_ids=true, to_apply=%region_27.28 | all-reduce | flops 8192 | bytes 65536 | tf_op jit(solution)/shard_map/psum | solution.py:78
  108.3 0.8 subtract_multiply_fusion.4
  109.2 1.4 fusion.9
  110.6 1.4 fusion.8
  113.4 17.5 %pmax.44 = f32[8192]{0:T(1024)S(1)} all-reduce(f32[8192]{0:T(1024)S(1)} %fusion.84), channel_id=1, replica_groups=mesh['region'=2,'user'=4,'item'=4] {'item'}, use_global_device_ids=true, to_apply=%region_33.34 | all-reduce | flops 8192 | bytes 65536 | tf_op jit(solution)/shard_map/pmax | solution.py:62
  131.0 1.6 exponential_reduce_fusion.15
  132.6 1.5 exponential_reduce_fusion.16
  135.8 15.8 %psum.60 = f32[8192]{0:T(1024)S(1)} all-reduce(f32[8192]{0:T(1024)S(1)} %fusion.88), channel_id=1, replica_groups=mesh['region'=2,'user'=4,'item'=4] {'item'}, use_global_device_ids=true, to_apply=%region_39.40 | all-reduce | flops 8192 | bytes 65536 | tf_op jit(solution)/shard_map/psum | solution.py:76
  151.6 0.8 subtract_multiply_fusion.3
  152.6 1.5 fusion.14
  154.1 1.4 fusion.13
  156.8 10.3 %pmax.45 = f32[8192]{0:T(1024)S(1)} all-reduce(f32[8192]{0:T(1024)S(1)} %fusion.92), channel_id=1, replica_groups=mesh['region'=2,'user'=4,'item'=4] {'user'}, use_global_device_ids=true, to_apply=%region_45.46 | all-reduce | flops 8192 | bytes 65536 | tf_op jit(solution)/shard_map/pmax | solution.py:64
  167.2 1.7 exponential_reduce_fusion.10
  168.9 1.5 exponential_reduce_fusion.11
  172.1 10.3 %psum.61 = f32[8192]{0:T(1024)S(1)} all-reduce(f32[8192]{0:T(1024)S(1)} %fusion.96), channel_id=1, replica_groups=mesh['region'=2,'user'=4,'item'=4] {'user'}, use_global_device_ids=true, to_apply=%region_51.52 | all-reduce | flops 8192 | bytes 65536 | tf_op jit(solution)/shard_map/psum | solution.py:78
  183.3 1.4 fusion.19
  184.7 1.4 fusion.18
  187.4 17.5 %pmax.46 = f32[8192]{0:T(1024)S(1)} all-reduce(f32[8192]{0:T(1024)S(1)} %fusion.100), channel_id=1, replica_groups=mesh['region'=2,'user'=4,'item'=4] {'item'}, use_global_device_ids=true, to_apply=%region_57.58 | all-reduce | flops 8192 | bytes 65536 | tf_op jit(solution)/shard_map/pmax | solution.py:62
  205.1 1.6 exponential_reduce_fusion.5
  206.7 1.5 exponential_reduce_fusion.6
  209.9 16.0 %psum.62 = f32[8192]{0:T(1024)S(1)} all-reduce(f32[8192]{0:T(1024)S(1)} %fusion.104), channel_id=1, replica_groups=mesh['region'=2,'user'=4,'item'=4] {'item'}, use_global_device_ids=true, to_apply=%region_63.64 | all-reduce | flops 8192 | bytes 65536 | tf_op jit(solution)/shard_map/psum | solution.py:76
  226.7 1.5 fusion.24
  228.2 1.4 fusion.23
  229.6 1.4 fusion.22
  231.0 1.4 fusion.21
  233.4 10.3 %pmax.47 = f32[8192]{0:T(1024)S(1)} all-reduce(f32[8192]{0:T(1024)S(1)} %fusion.108), channel_id=1, replica_groups=mesh['region'=2,'user'=4,'item'=4] {'user'}, use_global_device_ids=true, to_apply=%region_69.70 | all-reduce | flops 8192 | bytes 65536 | tf_op jit(solution)/shard_map/pmax | solution.py:64
  243.8 1.6 exponential_reduce_fusion
  245.4 1.5 exponential_reduce_fusion.1
  248.6 10.6 %psum.63 = f32[8192]{0:T(1024)S(1)} all-reduce(f32[8192]{0:T(1024)S(1)} %fusion.112), channel_id=1, replica_groups=mesh['region'=2,'user'=4,'item'=4] {'user'}, use_global_device_ids=true, to_apply=%region_75.76 | all-reduce | flops 8192 | bytes 65536 | tf_op jit(solution)/shard_map/psum | solution.py:78
  259.3 1.3 subtract_multiply_fusion
  (167 shorter events, 20.6 us)
Async XLA Ops:
  0.6 3.0 %copy-start = (bf16[8192,128]{1,0:T(8,128)(2,1)S(1)}, bf16[8192,128]{1,0:T(8,128)(2,1)}, u32[]{:S(2)}) copy-start(bf16[8192,128]{1,0:T(8,128)(2,1)} %param.7) | copy-start | bytes 6291460
  41.0 2.2 copy-start.1
  41.0 2.2 copy-start.6
  43.1 1.4 copy-start.24
  43.1 19.2 %copy-start.23 = (s32[8192]{0:T(1024)S(1)}, s32[8192]{0:T(1024)}, u32[]{:S(2)}) copy-start(s32[8192]{0:T(1024)} %param.8) | copy-start | bytes 98308
  93.0 3.3 %copy-start.19 = (f32[512,512]{0,1:T(8,128)S(1)}, f32[512,512]{0,1:T(8,128)}, u32[]{:S(2)}) copy-start(f32[512,512]{0,1:T(8,128)} %get-tuple-element.84) | copy-start | bytes 3145732
  93.0 3.6 %copy-start.15 = (f32[512,512]{0,1:T(8,128)S(1)}, f32[512,512]{0,1:T(8,128)}, u32[]{:S(2)}) copy-start(f32[512,512]{0,1:T(8,128)} %get-tuple-element.82) | copy-start | bytes 3145732
  93.1 3.8 %copy-start.11 = (f32[512,512]{0,1:T(8,128)S(1)}, f32[512,512]{0,1:T(8,128)}, u32[]{:S(2)}) copy-start(f32[512,512]{0,1:T(8,128)} %get-tuple-element.80) | copy-start | bytes 3145732
  108.3 3.7 %copy-start.7 = (f32[512,512]{0,1:T(8,128)S(1)}, f32[512,512]{0,1:T(8,128)}, u32[]{:S(2)}) copy-start(f32[512,512]{0,1:T(8,128)} %get-tuple-element.74) | copy-start | bytes 3145732
  108.3 3.9 %copy-start.2 = (f32[512,512]{0,1:T(8,128)S(1)}, f32[512,512]{0,1:T(8,128)}, u32[]{:S(2)}) copy-start(f32[512,512]{0,1:T(8,128)} %get-tuple-element.72) | copy-start | bytes 3145732
  130.9 3.3 %copy-start.8 = (f32[512,512]{0,1:T(8,128)S(1)}, f32[512,512]{0,1:T(8,128)}, u32[]{:S(2)}) copy-start(f32[512,512]{0,1:T(8,128)} %get-tuple-element.74) | copy-start | bytes 3145732
  130.9 3.6 %copy-start.3 = (f32[512,512]{0,1:T(8,128)S(1)}, f32[512,512]{0,1:T(8,128)}, u32[]{:S(2)}) copy-start(f32[512,512]{0,1:T(8,128)} %get-tuple-element.72) | copy-start | bytes 3145732
  151.6 3.8 %copy-start.20 = (f32[512,512]{0,1:T(8,128)S(1)}, f32[512,512]{0,1:T(8,128)}, u32[]{:S(2)}) copy-start(f32[512,512]{0,1:T(8,128)} %get-tuple-element.84) | copy-start | bytes 3145732
  151.6 4.0 %copy-start.16 = (f32[512,512]{0,1:T(8,128)S(1)}, f32[512,512]{0,1:T(8,128)}, u32[]{:S(2)}) copy-start(f32[512,512]{0,1:T(8,128)} %get-tuple-element.82) | copy-start | bytes 3145732
  152.6 3.3 %copy-start.12 = (f32[512,512]{0,1:T(8,128)S(1)}, f32[512,512]{0,1:T(8,128)}, u32[]{:S(2)}) copy-start(f32[512,512]{0,1:T(8,128)} %get-tuple-element.80) | copy-start | bytes 3145732
  167.1 3.3 %copy-start.21 = (f32[512,512]{0,1:T(8,128)S(1)}, f32[512,512]{0,1:T(8,128)}, u32[]{:S(2)}) copy-start(f32[512,512]{0,1:T(8,128)} %get-tuple-element.84) | copy-start | bytes 3145732
  167.1 3.6 %copy-start.17 = (f32[512,512]{0,1:T(8,128)S(1)}, f32[512,512]{0,1:T(8,128)}, u32[]{:S(2)}) copy-start(f32[512,512]{0,1:T(8,128)} %get-tuple-element.82) | copy-start | bytes 3145732
  167.2 3.8 %copy-start.13 = (f32[512,512]{0,1:T(8,128)S(1)}, f32[512,512]{0,1:T(8,128)}, u32[]{:S(2)}) copy-start(f32[512,512]{0,1:T(8,128)} %get-tuple-element.80) | copy-start | bytes 3145732
  182.4 3.7 %copy-start.9 = (f32[512,512]{0,1:T(8,128)S(1)}, f32[512,512]{0,1:T(8,128)}, u32[]{:S(2)}) copy-start(f32[512,512]{0,1:T(8,128)} %get-tuple-element.74) | copy-start | bytes 3145732
  182.4 3.9 %copy-start.4 = (f32[512,512]{0,1:T(8,128)S(1)}, f32[512,512]{0,1:T(8,128)}, u32[]{:S(2)}) copy-start(f32[512,512]{0,1:T(8,128)} %get-tuple-element.72) | copy-start | bytes 3145732
  205.0 3.3 %copy-start.10 = (f32[512,512]{0,1:T(8,128)S(1)}, f32[512,512]{0,1:T(8,128)}, u32[]{:S(2)}) copy-start(f32[512,512]{0,1:T(8,128)} %get-tuple-element.74) | copy-start | bytes 3145732
  205.0 3.6 %copy-start.5 = (f32[512,512]{0,1:T(8,128)S(1)}, f32[512,512]{0,1:T(8,128)}, u32[]{:S(2)}) copy-start(f32[512,512]{0,1:T(8,128)} %get-tuple-element.72) | copy-start | bytes 3145732
  226.6 5.8 %copy-start.25 = (f32[8192]{0:T(1024)}, f32[8192]{0:T(1024)S(1)}, u32[]{:S(2)}) copy-start(f32[8192]{0:T(1024)S(1)} %subtract_multiply_fusion.1) | copy-start | bytes 98308
  226.7 5.7 %copy-start.14 = (f32[512,512]{0,1:T(8,128)S(1)}, f32[512,512]{0,1:T(8,128)}, u32[]{:S(2)}) copy-start(f32[512,512]{0,1:T(8,128)} %get-tuple-element.80) | copy-start | bytes 3145732
  243.7 3.3 %copy-start.22 = (f32[512,512]{0,1:T(8,128)S(1)}, f32[512,512]{0,1:T(8,128)}, u32[]{:S(2)}) copy-start(f32[512,512]{0,1:T(8,128)} %get-tuple-element.84) | copy-start | bytes 3145732
  243.7 3.6 %copy-start.18 = (f32[512,512]{0,1:T(8,128)S(1)}, f32[512,512]{0,1:T(8,128)}, u32[]{:S(2)}) copy-start(f32[512,512]{0,1:T(8,128)} %get-tuple-element.82) | copy-start | bytes 3145732
where the time goes:
time: 262 us; the launch traced here: 261 us
  blocking collectives  174 us (66%)
  other arithmetic  54.3 us (21%)
  matrix products  21.1 us (8%)
  between operations  8.31 us (3%)
  local copies, waits for them, and re-layouts  2.96 us (1%)
    pmax x3, blocking collectives, potential(): top_rows = lax.pmax(top_local, 'item')  55.7 us
    psum x3, blocking collectives, potential(): mass_rows = lax.psum(mass_local, 'item')  49 us
    pmax x3, blocking collectives, potential(): top_rows = lax.pmax(top_local, 'user')  31.6 us
    psum x3, blocking collectives, potential(): mass_rows = lax.psum(mass_local, 'user')  31.2 us
    reduce_sum x28, other arithmetic, add_mass(): fresh_mass = old_mass + jnp.sum(jnp.exp(scores - anchor[:, None]), axis=1)  22.8 us
    dot_general x10, matrix products, block_scores(): lax.dot_general(row_block, col_block, (((1,), (1,)), ((), ())), preferred...  21.1 us
    reduce_max x20, other arithmetic, raise_top(): jnp.max(scores, axis=1)  16.1 us
    psum x1, blocking collectives, body(): user_total = lax.psum(jnp.sum(user_counts), 'user')  6.27 us

commit v1 on v0

v1 whole, which is shorter than its diff:
```python
import math

import jax
import jax.numpy as jnp
from jax import lax
from jax.experimental import pallas as pl
from jax.experimental.pallas import tpu as pltpu
from jax.sharding import PartitionSpec as P

CLUSTER = 512
LANES = 128
BLOCKS = CLUSTER // LANES
ROWS = 8
ITERS = 3
entropy = 0.25
lowest = -1e30
INTO = math.log2(math.e) / entropy
BACK = entropy * math.log(2.0)

HERE = pl.BlockSpec(memory_space=pltpu.VMEM)
SCALARS = pl.BlockSpec(memory_space=pltpu.SMEM)
FAR = pl.BlockSpec(memory_space=pltpu.HBM)
PACK = (ROWS, CLUSTER)


def near(shape, dtype=jnp.float32):
    return pltpu.VMEM(shape, dtype)


def keep(array):
    return pltpu.with_memory_space_constraint(array, pltpu.VMEM)


def note_at(slots, number):
    row = slots + number // BLOCKS
    lane = number % BLOCKS * LANES
    return slice(row, row + 1), slice(lane, lane + LANES)


def wide(block):
    return jnp.concatenate([block] * BLOCKS, axis=1)


def total_of(counts):
    total = jnp.sum(jnp.sum(counts.astype(jnp.float32), axis=0, keepdims=True), axis=1, keepdims=True)
    return jnp.broadcast_to(total, (1, LANES))


def write_notes(pack, tiles, which, counts):
    slots = tiles.shape[2]
    pack[slots:, :] = jnp.zeros((ROWS - slots, CLUSTER), jnp.float32)
    for slot in range(slots):
        number = jnp.full((1, LANES), tiles[0, 0, slot, which], jnp.int32)
        pack[note_at(slots, slot)] = number.astype(jnp.float32)
    pack[note_at(slots, slots)] = total_of(counts)


def first_kernel(tiles, filled, user_emb, item_emb, item_count, pack, users, items, scores, sems):
    slots = tiles.shape[2]
    copies = []
    for slot in range(slots):
        pair = []
        for which, (table, into) in enumerate(((user_emb, users), (item_emb, items))):
            start = pl.multiple_of(tiles[0, 0, slot, which] * CLUSTER, CLUSTER)
            copy = pltpu.make_async_copy(
                table.at[pl.ds(start, CLUSTER)], into.at[slot], sems.at[slot, which]
            )
            copy.start()
            pair.append(copy)
        copies.append(pair)
    write_notes(pack, tiles, 0, item_count[...])
    for slot in range(slots):
        for copy in copies[slot]:
            copy.wait()
        user_block = users[slot]
        top = jnp.full((8, CLUSTER), lowest, jnp.float32)
        for block in range(BLOCKS):
            rows = slice(block * LANES, (block + 1) * LANES)
            part = lax.dot_general(
                items[slot, rows, :], user_block, (((1,), (1,)), ((), ())),
                preferred_element_type=jnp.float32,
            ) * INTO
            scores[rows, :] = part
            top = jnp.maximum(top, jnp.max(part.reshape(LANES // 8, 8, CLUSTER), axis=0))
        top = jnp.max(top, axis=0, keepdims=True)
        mass = jnp.zeros((8, CLUSTER), jnp.float32)
        for block in range(BLOCKS):
            rows = slice(block * LANES, (block + 1) * LANES)
            terms = jnp.exp2(scores[rows, :] - top)
            mass += jnp.sum(terms.reshape(LANES // 8, 8, CLUSTER), axis=0)
        log_mass = top + jnp.log2(jnp.sum(mass, axis=0, keepdims=True))
        pack[slot : slot + 1, :] = jnp.where(filled[0, 0] > slot, log_mass, lowest)


def setup_kernel(
    tiles, filled, users, items, user_count, item_count,
    table, user_here, item_here, user_ids, item_ids, notes, active,
):
    slots = tiles.shape[2]
    for slot in range(slots):
        item_block = items[slot]
        for block in range(BLOCKS):
            rows = slice(block * LANES, (block + 1) * LANES)
            table[slot, rows, :] = lax.dot_general(
                users[slot, rows, :], item_block, (((1,), (1,)), ((), ())),
                preferred_element_type=jnp.float32,
            ) * INTO
    place = lax.broadcasted_iota(jnp.int32, (ROWS, LANES), 0)
    on = jnp.where(place < filled[0, 0], 1.0, 0.0)
    active[...] = wide(on)
    for which, (counts, here, ids) in enumerate(
        ((user_count, user_here, user_ids), (item_count, item_here, item_ids))
    ):
        numbers = jnp.full((ROWS, LANES), -1, jnp.int32)
        here[...] = jnp.ones(PACK, jnp.float32)
        for slot in range(slots):
            group = tiles[0, 0, slot, which]
            numbers = jnp.where(place == slot, group, numbers)
            for block in range(BLOCKS):
                here[slot : slot + 1, block * LANES : (block + 1) * LANES] = counts[
                    pl.ds(group * BLOCKS + block, 1), :
                ].astype(jnp.float32)
        ids[...] = numbers.astype(jnp.float32)
    notes[...] = jnp.zeros(PACK, jnp.float32)
    write_notes(notes, tiles, 1, user_count[...])


def matches(packs, ids, slots):
    return [
        [ids == pack[note_at(slots, slot)] for slot in range(slots)] for pack in packs
    ]


def log_merge(packs, chosen, slots, lanes, rows):
    width = lanes.stop - lanes.start
    spread = wide if width == CLUSTER else (lambda mask: mask)
    top = jnp.full((rows, width), lowest, jnp.float32)
    for pack, masks in zip(packs, chosen):
        for slot in range(slots):
            part = jnp.where(spread(masks[slot]), pack[slot : slot + 1, lanes], lowest)
            top = jnp.maximum(top, part)
    mass = jnp.zeros((rows, width), jnp.float32)
    for pack, masks in zip(packs, chosen):
        for slot in range(slots):
            part = jnp.exp2(pack[slot : slot + 1, lanes] - top)
            mass += jnp.where(spread(masks[slot]), part, 0.0)
    return top + jnp.log2(jnp.where(mass > 0.0, mass, 1.0))


def sum_merge(packs, chosen, slots, lanes, rows):
    width = lanes.stop - lanes.start
    spread = wide if width == CLUSTER else (lambda mask: mask)
    total = jnp.zeros((rows, width), jnp.float32)
    for pack, masks in zip(packs, chosen):
        for slot in range(slots):
            total += jnp.where(spread(masks[slot]), pack[slot : slot + 1, lanes], 0.0)
    return total


def total_in(packs, slots):
    total = packs[0][note_at(slots, slots)]
    for pack in packs[1:]:
        total = total + pack[note_at(slots, slots)]
    return total


def store_masks(masks, chosen):
    for index, mask in enumerate(mask for group in chosen for mask in group):
        masks[index] = jnp.where(mask, 1.0, 0.0)


def load_masks(masks, devices, slots):
    return [
        [masks[device * slots + slot] > 0.0 for slot in range(slots)] for device in range(devices)
    ]


def down_rows(vector, slot, block):
    row = vector[slot : slot + 1, block * LANES : (block + 1) * LANES]
    return jnp.broadcast_to(row, (LANES, LANES)).T


EVERY = slice(0, CLUSTER)


def second_kernel(devices, *refs):
    packs = refs[:devices]
    table, ids, counts, notes, active, pack, terms, tops, masks, totals, potential = refs[devices:]
    slots = table.shape[0]
    chosen = matches(packs, ids[...], slots)
    store_masks(masks, chosen)
    totals[...] = jnp.broadcast_to(total_in(packs, slots), totals.shape)
    potential[...] = jnp.log2(counts[...]) - log_merge(packs, chosen, slots, EVERY, ROWS)
    pack[...] = notes[...]
    tops[...] = jnp.full(PACK, lowest, jnp.float32)
    for slot in range(slots):
        top = jnp.full((8, CLUSTER), lowest, jnp.float32)
        for block in range(BLOCKS):
            rows = slice(block * LANES, (block + 1) * LANES)
            part = table[slot, rows, :] + wide(down_rows(potential, slot, block))
            terms[slot, rows, :] = part
            top = jnp.maximum(top, jnp.max(part.reshape(LANES // 8, 8, CLUSTER), axis=0))
        top = jnp.max(top, axis=0, keepdims=True)
        mass = jnp.zeros((8, CLUSTER), jnp.float32)
        for block in range(BLOCKS):
            rows = slice(block * LANES, (block + 1) * LANES)
            part = jnp.exp2(terms[slot, rows, :] - top)
            terms[slot, rows, :] = part
            mass += jnp.sum(part.reshape(LANES // 8, 8, CLUSTER), axis=0)
        log_mass = top + jnp.log2(jnp.sum(mass, axis=0, keepdims=True))
        on = active[slot : slot + 1, :] > 0.0
        pack[slot : slot + 1, :] = jnp.where(on, log_mass, lowest)
        tops[slot : slot + 1, :] = jnp.where(on, top, lowest)


def row_sums(terms, factor, pack):
    slots = terms.shape[0]
    pack[...] = jnp.zeros(PACK, jnp.float32)
    for slot in range(slots):
        for block in range(BLOCKS):
            rows = slice(block * LANES, (block + 1) * LANES)
            part = terms[slot, rows, 0:LANES] * factor[slot : slot + 1, 0:LANES]
            for other in range(1, BLOCKS):
                lanes = slice(other * LANES, (other + 1) * LANES)
                part += terms[slot, rows, lanes] * factor[slot : slot + 1, lanes]
            pack[slot : slot + 1, rows] = jnp.sum(part.T, axis=0, keepdims=True)


def column_sums(terms, factor, scale, pack):
    slots = terms.shape[0]
    pack[...] = jnp.zeros(PACK, jnp.float32)
    for slot in range(slots):
        mass = jnp.zeros((8, CLUSTER), jnp.float32)
        for block in range(BLOCKS):
            rows = slice(block * LANES, (block + 1) * LANES)
            part = terms[slot, rows, :] * wide(down_rows(factor, slot, block))
            mass += jnp.sum(part.reshape(LANES // 8, 8, CLUSTER), axis=0)
        pack[slot : slot + 1, :] = jnp.sum(mass, axis=0, keepdims=True) * scale[slot : slot + 1, :]


def third_kernel(devices, *refs):
    packs = refs[:devices]
    terms, tops, ids, counts, item_total, pack, factor, masks, totals = refs[devices:]
    slots = terms.shape[0]
    chosen = matches(packs, ids[...], slots)
    store_masks(masks, chosen)
    totals[...] = jnp.broadcast_to(total_in(packs, slots), totals.shape)
    log_share = jnp.log2(counts[...] / wide(item_total[...]))
    merged = log_merge(packs, chosen, slots, EVERY, ROWS)
    factor[...] = jnp.exp2(tops[...] + (log_share - merged))
    row_sums(terms, factor, pack)


def user_kernel(devices, *refs):
    packs = refs[:devices]
    terms, masks, counts, totals, scale, pack, factor = refs[devices:]
    slots = terms.shape[0]
    sums = sum_merge(packs, load_masks(masks, devices, slots), slots, EVERY, ROWS)
    factor[...] = counts[...] / (wide(totals[...]) * jnp.where(sums > 0.0, sums, 1.0))
    column_sums(terms, factor, scale, pack)


def item_kernel(devices, *refs):
    packs = refs[:devices]
    terms, masks, counts, totals, old, pack, factor = refs[devices:]
    slots = terms.shape[0]
    sums = sum_merge(packs, load_masks(masks, devices, slots), slots, EVERY, ROWS)
    share = counts[...] / (wide(totals[...]) * jnp.where(sums > 0.0, sums, 1.0))
    factor[...] = old[...] * share
    row_sums(terms, factor, pack)


def in_order(axis, devices, packs, ordered):
    me = lax.axis_index(axis)
    for step in range(devices):
        ordered[source(me, step, devices)] = packs[step][...]
    return [ordered.at[device] for device in range(devices)]


def cluster_matches(packs, slots, groups):
    numbers = lax.broadcasted_iota(jnp.int32, (groups, LANES), 0).astype(jnp.float32)
    return matches(packs, numbers, slots)


def user_out_kernel(axis, devices, slots, *refs):
    counts, totals, out, first_packs, last_packs = refs[2 * devices :]
    first = in_order(axis, devices, refs[:devices], first_packs)
    last = in_order(axis, devices, refs[devices : 2 * devices], last_packs)
    groups = counts.shape[0] // BLOCKS
    chosen = cluster_matches(first, slots, groups)
    for block in range(BLOCKS):
        lanes = slice(block * LANES, (block + 1) * LANES)
        here = pl.ds(block, groups, stride=BLOCKS)
        share = jnp.log2(counts[here, :].astype(jnp.float32) / totals[0:1, :])
        merged = log_merge(first, chosen, slots, lanes, groups)
        sums = sum_merge(last, chosen, slots, lanes, groups)
        out[here, :] = BACK * (2.0 * share - merged - jnp.log2(sums))


def item_base_kernel(axis, devices, slots, middles, *refs):
    given = (1 + middles) * devices
    counts, item_total, user_total, out, numbers, all_packs = refs[given:]
    packs = [
        in_order(axis, devices, refs[step * devices : (step + 1) * devices], all_packs.at[step])
        for step in range(1 + middles)
    ]
    groups = counts.shape[0] // BLOCKS
    chosen = cluster_matches(packs[0], slots, groups)
    for index, mask in enumerate(mask for group in chosen for mask in group):
        numbers[index] = jnp.where(mask, 1.0, 0.0)
    for block in range(BLOCKS):
        lanes = slice(block * LANES, (block + 1) * LANES)
        here = pl.ds(block, groups, stride=BLOCKS)
        share = jnp.log2(counts[here, :].astype(jnp.float32) / item_total[0:1, :])
        base = (2 + middles) * share + jnp.log2(user_total[0:1, :])
        base = base - log_merge(packs[0], chosen, slots, lanes, groups)
        for step in range(middles):
            base = base - jnp.log2(sum_merge(packs[1 + step], chosen, slots, lanes, groups))
        out[here, :] = base


def item_out_kernel(axis, devices, slots, *refs):
    base, numbers, out, packs_here = refs[devices:]
    packs = in_order(axis, devices, refs[:devices], packs_here)
    groups = base.shape[0] // BLOCKS
    chosen = load_masks(numbers, devices, slots)
    for block in range(BLOCKS):
        lanes = slice(block * LANES, (block + 1) * LANES)
        here = pl.ds(block, groups, stride=BLOCKS)
        sums = sum_merge(packs, chosen, slots, lanes, groups)
        out[here, :] = BACK * (base[here, :] - jnp.log2(sums))


def paired(devices):
    return devices & (devices - 1) == 0


def source(me, step, devices):
    if paired(devices):
        return jnp.bitwise_xor(me, step)
    return lax.rem(me + devices - step, devices)


def exchange(pack, axis, devices):
    packs = [pack]
    for step in range(1, devices):
        if paired(devices):
            route = [(device, device ^ step) for device in range(devices)]
        else:
            route = [(device, (device + step) % devices) for device in range(devices)]
        packs.append(keep(lax.ppermute(pack, axis, route)))
    return packs


def call(kernel, outs, operands, specs=None, scratch=(), **params):
    return pl.pallas_call(
        kernel,
        out_shape=outs,
        in_specs=specs or [HERE] * len(operands),
        out_specs=jax.tree.map(lambda _: HERE, outs, is_leaf=lambda leaf: not isinstance(leaf, list)),
        scratch_shapes=list(scratch),
        compiler_params=pltpu.CompilerParams(vmem_limit_bytes=16 << 20),
        **params,
    )(*operands)


def bind(kernel, *fixed):
    return lambda *refs: kernel(*fixed, *refs)


def make_body(n_user, n_item):
    def body(user_emb, item_emb, user_count, item_count, tiles, tile_count):
        slots = tiles.shape[2]
        tall = (slots, CLUSTER, CLUSTER)
        vectors = near(PACK)
        splat = near((ROWS, LANES))
        user_counts = user_count.reshape(-1, LANES)
        item_counts = item_count.reshape(-1, LANES)
        gathered = near((slots, CLUSTER, user_emb.shape[1]), user_emb.dtype)

        pack, users, items = call(
            first_kernel,
            [vectors, gathered, gathered],
            (tiles, tile_count, user_emb, item_emb, item_counts),
            [SCALARS, SCALARS, FAR, FAR, HERE],
            [near((CLUSTER, CLUSTER)), pltpu.SemaphoreType.DMA((slots, 2))],
        )
        first_packs = exchange(pack, "item", n_item)
        table, user_here, item_here, user_ids, item_ids, notes, active = call(
            setup_kernel,
            [near(tall), vectors, vectors, splat, splat, vectors, vectors],
            (tiles, tile_count, keep(users), keep(items), user_counts, item_counts),
            [SCALARS, SCALARS, HERE, HERE, HERE, HERE],
        )
        pack, terms, tops, user_masks, item_total = call(
            bind(second_kernel, n_item),
            [vectors, near(tall), vectors, near((n_item * slots, ROWS, LANES)), splat],
            (*first_packs, keep(table), user_ids, user_here, notes, active),
            scratch=[near(PACK)],
        )
        terms = keep(terms)
        second_packs = exchange(pack, "user", n_user)
        pack, factor, item_masks, user_total = call(
            bind(third_kernel, n_user),
            [vectors, vectors, near((n_user * slots, ROWS, LANES)), splat],
            (*second_packs, terms, tops, item_ids, item_here, item_total),
        )
        item_packs = [second_packs]
        for iteration in range(1, ITERS):
            user_packs = exchange(pack, "item", n_item)
            (pack,) = call(
                bind(user_kernel, n_item),
                [vectors],
                (*user_packs, terms, user_masks, user_here, user_total, factor),
                scratch=[near(PACK)],
            )
            item_packs.append(exchange(pack, "user", n_user))
            if iteration < ITERS - 1:
                pack, factor = call(
                    bind(item_kernel, n_user),
                    [vectors, vectors],
                    (*item_packs[-1], terms, item_masks, item_here, item_total, factor),
                )
        user_values = call(
            bind(user_out_kernel, "item", n_item, slots),
            jax.ShapeDtypeStruct(user_counts.shape, jnp.float32),
            (*first_packs, *user_packs, user_counts, user_total),
            scratch=[near((n_item, *PACK)), near((n_item, *PACK))],
        )
        middles = ITERS - 2
        groups = item_counts.shape[0] // BLOCKS
        base, numbers = call(
            bind(item_base_kernel, "user", n_user, slots, middles),
            [near(item_counts.shape), near((n_user * slots, groups, LANES))],
            (*(pack for packs in item_packs[:-1] for pack in packs), item_counts, item_total, user_total),
            scratch=[near((1 + middles, n_user, *PACK))],
        )
        item_values = call(
            bind(item_out_kernel, "user", n_user, slots),
            jax.ShapeDtypeStruct(item_counts.shape, jnp.float32),
            (*item_packs[-1], base, numbers),
            scratch=[near((n_user, *PACK))],
        )
        return user_values.reshape(-1), item_values.reshape(-1)

    return body


def solution(mesh):
    in_specs = (
        P(("region", "user"), None),
        P(("region", "item"), None),
        P(("region", "user")),
        P(("region", "item")),
        P(("region", "user"), "item", None, None),
        P(("region", "user"), "item"),
    )
    out_specs = (P(("region", "user")), P(("region", "item")))
    return jax.shard_map(
        make_body(mesh.shape["user"], mesh.shape["item"]),
        mesh=mesh,
        in_specs=in_specs,
        out_specs=out_specs,
        check_vma=False,
    )
```

time: 262 us -> 50.4 us (0.19)
  blocking collectives: 174 us -> 0 us
  other arithmetic: 54.3 us -> 0 us
  matrix products: 21.1 us -> 0 us
  starting transfers between devices: 0 us -> 20.5 us
  Pallas kernels: 0 us -> 11.5 us
  waiting for transfers between devices: 0 us -> 11.2 us
  between operations: 8.31 us -> 1.37 us
    pmax x6 -> x0, blocking collectives: 87.4 us -> none  [the longest x3 55.7 us: potential(): top_rows = lax.pmax(top_local, 'item')]
    psum x7 -> x0, blocking collectives: 86.4 us -> none  [the longest x3 49 us: potential(): mass_rows = lax.psum(mass_local, 'item')]
    reduce_sum x30 -> x0, other arithmetic: 24 us -> none  [the longest x28 22.8 us: add_mass(): fresh_mass = old_mass + jnp.sum(jnp.exp(scores - anchor[:, None]), axis=1)]
    dot_general x10 -> x0, matrix products: 21.1 us -> none  [block_scores(): lax.dot_general(row_block, col_block, (((1,), (1,)), ((), ())), preferred...]
    ppermute x0 -> x18, starting transfers between devices: none -> 20.5 us  [exchange(): packs.append(keep(lax.ppermute(pack, axis, route)))]
    reduce_max x20 -> x0, other arithmetic: 16.1 us -> none  [raise_top(): jnp.max(scores, axis=1)]
    pallas_call x0 -> x10, Pallas kernels: none -> 11.5 us  [call(): pl.pallas_call(kernel, out_shape=outs, in_specs=specs or [HERE] * len(ope...]
    ppermute x0 -> x18, waiting for transfers between devices: none -> 11.2 us  [exchange(): packs.append(keep(lax.ppermute(pack, axis, route)))]
  transfers between devices with their start and end apart: 0 -> 18, of which waited for: 0 -> 11; matrix products, arithmetic and copies ran while one was open for 0% -> 0% of each run, Pallas kernels for 0% -> 5%
where the time goes in v1:
time: 50.4 us; the launch traced here: 50 us
  starting transfers between devices  20.5 us (41%)
  Pallas kernels  11.5 us (23%)
  waiting for transfers between devices  11.2 us (22%)
  local copies, waits for them, and re-layouts  5.46 us (11%)
  between operations  1.37 us (3%)
    ppermute x18, starting transfers between devices, exchange(): packs.append(keep(lax.ppermute(pack, axis, route)))  20.5 us
    pallas_call x10, Pallas kernels, call(): pl.pallas_call(kernel, out_shape=outs, in_specs=specs or [HERE] * len(ope...  11.5 us
    ppermute x18, waiting for transfers between devices, exchange(): packs.append(keep(lax.ppermute(pack, axis, route)))  11.2 us
    unnamed x9, local copies, waits for them, and re-layouts  5.46 us
  transfers between devices with their start and end apart: 18, of which 11 were waited for; matrix products, arithmetic and copies ran while one was open for 0% of the time, Pallas kernels for 5%

profile of v1, /device:TPU:0, one launch (start us, length us, event | category | flops | bytes accessed | tf_op | source)
XLA Modules:
  0.0 50.0 jit_solution(9985249897496391309)
XLA Ops:
  1.3 0.8 %copy.8.tiles = s32[1,1,5,2]{3,2,1,0:T(8,128)S(1)} copy(s32[1,1,5,2]{2,3,1,0:T(2,128)} %param.10) | data formatting | bytes 80 | tf_op args[4]
  2.0 1.6 %copy-done = bf16[8192,128]{1,0:T(8,128)(2,1)S(1)} copy-done((bf16[8192,128]{1,0:T(8,128)(2,1)S(1)}, bf16[8192,128]{1,0:T(8,128)(2,1)}, u32[]{:S(2)}) %copy-start) | copy-done | bytes 2097176
  3.6 1.6 %copy-done.1 = bf16[8192,128]{1,0:T(8,128)(2,1)S(1)} copy-done((bf16[8192,128]{1,0:T(8,128)(2,1)S(1)}, bf16[8192,128]{1,0:T(8,128)(2,1)}, u32[]{:S(2)}) %copy-start.1) | copy-done | bytes 2097176
  5.2 0.8 %copy-done.2 = s32[8192]{0:T(1024)S(1)} copy-done((s32[8192]{0:T(1024)S(1)}, s32[8192]{0:T(1024)}, u32[]{:S(2)}) %copy-start.2) | copy-done | bytes 32792
  6.0 4.9 %shard_map.77 = (f32[8,512]{1,0:T(8,128)S(1)}, bf16[5,512,128]{2,1,0:T(8,128)(2,1)S(1)}, bf16[5,512,128]{2,1,0:T(8,128)(2,1)S(1)}) custom-call(s32[1,1,5,2]{3,2,1,0:T(8,128)S(1)} %copy.8.tiles, s32[1,1]{1,0:T(1,128)S(6)} %copy.10.filled, bf16[8192,128]{1,0:T(8,128)(2,1)S(1)} %copy-done, bf16[8192,128]{1,0:T(8,128)(2,1)S(1)} %copy-done.1, s32[64,128]{1,0:T(8,128)S(1)} %bitcast.4), custom_call_target="tpu_custom_call" | custom-call | tf_op jit(solution)/shard_map/pallas_call | solution.py:356
  10.9 5.1 %collective-permute-start.2 = (f32[8,512]{1,0:T(8,128)S(1)}, f32[8,512]{1,0:T(8,128)S(1)}, u32[]{:S(2)}, u32[]{:S(2)}) collective-permute-start(f32[8,512]{1,0:T(8,128)S(1)} %get-tuple-element.25.refs_0_), channel_id=1, source_target_pairs={{0,3},{1,2},{2,1},{3,0},{4,7},{5,6},{6,5},{7,4},{8,11},{9,10},{10,... | collective-permute-start | bytes 49160 | tf_op jit(solution)/shard_map/ppermute | solution.py:351
  16.0 0.0 collective-permute-start.1
  16.0 0.6 %collective-permute-start = (f32[8,512]{1,0:T(8,128)S(1)}, f32[8,512]{1,0:T(8,128)S(1)}, u32[]{:S(2)}, u32[]{:S(2)}) collective-permute-start(f32[8,512]{1,0:T(8,128)S(1)} %get-tuple-element.25.refs_0_), channel_id=1, source_target_pairs={{0,1},{1,0},{2,3},{3,2},{4,5},{5,4},{6,7},{7,6},{8,9},{9,8},{10,11... | collective-permute-start | bytes 49160 | tf_op jit(solution)/shard_map/ppermute | solution.py:351
  16.7 0.8 %copy-done.3 = s32[8192]{0:T(1024)S(1)} copy-done((s32[8192]{0:T(1024)S(1)}, s32[8192]{0:T(1024)}, u32[]{:S(2)}) %copy-start.3) | copy-done | bytes 32792
  17.4 1.4 %shard_map.78 = (f32[5,512,512]{2,1,0:T(8,128)S(1)}, f32[8,512]{1,0:T(8,128)S(1)}, f32[8,512]{1,0:T(8,128)S(1)}, f32[8,128]{1,0:T(8,128)S(1)}, f32[8,128]{1,0:T(...) custom-call(s32[1,1,5,2]{3,2,1,0:T(8,128)S(1)} %copy.8.tiles, s32[1,1]{1,0:T(1,128)S(6)} %copy.10.filled, ...), custom_call_target="tpu_custom_call" | custom-call | tf_op jit(solution)/shard_map/pallas_call | solution.py:356
  18.9 0.0 collective-permute-done.2.refs_3_
  18.9 1.8 %collective-permute-done.1.refs_2_ = f32[8,512]{1,0:T(8,128)S(1)} collective-permute-done((f32[8,512]{1,0:T(8,128)S(1)}, f32[8,512]{1,0:T(8,128)S(1)}, u32[]{:S(2)}, u32[]{:S(2)}) %collective-permute-start.1) | collective-permute-done | bytes 16416 | tf_op jit(solution)/shard_map/ppermute | solution.py:351
  20.7 0.0 collective-permute-done.refs_1_
  20.7 1.3 %shard_map.79 = (f32[8,512]{1,0:T(8,128)S(1)}, f32[5,512,512]{2,1,0:T(8,128)S(1)}, f32[8,512]{1,0:T(8,128)S(1)}, f32[20,8,128]{2,1,0:T(8,128)S(1)}, f32[8,128]{1,0:T(8,128)S(1)}) custom-call(f32[8,512]{1,0:T(8,128)S(1)} %get-tuple-element.25.refs_0_, f32[8,512]{1,0:T(8,128)S(1)} %collective-permute-done.refs_1_, ...), custom_call_target="tpu_custom_call" | custom-call | tf_op jit(solution)/shard_map/pallas_call | solution.py:356
  22.0 0.1 collective-permute-start.5
  22.1 1.6 %collective-permute-start.4 = (f32[8,512]{1,0:T(8,128)S(1)}, f32[8,512]{1,0:T(8,128)S(1)}, u32[]{:S(2)}, u32[]{:S(2)}) collective-permute-start(f32[8,512]{1,0:T(8,128)S(1)} %get-tuple-element.33.refs_0_), channel_id=1, source_target_pairs={{0,8},{4,12},{8,0},{12,4},{1,9},{5,13},{9,1},{13,5},{2,10},{6,14},... | collective-permute-start | bytes 49160 | tf_op jit(solution)/shard_map/ppermute | solution.py:351
  23.6 0.3 collective-permute-start.3
  23.9 1.4 %collective-permute-done.5.refs_3_ = f32[8,512]{1,0:T(8,128)S(1)} collective-permute-done((f32[8,512]{1,0:T(8,128)S(1)}, f32[8,512]{1,0:T(8,128)S(1)}, u32[]{:S(2)}, u32[]{:S(2)}) %collective-permute-start.5) | collective-permute-done | bytes 16416 | tf_op jit(solution)/shard_map/ppermute | solution.py:351
  25.3 0.5 %collective-permute-done.4.refs_2_ = f32[8,512]{1,0:T(8,128)S(1)} collective-permute-done((f32[8,512]{1,0:T(8,128)S(1)}, f32[8,512]{1,0:T(8,128)S(1)}, u32[]{:S(2)}, u32[]{:S(2)}) %collective-permute-start.4) | collective-permute-done | bytes 16416 | tf_op jit(solution)/shard_map/ppermute | solution.py:351
  25.9 0.0 collective-permute-done.3.refs_1_
  25.9 0.5 %shard_map.80 = (f32[8,512]{1,0:T(8,128)S(1)}, f32[8,512]{1,0:T(8,128)S(1)}, f32[20,8,128]{2,1,0:T(8,128)S(1)}, f32[8,128]{1,0:T(8,128)S(1)}) custom-call(f32[8,512]{1,0:T(8,128)S(1)} %get-tuple-element.33.refs_0_, f32[8,512]{1,0:T(8,128)S(1)} %collective-permute-done.3.refs_1_, f32[8,512]{1,0:T(8,128)S(1)} %collective-permute-done.4.refs_2_, ...), custom_call_target="tpu_custom_call" | custom-call | tf_op jit(solution)/shard_map/pallas_call | solution.py:356
  26.4 2.1 %collective-permute-start.8 = (f32[8,512]{1,0:T(8,128)S(1)}, f32[8,512]{1,0:T(8,128)S(1)}, u32[]{:S(2)}, u32[]{:S(2)}) collective-permute-start(f32[8,512]{1,0:T(8,128)S(1)} %get-tuple-element.39.refs_0_), channel_id=1, source_target_pairs={{0,3},{1,2},{2,1},{3,0},{4,7},{5,6},{6,5},{7,4},{8,11},{9,10},{10,... | collective-permute-start | bytes 49160 | tf_op jit(solution)/shard_map/ppermute | solution.py:351
  28.5 0.1 collective-permute-start.7
  28.6 2.3 %collective-permute-start.6 = (f32[8,512]{1,0:T(8,128)S(1)}, f32[8,512]{1,0:T(8,128)S(1)}, u32[]{:S(2)}, u32[]{:S(2)}) collective-permute-start(f32[8,512]{1,0:T(8,128)S(1)} %get-tuple-element.39.refs_0_), channel_id=1, source_target_pairs={{0,1},{1,0},{2,3},{3,2},{4,5},{5,4},{6,7},{7,6},{8,9},{9,8},{10,11... | collective-permute-start | bytes 49160 | tf_op jit(solution)/shard_map/ppermute | solution.py:351
  30.9 1.1 %collective-permute-done.8.refs_3_ = f32[8,512]{1,0:T(8,128)S(1)} collective-permute-done((f32[8,512]{1,0:T(8,128)S(1)}, f32[8,512]{1,0:T(8,128)S(1)}, u32[]{:S(2)}, u32[]{:S(2)}) %collective-permute-start.8) | collective-permute-done | bytes 16416 | tf_op jit(solution)/shard_map/ppermute | solution.py:351
  32.0 1.3 %collective-permute-done.7.refs_2_ = f32[8,512]{1,0:T(8,128)S(1)} collective-permute-done((f32[8,512]{1,0:T(8,128)S(1)}, f32[8,512]{1,0:T(8,128)S(1)}, u32[]{:S(2)}, u32[]{:S(2)}) %collective-permute-start.7) | collective-permute-done | bytes 16416 | tf_op jit(solution)/shard_map/ppermute | solution.py:351
  33.3 0.5 shard_map.81.refs_0_.refs_4_
  33.8 0.1 collective-permute-start.11
  33.9 1.5 %collective-permute-start.10 = (f32[8,512]{1,0:T(8,128)S(1)}, f32[8,512]{1,0:T(8,128)S(1)}, u32[]{:S(2)}, u32[]{:S(2)}) collective-permute-start(f32[8,512]{1,0:T(8,128)S(1)} %shard_map.81.refs_0_.refs_4_), channel_id=1, source_target_pairs={{0,8},{4,12},{8,0},{12,4},{1,9},{5,13},{9,1},{13,5},{2,10},{6,14},... | collective-permute-start | bytes 49160 | tf_op jit(solution)/shard_map/ppermute | solution.py:351
  35.4 0.3 collective-permute-start.9
  35.7 1.4 %collective-permute-done.11.refs_3_.refs_7_ = f32[8,512]{1,0:T(8,128)S(1)} collective-permute-done((f32[8,512]{1,0:T(8,128)S(1)}, f32[8,512]{1,0:T(8,128)S(1)}, u32[]{:S(2)}, u32[]{:S(2)}) %collective-permute-start.11) | collective-permute-done | bytes 16416 | tf_op jit(solution)/shard_map/ppermute | solution.py:351
  37.2 0.5 %collective-permute-done.10.refs_2_.refs_6_ = f32[8,512]{1,0:T(8,128)S(1)} collective-permute-done((f32[8,512]{1,0:T(8,128)S(1)}, f32[8,512]{1,0:T(8,128)S(1)}, u32[]{:S(2)}, u32[]{:S(2)}) %collective-permute-start.10) | collective-permute-done | bytes 16416 | tf_op jit(solution)/shard_map/ppermute | solution.py:351
  37.7 0.0 collective-permute-done.9.refs_1_.refs_5_
  37.7 0.5 shard_map.82
  38.2 2.0 %collective-permute-start.14 = (f32[8,512]{1,0:T(8,128)S(1)}, f32[8,512]{1,0:T(8,128)S(1)}, u32[]{:S(2)}, u32[]{:S(2)}) collective-permute-start(f32[8,512]{1,0:T(8,128)S(1)} %get-tuple-element.44.refs_4_.refs_0_), channel_id=1, source_target_pairs={{0,3},{1,2},{2,1},{3,0},{4,7},{5,6},{6,5},{7,4},{8,11},{9,10},{10,... | collective-permute-start | bytes 49160 | tf_op jit(solution)/shard_map/ppermute | solution.py:351
  40.1 0.9 %collective-permute-start.13 = (f32[8,512]{1,0:T(8,128)S(1)}, f32[8,512]{1,0:T(8,128)S(1)}, u32[]{:S(2)}, u32[]{:S(2)}) collective-permute-start(f32[8,512]{1,0:T(8,128)S(1)} %get-tuple-element.44.refs_4_.refs_0_), channel_id=1, source_target_pairs={{0,2},{1,3},{2,0},{3,1},{4,6},{5,7},{6,4},{7,5},{8,10},{9,11},{10,... | collective-permute-start | bytes 49160 | tf_op jit(solution)/shard_map/ppermute | solution.py:351
  41.0 1.6 %collective-permute-start.12 = (f32[8,512]{1,0:T(8,128)S(1)}, f32[8,512]{1,0:T(8,128)S(1)}, u32[]{:S(2)}, u32[]{:S(2)}) collective-permute-start(f32[8,512]{1,0:T(8,128)S(1)} %get-tuple-element.44.refs_4_.refs_0_), channel_id=1, source_target_pairs={{0,1},{1,0},{2,3},{3,2},{4,5},{5,4},{6,7},{7,6},{8,9},{9,8},{10,11... | collective-permute-start | bytes 49160 | tf_op jit(solution)/shard_map/ppermute | solution.py:351
  42.6 1.3 %collective-permute-done.14.refs_7_.refs_3_ = f32[8,512]{1,0:T(8,128)S(1)} collective-permute-done((f32[8,512]{1,0:T(8,128)S(1)}, f32[8,512]{1,0:T(8,128)S(1)}, u32[]{:S(2)}, u32[]{:S(2)}) %collective-permute-start.14) | collective-permute-done | bytes 16416 | tf_op jit(solution)/shard_map/ppermute | solution.py:351
  43.9 1.0 %collective-permute-done.13.refs_6_.refs_2_ = f32[8,512]{1,0:T(8,128)S(1)} collective-permute-done((f32[8,512]{1,0:T(8,128)S(1)}, f32[8,512]{1,0:T(8,128)S(1)}, u32[]{:S(2)}, u32[]{:S(2)}) %collective-permute-start.13) | collective-permute-done | bytes 16416 | tf_op jit(solution)/shard_map/ppermute | solution.py:351
  44.9 0.5 shard_map.84.refs_0_
  45.4 0.1 collective-permute-start.17
  45.5 1.5 %collective-permute-start.16 = (f32[8,512]{1,0:T(8,128)S(1)}, f32[8,512]{1,0:T(8,128)S(1)}, u32[]{:S(2)}, u32[]{:S(2)}) collective-permute-start(f32[8,512]{1,0:T(8,128)S(1)} %shard_map.84.refs_0_), channel_id=1, source_target_pairs={{0,8},{4,12},{8,0},{12,4},{1,9},{5,13},{9,1},{13,5},{2,10},{6,14},... | collective-permute-start | bytes 49160 | tf_op jit(solution)/shard_map/ppermute | solution.py:351
  47.0 0.3 collective-permute-start.15
  47.4 0.3 shard_map.85
  47.6 0.9 %shard_map.83 = f32[64,128]{1,0:T(8,128)} custom-call(f32[8,512]{1,0:T(8,128)S(1)} %get-tuple-element.25.refs_0_, f32[8,512]{1,0:T(8,128)S(1)} %collective-permute-done.refs_1_, f32[8,512]{1,0:T(8,128)S(1)} %collective-permute-done.1.refs_2_, f32[8,512]{1,0:T(8,128)S(1)} %collective-permute-done.2.refs_3_, f32[8,512]{1,0:T(8,128)S(1)} %get-tuple-element.44.refs_4_.refs_0_, ...), custom_call_target="tpu_custom_call" | custom-call | tf_op jit(solution)/shard_map/pallas_call | solution.py:356
  48.5 0.3 collective-permute-done.17.refs_3_
  48.8 0.5 collective-permute-done.16.refs_2_
  49.3 0.7 %shard_map.86 = f32[64,128]{1,0:T(8,128)} custom-call(f32[8,512]{1,0:T(8,128)S(1)} %shard_map.84.refs_0_, f32[8,512]{1,0:T(8,128)S(1)} %collective-permute-done.15.refs_1_, f32[8,512]{1,0:T(8,128)S(1)} %collective-permute-done.16.refs_2_, f32[8,512]{1,0:T(8,128)S(1)} %collective-permute-done.17.refs_3_, f32[64,128]{1,0:T(8,128)S(1)} %get-tuple-element.46.refs_4_, ...), custom_call_target="tpu_custom_call" | custom-call | tf_op jit(solution)/shard_map/pallas_call | solution.py:356
  (7 shorter events, 0.0 us)
Async XLA Ops:
  2.0 1.6 %copy-start = (bf16[8192,128]{1,0:T(8,128)(2,1)S(1)}, bf16[8192,128]{1,0:T(8,128)(2,1)}, u32[]{:S(2)}) copy-start(bf16[8192,128]{1,0:T(8,128)(2,1)} %user_emb.1) | copy-start | bytes 6291460
  3.6 1.6 %copy-start.1 = (bf16[8192,128]{1,0:T(8,128)(2,1)S(1)}, bf16[8192,128]{1,0:T(8,128)(2,1)}, u32[]{:S(2)}) copy-start(bf16[8192,128]{1,0:T(8,128)(2,1)} %item_emb.1) | copy-start | bytes 6291460
  5.2 0.8 %copy-start.2 = (s32[8192]{0:T(1024)S(1)}, s32[8192]{0:T(1024)}, u32[]{:S(2)}) copy-start(s32[8192]{0:T(1024)} %param.9) | copy-start | bytes 98308
  10.9 8.0 %collective-permute-start.2 = (f32[8,512]{1,0:T(8,128)S(1)}, f32[8,512]{1,0:T(8,128)S(1)}, u32[]{:S(2)}, u32[]{:S(2)}) collective-permute-start(f32[8,512]{1,0:T(8,128)S(1)} %get-tuple-element.25.refs_0_), channel_id=1, source_target_pairs={{0,3},{1,2},{2,1},{3,0},{4,7},{5,6},{6,5},{7,4},{8,11},{9,10},{10,... | collective-permute-start | bytes 49160 | tf_op jit(solution)/shard_map/ppermute | solution.py:351
  16.0 4.6 %collective-permute-start.1 = (f32[8,512]{1,0:T(8,128)S(1)}, f32[8,512]{1,0:T(8,128)S(1)}, u32[]{:S(2)}, u32[]{:S(2)}) collective-permute-start(f32[8,512]{1,0:T(8,128)S(1)} %get-tuple-element.25.refs_0_), channel_id=1, source_target_pairs={{0,2},{1,3},{2,0},{3,1},{4,6},{5,7},{6,4},{7,5},{8,10},{9,11},{10,... | collective-permute-start | bytes 49160 | tf_op jit(solution)/shard_map/ppermute | solution.py:351
  16.0 4.6 %collective-permute-start = (f32[8,512]{1,0:T(8,128)S(1)}, f32[8,512]{1,0:T(8,128)S(1)}, u32[]{:S(2)}, u32[]{:S(2)}) collective-permute-start(f32[8,512]{1,0:T(8,128)S(1)} %get-tuple-element.25.refs_0_), channel_id=1, source_target_pairs={{0,1},{1,0},{2,3},{3,2},{4,5},{5,4},{6,7},{7,6},{8,9},{9,8},{10,11... | collective-permute-start | bytes 49160 | tf_op jit(solution)/shard_map/ppermute | solution.py:351
  16.7 0.8 %copy-start.3 = (s32[8192]{0:T(1024)S(1)}, s32[8192]{0:T(1024)}, u32[]{:S(2)}) copy-start(s32[8192]{0:T(1024)} %param.8) | copy-start | bytes 98308
  22.0 3.4 %collective-permute-start.5 = (f32[8,512]{1,0:T(8,128)S(1)}, f32[8,512]{1,0:T(8,128)S(1)}, u32[]{:S(2)}, u32[]{:S(2)}) collective-permute-start(f32[8,512]{1,0:T(8,128)S(1)} %get-tuple-element.33.refs_0_), channel_id=1, source_target_pairs={{0,12},{4,8},{8,4},{12,0},{1,13},{5,9},{9,5},{13,1},{2,14},{6,10},... | collective-permute-start | bytes 49160 | tf_op jit(solution)/shard_map/ppermute | solution.py:351
  22.1 3.8 %collective-permute-start.4 = (f32[8,512]{1,0:T(8,128)S(1)}, f32[8,512]{1,0:T(8,128)S(1)}, u32[]{:S(2)}, u32[]{:S(2)}) collective-permute-start(f32[8,512]{1,0:T(8,128)S(1)} %get-tuple-element.33.refs_0_), channel_id=1, source_target_pairs={{0,8},{4,12},{8,0},{12,4},{1,9},{5,13},{9,1},{13,5},{2,10},{6,14},... | collective-permute-start | bytes 49160 | tf_op jit(solution)/shard_map/ppermute | solution.py:351
  23.6 2.2 %collective-permute-start.3 = (f32[8,512]{1,0:T(8,128)S(1)}, f32[8,512]{1,0:T(8,128)S(1)}, u32[]{:S(2)}, u32[]{:S(2)}) collective-permute-start(f32[8,512]{1,0:T(8,128)S(1)} %get-tuple-element.33.refs_0_), channel_id=1, source_target_pairs={{0,4},{4,0},{8,12},{12,8},{1,5},{5,1},{9,13},{13,9},{2,6},{6,2},{1... | collective-permute-start | bytes 49160 | tf_op jit(solution)/shard_map/ppermute | solution.py:351
  26.4 5.6 %collective-permute-start.8 = (f32[8,512]{1,0:T(8,128)S(1)}, f32[8,512]{1,0:T(8,128)S(1)}, u32[]{:S(2)}, u32[]{:S(2)}) collective-permute-start(f32[8,512]{1,0:T(8,128)S(1)} %get-tuple-element.39.refs_0_), channel_id=1, source_target_pairs={{0,3},{1,2},{2,1},{3,0},{4,7},{5,6},{6,5},{7,4},{8,11},{9,10},{10,... | collective-permute-start | bytes 49160 | tf_op jit(solution)/shard_map/ppermute | solution.py:351
  28.5 4.8 %collective-permute-start.7 = (f32[8,512]{1,0:T(8,128)S(1)}, f32[8,512]{1,0:T(8,128)S(1)}, u32[]{:S(2)}, u32[]{:S(2)}) collective-permute-start(f32[8,512]{1,0:T(8,128)S(1)} %get-tuple-element.39.refs_0_), channel_id=1, source_target_pairs={{0,2},{1,3},{2,0},{3,1},{4,6},{5,7},{6,4},{7,5},{8,10},{9,11},{10,... | collective-permute-start | bytes 49160 | tf_op jit(solution)/shard_map/ppermute | solution.py:351
  28.6 4.7 %collective-permute-start.6 = (f32[8,512]{1,0:T(8,128)S(1)}, f32[8,512]{1,0:T(8,128)S(1)}, u32[]{:S(2)}, u32[]{:S(2)}) collective-permute-start(f32[8,512]{1,0:T(8,128)S(1)} %get-tuple-element.39.refs_0_), channel_id=1, source_target_pairs={{0,1},{1,0},{2,3},{3,2},{4,5},{5,4},{6,7},{7,6},{8,9},{9,8},{10,11... | collective-permute-start | bytes 49160 | tf_op jit(solution)/shard_map/ppermute | solution.py:351
  33.8 3.4 %collective-permute-start.11 = (f32[8,512]{1,0:T(8,128)S(1)}, f32[8,512]{1,0:T(8,128)S(1)}, u32[]{:S(2)}, u32[]{:S(2)}) collective-permute-start(f32[8,512]{1,0:T(8,128)S(1)} %shard_map.81.refs_0_.refs_4_), channel_id=1, source_target_pairs={{0,12},{4,8},{8,4},{12,0},{1,13},{5,9},{9,5},{13,1},{2,14},{6,10},... | collective-permute-start | bytes 49160 | tf_op jit(solution)/shard_map/ppermute | solution.py:351
  33.9 3.8 %collective-permute-start.10 = (f32[8,512]{1,0:T(8,128)S(1)}, f32[8,512]{1,0:T(8,128)S(1)}, u32[]{:S(2)}, u32[]{:S(2)}) collective-permute-start(f32[8,512]{1,0:T(8,128)S(1)} %shard_map.81.refs_0_.refs_4_), channel_id=1, source_target_pairs={{0,8},{4,12},{8,0},{12,4},{1,9},{5,13},{9,1},{13,5},{2,10},{6,14},... | collective-permute-start | bytes 49160 | tf_op jit(solution)/shard_map/ppermute | solution.py:351
  35.4 2.3 %collective-permute-start.9 = (f32[8,512]{1,0:T(8,128)S(1)}, f32[8,512]{1,0:T(8,128)S(1)}, u32[]{:S(2)}, u32[]{:S(2)}) collective-permute-start(f32[8,512]{1,0:T(8,128)S(1)} %shard_map.81.refs_0_.refs_4_), channel_id=1, source_target_pairs={{0,4},{4,0},{8,12},{12,8},{1,5},{5,1},{9,13},{13,9},{2,6},{6,2},{1... | collective-permute-start | bytes 49160 | tf_op jit(solution)/shard_map/ppermute | solution.py:351
  38.2 5.8 %collective-permute-start.14 = (f32[8,512]{1,0:T(8,128)S(1)}, f32[8,512]{1,0:T(8,128)S(1)}, u32[]{:S(2)}, u32[]{:S(2)}) collective-permute-start(f32[8,512]{1,0:T(8,128)S(1)} %get-tuple-element.44.refs_4_.refs_0_), channel_id=1, source_target_pairs={{0,3},{1,2},{2,1},{3,0},{4,7},{5,6},{6,5},{7,4},{8,11},{9,10},{10,... | collective-permute-start | bytes 49160 | tf_op jit(solution)/shard_map/ppermute | solution.py:351
  40.1 4.8 %collective-permute-start.13 = (f32[8,512]{1,0:T(8,128)S(1)}, f32[8,512]{1,0:T(8,128)S(1)}, u32[]{:S(2)}, u32[]{:S(2)}) collective-permute-start(f32[8,512]{1,0:T(8,128)S(1)} %get-tuple-element.44.refs_4_.refs_0_), channel_id=1, source_target_pairs={{0,2},{1,3},{2,0},{3,1},{4,6},{5,7},{6,4},{7,5},{8,10},{9,11},{10,... | collective-permute-start | bytes 49160 | tf_op jit(solution)/shard_map/ppermute | solution.py:351
  41.0 3.9 %collective-permute-start.12 = (f32[8,512]{1,0:T(8,128)S(1)}, f32[8,512]{1,0:T(8,128)S(1)}, u32[]{:S(2)}, u32[]{:S(2)}) collective-permute-start(f32[8,512]{1,0:T(8,128)S(1)} %get-tuple-element.44.refs_4_.refs_0_), channel_id=1, source_target_pairs={{0,1},{1,0},{2,3},{3,2},{4,5},{5,4},{6,7},{7,6},{8,9},{9,8},{10,11... | collective-permute-start | bytes 49160 | tf_op jit(solution)/shard_map/ppermute | solution.py:351
  45.4 3.4 %collective-permute-start.17 = (f32[8,512]{1,0:T(8,128)S(1)}, f32[8,512]{1,0:T(8,128)S(1)}, u32[]{:S(2)}, u32[]{:S(2)}) collective-permute-start(f32[8,512]{1,0:T(8,128)S(1)} %shard_map.84.refs_0_), channel_id=1, source_target_pairs={{0,12},{4,8},{8,4},{12,0},{1,13},{5,9},{9,5},{13,1},{2,14},{6,10},... | collective-permute-start | bytes 49160 | tf_op jit(solution)/shard_map/ppermute | solution.py:351
  45.5 3.8 %collective-permute-start.16 = (f32[8,512]{1,0:T(8,128)S(1)}, f32[8,512]{1,0:T(8,128)S(1)}, u32[]{:S(2)}, u32[]{:S(2)}) collective-permute-start(f32[8,512]{1,0:T(8,128)S(1)} %shard_map.84.refs_0_), channel_id=1, source_target_pairs={{0,8},{4,12},{8,0},{12,4},{1,9},{5,13},{9,1},{13,5},{2,10},{6,14},... | collective-permute-start | bytes 49160 | tf_op jit(solution)/shard_map/ppermute | solution.py:351
  47.0 2.3 %collective-permute-start.15 = (f32[8,512]{1,0:T(8,128)S(1)}, f32[8,512]{1,0:T(8,128)S(1)}, u32[]{:S(2)}, u32[]{:S(2)}) collective-permute-start(f32[8,512]{1,0:T(8,128)S(1)} %shard_map.84.refs_0_), channel_id=1, source_target_pairs={{0,4},{4,0},{8,12},{12,8},{1,5},{5,1},{9,13},{13,9},{2,6},{6,2},{1... | collective-permute-start | bytes 49160 | tf_op jit(solution)/shard_map/ppermute | solution.py:351

commit v2 on v1

--- a/solution.py
+++ b/solution.py
@@ -31,6 +31,10 @@
     return pltpu.with_memory_space_constraint(array, pltpu.VMEM)
 
 
+def away(array):
+    return pltpu.with_memory_space_constraint(array, pltpu.HBM)
+
+
 def note_at(slots, number):
     row = slots + number // BLOCKS
     lane = number % BLOCKS * LANES
@@ -47,27 +51,51 @@
 
 
 def write_notes(pack, tiles, which, counts):
-    slots = tiles.shape[2]
+    slots = tiles.shape[1]
     pack[slots:, :] = jnp.zeros((ROWS - slots, CLUSTER), jnp.float32)
     for slot in range(slots):
-        number = jnp.full((1, LANES), tiles[0, 0, slot, which], jnp.int32)
+        number = jnp.full((1, LANES), tiles[which, slot], jnp.int32)
         pack[note_at(slots, slot)] = number.astype(jnp.float32)
     pack[note_at(slots, slots)] = total_of(counts)
 
 
-def first_kernel(tiles, filled, user_emb, item_emb, item_count, pack, users, items, scores, sems):
-    slots = tiles.shape[2]
-    copies = []
-    for slot in range(slots):
+def first_kernel(
+    devices, far_tiles, filled, user_emb, item_emb, far_count, pack, users, items,
+    tiles, item_count, scores, small_sems, sems,
+):
+    slots = tiles.shape[1]
+    groups = user_emb.shape[0] // CLUSTER
+    small = [
+        pltpu.make_async_copy(source, target, small_sems.at[index])
+        for index, (source, target) in enumerate(
+            ((far_tiles, tiles), (far_count, item_count))
+        )
+    ]
+    for copy in small:
+        copy.start()
+
+    def fetch(slot, groups_here):
         pair = []
         for which, (table, into) in enumerate(((user_emb, users), (item_emb, items))):
-            start = pl.multiple_of(tiles[0, 0, slot, which] * CLUSTER, CLUSTER)
+            start = pl.multiple_of(groups_here[which] * CLUSTER, CLUSTER)
             copy = pltpu.make_async_copy(
                 table.at[pl.ds(start, CLUSTER)], into.at[slot], sems.at[slot, which]
             )
             copy.start()
             pair.append(copy)
-        copies.append(pair)
+        return pair
+
+    n_user, n_item = devices
+    fixed = min(groups // n_user, groups // n_item, slots)
+    row, column = lax.axis_index("user"), lax.axis_index("item")
+    copies = [
+        fetch(slot, [lax.rem(place * fixed + slot, groups) for place in (column, row)])
+        for slot in range(fixed)
+    ]
+    for copy in small:
+        copy.wait()
+    for slot in range(fixed, slots):
+        copies.append(fetch(slot, [tiles[which, slot] for which in range(2)]))
     write_notes(pack, tiles, 0, item_count[...])
     for slot in range(slots):
         for copy in copies[slot]:
@@ -93,10 +121,23 @@
 
 
 def setup_kernel(
-    tiles, filled, users, items, user_count, item_count,
+    far_tiles, filled, users, items, far_users, far_items,
     table, user_here, item_here, user_ids, item_ids, notes, active,
+    tiles, user_count, item_count, sems,
 ):
-    slots = tiles.shape[2]
+    slots = tiles.shape[1]
+    copies = [
+        pltpu.make_async_copy(source, target, sems.at[index])
+        for index, (source, target) in enumerate(
+            (
+                (far_tiles, tiles),
+                (far_users, user_count),
+                (far_items, item_count),
+            )
+        )
+    ]
+    for copy in copies:
+        copy.start()
     for slot in range(slots):
         item_block = items[slot]
         for block in range(BLOCKS):
@@ -105,6 +146,8 @@
                 users[slot, rows, :], item_block, (((1,), (1,)), ((), ())),
                 preferred_element_type=jnp.float32,
             ) * INTO
+    for copy in copies:
+        copy.wait()
     place = lax.broadcasted_iota(jnp.int32, (ROWS, LANES), 0)
     on = jnp.where(place < filled[0, 0], 1.0, 0.0)
     active[...] = wide(on)
@@ -114,7 +157,7 @@
         numbers = jnp.full((ROWS, LANES), -1, jnp.int32)
         here[...] = jnp.ones(PACK, jnp.float32)
         for slot in range(slots):
-            group = tiles[0, 0, slot, which]
+            group = tiles[which, slot]
             numbers = jnp.where(place == slot, group, numbers)
             for block in range(BLOCKS):
                 here[slot : slot + 1, block * LANES : (block + 1) * LANES] = counts[
@@ -273,7 +316,7 @@
 def in_order(axis, devices, packs, ordered):
     me = lax.axis_index(axis)
     for step in range(devices):
-        ordered[source(me, step, devices)] = packs[step][...]
+        ordered[partner(me, step, devices)] = packs[step][...]
     return [ordered.at[device] for device in range(devices)]
 
 
@@ -335,7 +378,7 @@
     return devices & (devices - 1) == 0
 
 
-def source(me, step, devices):
+def partner(me, step, devices):
     if paired(devices):
         return jnp.bitwise_xor(me, step)
     return lax.rem(me + devices - step, devices)
@@ -378,19 +421,38 @@
         item_counts = item_count.reshape(-1, LANES)
         gathered = near((slots, CLUSTER, user_emb.shape[1]), user_emb.dtype)
 
+        small = pltpu.SMEM((2, slots), jnp.int32)
+        far_tiles = jnp.transpose(tiles, (0, 1, 3, 2)).reshape(2, slots)
         pack, users, items = call(
-            first_kernel,
+            bind(first_kernel, (n_user, n_item)),
             [vectors, gathered, gathered],
-            (tiles, tile_count, user_emb, item_emb, item_counts),
-            [SCALARS, SCALARS, FAR, FAR, HERE],
-            [near((CLUSTER, CLUSTER)), pltpu.SemaphoreType.DMA((slots, 2))],
+            (
+                away(far_tiles), tile_count, away(user_emb), away(item_emb), away(item_counts),
+            ),
+            [FAR, SCALARS, FAR, FAR, FAR],
+            [
+                small,
+                near(item_counts.shape, jnp.int32),
+                near((CLUSTER, CLUSTER)),
+                pltpu.SemaphoreType.DMA((2,)),
+                pltpu.SemaphoreType.DMA((slots, 2)),
+            ],
         )
         first_packs = exchange(pack, "item", n_item)
         table, user_here, item_here, user_ids, item_ids, notes, active = call(
             setup_kernel,
             [near(tall), vectors, vectors, splat, splat, vectors, vectors],
-            (tiles, tile_count, keep(users), keep(items), user_counts, item_counts),
-            [SCALARS, SCALARS, HERE, HERE, HERE, HERE],
+            (
+                away(far_tiles), tile_count, keep(users), keep(items),
+                away(user_counts), away(item_counts),
+            ),
+            [FAR, SCALARS, HERE, HERE, FAR, FAR],
+            [
+                small,
+                near(user_counts.shape, jnp.int32),
+                near(item_counts.shape, jnp.int32),
+                pltpu.SemaphoreType.DMA((3,)),
+            ],
         )
         pack, terms, tops, user_masks, item_total = call(
             bind(second_kernel, n_item),

time: 50.4 us -> 44.4 us (0.88)
  local copies, waits for them, and re-layouts: 5.46 us -> 0.01 us
  Pallas kernels: 11.5 us -> 10.5 us
  waiting for transfers between devices: 11.2 us -> 11.8 us
    unnamed x9 -> x4, local copies, waits for them, and re-layouts: 5.46 us -> 0.01 us
    pallas_call x10, Pallas kernels: 11.5 us -> 10.5 us  [call(): pl.pallas_call(kernel, out_shape=outs, in_specs=specs or [HERE] * len(ope...]
    ppermute x18, waiting for transfers between devices: 11.2 us -> 11.8 us  [exchange(): packs.append(keep(lax.ppermute(pack, axis, route)))]
  transfers between devices with their start and end apart: 18 -> 18, of which waited for: 11 -> 13; matrix products, arithmetic and copies ran while one was open for 0% -> 0% of each run, Pallas kernels for 5% -> 6%
where the time goes in v2:
time: 44.4 us; the launch traced here: 44.1 us
  starting transfers between devices  20.4 us (46%)
  waiting for transfers between devices  11.8 us (27%)
  Pallas kernels  10.5 us (24%)
  between operations  1.38 us (3%)
    ppermute x18, starting transfers between devices, exchange(): packs.append(keep(lax.ppermute(pack, axis, route)))  20.4 us
    ppermute x18, waiting for transfers between devices, exchange(): packs.append(keep(lax.ppermute(pack, axis, route)))  11.8 us
    pallas_call x10, Pallas kernels, call(): pl.pallas_call(kernel, out_shape=outs, in_specs=specs or [HERE] * len(ope...  10.5 us
  transfers between devices with their start and end apart: 18, of which 13 were waited for; matrix products, arithmetic and copies ran while one was open for 0% of the time, Pallas kernels for 6%

profile of v2, /device:TPU:0, one launch (start us, length us, event | category | flops | bytes accessed | tf_op | source)
XLA Modules:
  0.0 44.1 jit_solution(4435584768493248368)
XLA Ops:
  1.3 3.7 %shard_map.77 = (f32[8,512]{1,0:T(8,128)S(1)}, bf16[5,512,128]{2,1,0:T(8,128)(2,1)S(1)}, bf16[5,512,128]{2,1,0:T(8,128)(2,1)S(1)}) custom-call(s32[2,5]{1,0:T(2,128)} %bitcast.14, s32[1,1]{1,0:T(1,128)S(6)} %copy.8.refs_1_.filled, bf16[8192,128]{1,0:T(8,128)(2,1)} %refs_2_.1, bf16[8192,128]{1,0:T(8,128)(2,1)} %refs_3_.1, s32[64,128]{1,0:T(8,128)} %bitcast.7), custom_call_target="tpu_custom_call" | custom-call | tf_op jit(solution)/shard_map/pallas_call | solution.py:399
  5.0 5.1 %collective-permute-start.2 = (f32[8,512]{1,0:T(8,128)S(1)}, f32[8,512]{1,0:T(8,128)S(1)}, u32[]{:S(2)}, u32[]{:S(2)}) collective-permute-start(f32[8,512]{1,0:T(8,128)S(1)} %get-tuple-element.25.refs_0_), channel_id=1, source_target_pairs={{0,3},{1,2},{2,1},{3,0},{4,7},{5,6},{6,5},{7,4},{8,11},{9,10},{10,... | collective-permute-start | bytes 49160 | tf_op jit(solution)/shard_map/ppermute | solution.py:394
  10.2 0.0 collective-permute-start.1
  10.2 0.6 %collective-permute-start = (f32[8,512]{1,0:T(8,128)S(1)}, f32[8,512]{1,0:T(8,128)S(1)}, u32[]{:S(2)}, u32[]{:S(2)}) collective-permute-start(f32[8,512]{1,0:T(8,128)S(1)} %get-tuple-element.25.refs_0_), channel_id=1, source_target_pairs={{0,1},{1,0},{2,3},{3,2},{4,5},{5,4},{6,7},{7,6},{8,9},{9,8},{10,11... | collective-permute-start | bytes 49160 | tf_op jit(solution)/shard_map/ppermute | solution.py:394
  10.8 1.6 %shard_map.78 = (f32[5,512,512]{2,1,0:T(8,128)S(1)}, f32[8,512]{1,0:T(8,128)S(1)}, f32[8,512]{1,0:T(8,128)S(1)}, f32[8,128]{1,0:T(8,128)S(1)}, f32[8,128]{1,0:T(...) custom-call(s32[2,5]{1,0:T(2,128)} %bitcast.15, s32[1,1]{1,0:T(1,128)S(6)} %copy.8.refs_1_.filled, ...), custom_call_target="tpu_custom_call" | custom-call | tf_op jit(solution)/shard_map/pallas_call | solution.py:399
  12.4 0.0 collective-permute-done.2.refs_3_
  12.4 2.4 %collective-permute-done.1.refs_2_ = f32[8,512]{1,0:T(8,128)S(1)} collective-permute-done((f32[8,512]{1,0:T(8,128)S(1)}, f32[8,512]{1,0:T(8,128)S(1)}, u32[]{:S(2)}, u32[]{:S(2)}) %collective-permute-start.1) | collective-permute-done | bytes 16416 | tf_op jit(solution)/shard_map/ppermute | solution.py:394
  14.8 0.0 collective-permute-done.refs_1_
  14.8 1.3 %shard_map.79 = (f32[8,512]{1,0:T(8,128)S(1)}, f32[5,512,512]{2,1,0:T(8,128)S(1)}, f32[8,512]{1,0:T(8,128)S(1)}, f32[20,8,128]{2,1,0:T(8,128)S(1)}, f32[8,128]{1,0:T(8,128)S(1)}) custom-call(f32[8,512]{1,0:T(8,128)S(1)} %get-tuple-element.25.refs_0_, f32[8,512]{1,0:T(8,128)S(1)} %collective-permute-done.refs_1_, ...), custom_call_target="tpu_custom_call" | custom-call | tf_op jit(solution)/shard_map/pallas_call | solution.py:399
  16.1 0.1 collective-permute-start.5
  16.2 1.5 %collective-permute-start.4 = (f32[8,512]{1,0:T(8,128)S(1)}, f32[8,512]{1,0:T(8,128)S(1)}, u32[]{:S(2)}, u32[]{:S(2)}) collective-permute-start(f32[8,512]{1,0:T(8,128)S(1)} %get-tuple-element.33.refs_0_), channel_id=1, source_target_pairs={{0,8},{4,12},{8,0},{12,4},{1,9},{5,13},{9,1},{13,5},{2,10},{6,14},... | collective-permute-start | bytes 49160 | tf_op jit(solution)/shard_map/ppermute | solution.py:394
  17.7 0.3 collective-permute-start.3
  18.0 1.4 %collective-permute-done.5.refs_3_ = f32[8,512]{1,0:T(8,128)S(1)} collective-permute-done((f32[8,512]{1,0:T(8,128)S(1)}, f32[8,512]{1,0:T(8,128)S(1)}, u32[]{:S(2)}, u32[]{:S(2)}) %collective-permute-start.5) | collective-permute-done | bytes 16416 | tf_op jit(solution)/shard_map/ppermute | solution.py:394
  19.5 0.5 %collective-permute-done.4.refs_2_ = f32[8,512]{1,0:T(8,128)S(1)} collective-permute-done((f32[8,512]{1,0:T(8,128)S(1)}, f32[8,512]{1,0:T(8,128)S(1)}, u32[]{:S(2)}, u32[]{:S(2)}) %collective-permute-start.4) | collective-permute-done | bytes 16416 | tf_op jit(solution)/shard_map/ppermute | solution.py:394
  20.0 0.0 collective-permute-done.3.refs_1_
  20.0 0.5 %shard_map.80 = (f32[8,512]{1,0:T(8,128)S(1)}, f32[8,512]{1,0:T(8,128)S(1)}, f32[20,8,128]{2,1,0:T(8,128)S(1)}, f32[8,128]{1,0:T(8,128)S(1)}) custom-call(f32[8,512]{1,0:T(8,128)S(1)} %get-tuple-element.33.refs_0_, f32[8,512]{1,0:T(8,128)S(1)} %collective-permute-done.3.refs_1_, f32[8,512]{1,0:T(8,128)S(1)} %collective-permute-done.4.refs_2_, ...), custom_call_target="tpu_custom_call" | custom-call | tf_op jit(solution)/shard_map/pallas_call | solution.py:399
  20.5 1.5 %collective-permute-start.8 = (f32[8,512]{1,0:T(8,128)S(1)}, f32[8,512]{1,0:T(8,128)S(1)}, u32[]{:S(2)}, u32[]{:S(2)}) collective-permute-start(f32[8,512]{1,0:T(8,128)S(1)} %get-tuple-element.39.refs_0_), channel_id=1, source_target_pairs={{0,3},{1,2},{2,1},{3,0},{4,7},{5,6},{6,5},{7,4},{8,11},{9,10},{10,... | collective-permute-start | bytes 49160 | tf_op jit(solution)/shard_map/ppermute | solution.py:394
  22.1 0.6 %collective-permute-start.7 = (f32[8,512]{1,0:T(8,128)S(1)}, f32[8,512]{1,0:T(8,128)S(1)}, u32[]{:S(2)}, u32[]{:S(2)}) collective-permute-start(f32[8,512]{1,0:T(8,128)S(1)} %get-tuple-element.39.refs_0_), channel_id=1, source_target_pairs={{0,2},{1,3},{2,0},{3,1},{4,6},{5,7},{6,4},{7,5},{8,10},{9,11},{10,... | collective-permute-start | bytes 49160 | tf_op jit(solution)/shard_map/ppermute | solution.py:394
  22.7 2.3 %collective-permute-start.6 = (f32[8,512]{1,0:T(8,128)S(1)}, f32[8,512]{1,0:T(8,128)S(1)}, u32[]{:S(2)}, u32[]{:S(2)}) collective-permute-start(f32[8,512]{1,0:T(8,128)S(1)} %get-tuple-element.39.refs_0_), channel_id=1, source_target_pairs={{0,1},{1,0},{2,3},{3,2},{4,5},{5,4},{6,7},{7,6},{8,9},{9,8},{10,11... | collective-permute-start | bytes 49160 | tf_op jit(solution)/shard_map/ppermute | solution.py:394
  25.0 1.2 %collective-permute-done.8.refs_3_ = f32[8,512]{1,0:T(8,128)S(1)} collective-permute-done((f32[8,512]{1,0:T(8,128)S(1)}, f32[8,512]{1,0:T(8,128)S(1)}, u32[]{:S(2)}, u32[]{:S(2)}) %collective-permute-start.8) | collective-permute-done | bytes 16416 | tf_op jit(solution)/shard_map/ppermute | solution.py:394
  26.2 0.6 %collective-permute-done.7.refs_2_ = f32[8,512]{1,0:T(8,128)S(1)} collective-permute-done((f32[8,512]{1,0:T(8,128)S(1)}, f32[8,512]{1,0:T(8,128)S(1)}, u32[]{:S(2)}, u32[]{:S(2)}) %collective-permute-start.7) | collective-permute-done | bytes 16416 | tf_op jit(solution)/shard_map/ppermute | solution.py:394
  26.7 0.2 collective-permute-done.6.refs_1_
  26.9 0.5 %shard_map.81.refs_0_.refs_4_ = f32[8,512]{1,0:T(8,128)S(1)} custom-call(f32[8,512]{1,0:T(8,128)S(1)} %get-tuple-element.39.refs_0_, f32[8,512]{1,0:T(8,128)S(1)} %collective-permute-done.6.refs_1_, f32[8,512]{1,0:T(8,128)S(1)} %collective-permute-done.7.refs_2_, f32[8,512]{1,0:T(8,128)S(1)} %collective-permute-done.8.refs_3_, ...), custom_call_target="tpu_custom_call" | custom-call | tf_op jit(solution)/shard_map/pallas_call | solution.py:399
  27.4 0.1 collective-permute-start.11
  27.5 1.5 %collective-permute-start.10 = (f32[8,512]{1,0:T(8,128)S(1)}, f32[8,512]{1,0:T(8,128)S(1)}, u32[]{:S(2)}, u32[]{:S(2)}) collective-permute-start(f32[8,512]{1,0:T(8,128)S(1)} %shard_map.81.refs_0_.refs_4_), channel_id=1, source_target_pairs={{0,8},{4,12},{8,0},{12,4},{1,9},{5,13},{9,1},{13,5},{2,10},{6,14},... | collective-permute-start | bytes 49160 | tf_op jit(solution)/shard_map/ppermute | solution.py:394
  29.0 0.3 collective-permute-start.9
  29.3 1.5 %collective-permute-done.11.refs_3_.refs_7_ = f32[8,512]{1,0:T(8,128)S(1)} collective-permute-done((f32[8,512]{1,0:T(8,128)S(1)}, f32[8,512]{1,0:T(8,128)S(1)}, u32[]{:S(2)}, u32[]{:S(2)}) %collective-permute-start.11) | collective-permute-done | bytes 16416 | tf_op jit(solution)/shard_map/ppermute | solution.py:394
  30.8 0.5 %collective-permute-done.10.refs_2_.refs_6_ = f32[8,512]{1,0:T(8,128)S(1)} collective-permute-done((f32[8,512]{1,0:T(8,128)S(1)}, f32[8,512]{1,0:T(8,128)S(1)}, u32[]{:S(2)}, u32[]{:S(2)}) %collective-permute-start.10) | collective-permute-done | bytes 16416 | tf_op jit(solution)/shard_map/ppermute | solution.py:394
  31.3 0.0 collective-permute-done.9.refs_1_.refs_5_
  31.3 0.5 %shard_map.82 = (f32[8,512]{1,0:T(8,128)S(1)}, f32[8,512]{1,0:T(8,128)S(1)}) custom-call(f32[8,512]{1,0:T(8,128)S(1)} %shard_map.81.refs_0_.refs_4_, f32[8,512]{1,0:T(8,128)S(1)} %collective-permute-done.9.refs_1_.refs_5_, f32[8,512]{1,0:T(8,128)S(1)} %collective-permute-done.10.refs_2_.refs_6_, f32[8,512]{1,0:T(8,128)S(1)} %collective-permute-done.11.refs_3_.refs_7_, ...), custom_call_target="tpu_custom_call" | custom-call | tf_op jit(solution)/shard_map/pallas_call | solution.py:399
  31.8 2.5 %collective-permute-start.14 = (f32[8,512]{1,0:T(8,128)S(1)}, f32[8,512]{1,0:T(8,128)S(1)}, u32[]{:S(2)}, u32[]{:S(2)}) collective-permute-start(f32[8,512]{1,0:T(8,128)S(1)} %get-tuple-element.44.refs_4_.refs_0_), channel_id=1, source_target_pairs={{0,3},{1,2},{2,1},{3,0},{4,7},{5,6},{6,5},{7,4},{8,11},{9,10},{10,... | collective-permute-start | bytes 49160 | tf_op jit(solution)/shard_map/ppermute | solution.py:394
  34.2 0.9 %collective-permute-start.13 = (f32[8,512]{1,0:T(8,128)S(1)}, f32[8,512]{1,0:T(8,128)S(1)}, u32[]{:S(2)}, u32[]{:S(2)}) collective-permute-start(f32[8,512]{1,0:T(8,128)S(1)} %get-tuple-element.44.refs_4_.refs_0_), channel_id=1, source_target_pairs={{0,2},{1,3},{2,0},{3,1},{4,6},{5,7},{6,4},{7,5},{8,10},{9,11},{10,... | collective-permute-start | bytes 49160 | tf_op jit(solution)/shard_map/ppermute | solution.py:394
  35.1 1.1 %collective-permute-start.12 = (f32[8,512]{1,0:T(8,128)S(1)}, f32[8,512]{1,0:T(8,128)S(1)}, u32[]{:S(2)}, u32[]{:S(2)}) collective-permute-start(f32[8,512]{1,0:T(8,128)S(1)} %get-tuple-element.44.refs_4_.refs_0_), channel_id=1, source_target_pairs={{0,1},{1,0},{2,3},{3,2},{4,5},{5,4},{6,7},{7,6},{8,9},{9,8},{10,11... | collective-permute-start | bytes 49160 | tf_op jit(solution)/shard_map/ppermute | solution.py:394
  36.2 1.3 %collective-permute-done.14.refs_7_.refs_3_ = f32[8,512]{1,0:T(8,128)S(1)} collective-permute-done((f32[8,512]{1,0:T(8,128)S(1)}, f32[8,512]{1,0:T(8,128)S(1)}, u32[]{:S(2)}, u32[]{:S(2)}) %collective-permute-start.14) | collective-permute-done | bytes 16416 | tf_op jit(solution)/shard_map/ppermute | solution.py:394
  37.5 1.4 %collective-permute-done.13.refs_6_.refs_2_ = f32[8,512]{1,0:T(8,128)S(1)} collective-permute-done((f32[8,512]{1,0:T(8,128)S(1)}, f32[8,512]{1,0:T(8,128)S(1)}, u32[]{:S(2)}, u32[]{:S(2)}) %collective-permute-start.13) | collective-permute-done | bytes 16416 | tf_op jit(solution)/shard_map/ppermute | solution.py:394
  38.9 0.2 collective-permute-done.12.refs_5_.refs_1_
  39.0 0.5 %shard_map.84.refs_0_ = f32[8,512]{1,0:T(8,128)S(1)} custom-call(f32[8,512]{1,0:T(8,128)S(1)} %get-tuple-element.44.refs_4_.refs_0_, f32[8,512]{1,0:T(8,128)S(1)} %collective-permute-done.12.refs_5_.refs_1_, f32[8,512]{1,0:T(8,128)S(1)} %collective-permute-done.13.refs_6_.refs_2_, f32[8,512]{1,0:T(8,128)S(1)} %collective-permute-done.14.refs_7_.refs_3_, ...), custom_call_target="tpu_custom_call" | custom-call | tf_op jit(solution)/shard_map/pallas_call | solution.py:399
  39.5 0.1 collective-permute-start.17
  39.6 1.5 %collective-permute-start.16 = (f32[8,512]{1,0:T(8,128)S(1)}, f32[8,512]{1,0:T(8,128)S(1)}, u32[]{:S(2)}, u32[]{:S(2)}) collective-permute-start(f32[8,512]{1,0:T(8,128)S(1)} %shard_map.84.refs_0_), channel_id=1, source_target_pairs={{0,8},{4,12},{8,0},{12,4},{1,9},{5,13},{9,1},{13,5},{2,10},{6,14},... | collective-permute-start | bytes 49160 | tf_op jit(solution)/shard_map/ppermute | solution.py:394
  41.1 0.3 collective-permute-start.15
  41.5 0.0 copy-done
  41.5 0.3 shard_map.85
  41.7 0.0 copy-done.1
  41.8 0.9 %shard_map.83 = f32[64,128]{1,0:T(8,128)} custom-call(f32[8,512]{1,0:T(8,128)S(1)} %get-tuple-element.25.refs_0_, f32[8,512]{1,0:T(8,128)S(1)} %collective-permute-done.refs_1_, f32[8,512]{1,0:T(8,128)S(1)} %collective-permute-done.1.refs_2_, f32[8,512]{1,0:T(8,128)S(1)} %collective-permute-done.2.refs_3_, f32[8,512]{1,0:T(8,128)S(1)} %get-tuple-element.44.refs_4_.refs_0_, ...), custom_call_target="tpu_custom_call" | custom-call | tf_op jit(solution)/shard_map/pallas_call | solution.py:399
  42.6 0.3 collective-permute-done.17.refs_3_
  42.9 0.5 %collective-permute-done.16.refs_2_ = f32[8,512]{1,0:T(8,128)S(1)} collective-permute-done((f32[8,512]{1,0:T(8,128)S(1)}, f32[8,512]{1,0:T(8,128)S(1)}, u32[]{:S(2)}, u32[]{:S(2)}) %collective-permute-start.16) | collective-permute-done | bytes 16416 | tf_op jit(solution)/shard_map/ppermute | solution.py:394
  43.4 0.0 collective-permute-done.15.refs_1_
  43.4 0.7 %shard_map.86 = f32[64,128]{1,0:T(8,128)} custom-call(f32[8,512]{1,0:T(8,128)S(1)} %shard_map.84.refs_0_, f32[8,512]{1,0:T(8,128)S(1)} %collective-permute-done.15.refs_1_, f32[8,512]{1,0:T(8,128)S(1)} %collective-permute-done.16.refs_2_, f32[8,512]{1,0:T(8,128)S(1)} %collective-permute-done.17.refs_3_, f32[64,128]{1,0:T(8,128)S(1)} %get-tuple-element.46.refs_4_, ...), custom_call_target="tpu_custom_call" | custom-call | tf_op jit(solution)/shard_map/pallas_call | solution.py:399
  (2 shorter events, 0.0 us)
Async XLA Ops:
  5.0 7.4 %collective-permute-start.2 = (f32[8,512]{1,0:T(8,128)S(1)}, f32[8,512]{1,0:T(8,128)S(1)}, u32[]{:S(2)}, u32[]{:S(2)}) collective-permute-start(f32[8,512]{1,0:T(8,128)S(1)} %get-tuple-element.25.refs_0_), channel_id=1, source_target_pairs={{0,3},{1,2},{2,1},{3,0},{4,7},{5,6},{6,5},{7,4},{8,11},{9,10},{10,... | collective-permute-start | bytes 49160 | tf_op jit(solution)/shard_map/ppermute | solution.py:394
  10.2 4.6 %collective-permute-start.1 = (f32[8,512]{1,0:T(8,128)S(1)}, f32[8,512]{1,0:T(8,128)S(1)}, u32[]{:S(2)}, u32[]{:S(2)}) collective-permute-start(f32[8,512]{1,0:T(8,128)S(1)} %get-tuple-element.25.refs_0_), channel_id=1, source_target_pairs={{0,2},{1,3},{2,0},{3,1},{4,6},{5,7},{6,4},{7,5},{8,10},{9,11},{10,... | collective-permute-start | bytes 49160 | tf_op jit(solution)/shard_map/ppermute | solution.py:394
  10.2 4.6 %collective-permute-start = (f32[8,512]{1,0:T(8,128)S(1)}, f32[8,512]{1,0:T(8,128)S(1)}, u32[]{:S(2)}, u32[]{:S(2)}) collective-permute-start(f32[8,512]{1,0:T(8,128)S(1)} %get-tuple-element.25.refs_0_), channel_id=1, source_target_pairs={{0,1},{1,0},{2,3},{3,2},{4,5},{5,4},{6,7},{7,6},{8,9},{9,8},{10,11... | collective-permute-start | bytes 49160 | tf_op jit(solution)/shard_map/ppermute | solution.py:394
  16.1 3.4 %collective-permute-start.5 = (f32[8,512]{1,0:T(8,128)S(1)}, f32[8,512]{1,0:T(8,128)S(1)}, u32[]{:S(2)}, u32[]{:S(2)}) collective-permute-start(f32[8,512]{1,0:T(8,128)S(1)} %get-tuple-element.33.refs_0_), channel_id=1, source_target_pairs={{0,12},{4,8},{8,4},{12,0},{1,13},{5,9},{9,5},{13,1},{2,14},{6,10},... | collective-permute-start | bytes 49160 | tf_op jit(solution)/shard_map/ppermute | solution.py:394
  16.2 3.8 %collective-permute-start.4 = (f32[8,512]{1,0:T(8,128)S(1)}, f32[8,512]{1,0:T(8,128)S(1)}, u32[]{:S(2)}, u32[]{:S(2)}) collective-permute-start(f32[8,512]{1,0:T(8,128)S(1)} %get-tuple-element.33.refs_0_), channel_id=1, source_target_pairs={{0,8},{4,12},{8,0},{12,4},{1,9},{5,13},{9,1},{13,5},{2,10},{6,14},... | collective-permute-start | bytes 49160 | tf_op jit(solution)/shard_map/ppermute | solution.py:394
  17.7 2.3 %collective-permute-start.3 = (f32[8,512]{1,0:T(8,128)S(1)}, f32[8,512]{1,0:T(8,128)S(1)}, u32[]{:S(2)}, u32[]{:S(2)}) collective-permute-start(f32[8,512]{1,0:T(8,128)S(1)} %get-tuple-element.33.refs_0_), channel_id=1, source_target_pairs={{0,4},{4,0},{8,12},{12,8},{1,5},{5,1},{9,13},{13,9},{2,6},{6,2},{1... | collective-permute-start | bytes 49160 | tf_op jit(solution)/shard_map/ppermute | solution.py:394
  20.5 5.6 %collective-permute-start.8 = (f32[8,512]{1,0:T(8,128)S(1)}, f32[8,512]{1,0:T(8,128)S(1)}, u32[]{:S(2)}, u32[]{:S(2)}) collective-permute-start(f32[8,512]{1,0:T(8,128)S(1)} %get-tuple-element.39.refs_0_), channel_id=1, source_target_pairs={{0,3},{1,2},{2,1},{3,0},{4,7},{5,6},{6,5},{7,4},{8,11},{9,10},{10,... | collective-permute-start | bytes 49160 | tf_op jit(solution)/shard_map/ppermute | solution.py:394
  22.1 4.7 %collective-permute-start.7 = (f32[8,512]{1,0:T(8,128)S(1)}, f32[8,512]{1,0:T(8,128)S(1)}, u32[]{:S(2)}, u32[]{:S(2)}) collective-permute-start(f32[8,512]{1,0:T(8,128)S(1)} %get-tuple-element.39.refs_0_), channel_id=1, source_target_pairs={{0,2},{1,3},{2,0},{3,1},{4,6},{5,7},{6,4},{7,5},{8,10},{9,11},{10,... | collective-permute-start | bytes 49160 | tf_op jit(solution)/shard_map/ppermute | solution.py:394
  22.7 4.2 %collective-permute-start.6 = (f32[8,512]{1,0:T(8,128)S(1)}, f32[8,512]{1,0:T(8,128)S(1)}, u32[]{:S(2)}, u32[]{:S(2)}) collective-permute-start(f32[8,512]{1,0:T(8,128)S(1)} %get-tuple-element.39.refs_0_), channel_id=1, source_target_pairs={{0,1},{1,0},{2,3},{3,2},{4,5},{5,4},{6,7},{7,6},{8,9},{9,8},{10,11... | collective-permute-start | bytes 49160 | tf_op jit(solution)/shard_map/ppermute | solution.py:394
  27.4 3.4 %collective-permute-start.11 = (f32[8,512]{1,0:T(8,128)S(1)}, f32[8,512]{1,0:T(8,128)S(1)}, u32[]{:S(2)}, u32[]{:S(2)}) collective-permute-start(f32[8,512]{1,0:T(8,128)S(1)} %shard_map.81.refs_0_.refs_4_), channel_id=1, source_target_pairs={{0,12},{4,8},{8,4},{12,0},{1,13},{5,9},{9,5},{13,1},{2,14},{6,10},... | collective-permute-start | bytes 49160 | tf_op jit(solution)/shard_map/ppermute | solution.py:394
  27.5 3.8 %collective-permute-start.10 = (f32[8,512]{1,0:T(8,128)S(1)}, f32[8,512]{1,0:T(8,128)S(1)}, u32[]{:S(2)}, u32[]{:S(2)}) collective-permute-start(f32[8,512]{1,0:T(8,128)S(1)} %shard_map.81.refs_0_.refs_4_), channel_id=1, source_target_pairs={{0,8},{4,12},{8,0},{12,4},{1,9},{5,13},{9,1},{13,5},{2,10},{6,14},... | collective-permute-start | bytes 49160 | tf_op jit(solution)/shard_map/ppermute | solution.py:394
  29.0 2.3 %collective-permute-start.9 = (f32[8,512]{1,0:T(8,128)S(1)}, f32[8,512]{1,0:T(8,128)S(1)}, u32[]{:S(2)}, u32[]{:S(2)}) collective-permute-start(f32[8,512]{1,0:T(8,128)S(1)} %shard_map.81.refs_0_.refs_4_), channel_id=1, source_target_pairs={{0,4},{4,0},{8,12},{12,8},{1,5},{5,1},{9,13},{13,9},{2,6},{6,2},{1... | collective-permute-start | bytes 49160 | tf_op jit(solution)/shard_map/ppermute | solution.py:394
  31.3 10.2 %copy-start = (s32[8192]{0:T(1024)S(1)}, s32[8192]{0:T(1024)}, u32[]{:S(2)}) copy-start(s32[8192]{0:T(1024)} %param.9) | copy-start | bytes 98308
  31.3 10.5 %copy-start.1 = (s32[8192]{0:T(1024)S(1)}, s32[8192]{0:T(1024)}, u32[]{:S(2)}) copy-start(s32[8192]{0:T(1024)} %param.8) | copy-start | bytes 98308
  31.8 5.7 %collective-permute-start.14 = (f32[8,512]{1,0:T(8,128)S(1)}, f32[8,512]{1,0:T(8,128)S(1)}, u32[]{:S(2)}, u32[]{:S(2)}) collective-permute-start(f32[8,512]{1,0:T(8,128)S(1)} %get-tuple-element.44.refs_4_.refs_0_), channel_id=1, source_target_pairs={{0,3},{1,2},{2,1},{3,0},{4,7},{5,6},{6,5},{7,4},{8,11},{9,10},{10,... | collective-permute-start | bytes 49160 | tf_op jit(solution)/shard_map/ppermute | solution.py:394
  34.2 4.7 %collective-permute-start.13 = (f32[8,512]{1,0:T(8,128)S(1)}, f32[8,512]{1,0:T(8,128)S(1)}, u32[]{:S(2)}, u32[]{:S(2)}) collective-permute-start(f32[8,512]{1,0:T(8,128)S(1)} %get-tuple-element.44.refs_4_.refs_0_), channel_id=1, source_target_pairs={{0,2},{1,3},{2,0},{3,1},{4,6},{5,7},{6,4},{7,5},{8,10},{9,11},{10,... | collective-permute-start | bytes 49160 | tf_op jit(solution)/shard_map/ppermute | solution.py:394
  35.1 3.9 %collective-permute-start.12 = (f32[8,512]{1,0:T(8,128)S(1)}, f32[8,512]{1,0:T(8,128)S(1)}, u32[]{:S(2)}, u32[]{:S(2)}) collective-permute-start(f32[8,512]{1,0:T(8,128)S(1)} %get-tuple-element.44.refs_4_.refs_0_), channel_id=1, source_target_pairs={{0,1},{1,0},{2,3},{3,2},{4,5},{5,4},{6,7},{7,6},{8,9},{9,8},{10,11... | collective-permute-start | bytes 49160 | tf_op jit(solution)/shard_map/ppermute | solution.py:394
  39.5 3.4 %collective-permute-start.17 = (f32[8,512]{1,0:T(8,128)S(1)}, f32[8,512]{1,0:T(8,128)S(1)}, u32[]{:S(2)}, u32[]{:S(2)}) collective-permute-start(f32[8,512]{1,0:T(8,128)S(1)} %shard_map.84.refs_0_), channel_id=1, source_target_pairs={{0,12},{4,8},{8,4},{12,0},{1,13},{5,9},{9,5},{13,1},{2,14},{6,10},... | collective-permute-start | bytes 49160 | tf_op jit(solution)/shard_map/ppermute | solution.py:394
  39.6 3.8 %collective-permute-start.16 = (f32[8,512]{1,0:T(8,128)S(1)}, f32[8,512]{1,0:T(8,128)S(1)}, u32[]{:S(2)}, u32[]{:S(2)}) collective-permute-start(f32[8,512]{1,0:T(8,128)S(1)} %shard_map.84.refs_0_), channel_id=1, source_target_pairs={{0,8},{4,12},{8,0},{12,4},{1,9},{5,13},{9,1},{13,5},{2,10},{6,14},... | collective-permute-start | bytes 49160 | tf_op jit(solution)/shard_map/ppermute | solution.py:394
  41.1 2.3 %collective-permute-start.15 = (f32[8,512]{1,0:T(8,128)S(1)}, f32[8,512]{1,0:T(8,128)S(1)}, u32[]{:S(2)}, u32[]{:S(2)}) collective-permute-start(f32[8,512]{1,0:T(8,128)S(1)} %shard_map.84.refs_0_), channel_id=1, source_target_pairs={{0,4},{4,0},{8,12},{12,8},{1,5},{5,1},{9,13},{13,9},{2,6},{6,2},{1... | collective-permute-start | bytes 49160 | tf_op jit(solution)/shard_map/ppermute | solution.py:394

commit v3 on v2

--- a/solution.py
+++ b/solution.py
@@ -57,6 +57,15 @@
         number = jnp.full((1, LANES), tiles[which, slot], jnp.int32)
         pack[note_at(slots, slot)] = number.astype(jnp.float32)
     pack[note_at(slots, slots)] = total_of(counts)
+
+
+def staggered(slots, raise_top, add_mass):
+    top = raise_top(0)
+    for slot in range(1, slots):
+        later = raise_top(slot)
+        add_mass(slot - 1, top)
+        top = later
+    add_mass(slots - 1, top)
 
 
 def first_kernel(
@@ -97,9 +106,13 @@
     for slot in range(fixed, slots):
         copies.append(fetch(slot, [tiles[which, slot] for which in range(2)]))
     write_notes(pack, tiles, 0, item_count[...])
-    for slot in range(slots):
-        for copy in copies[slot]:
-            copy.wait()
+    early = max(1, 3 * fixed // 4)
+
+    def raise_top(slot):
+        if slot in (0, early):
+            for pair in copies[:early] if slot == 0 else copies[early:]:
+                for copy in pair:
+                    copy.wait()
         user_block = users[slot]
         top = jnp.full((8, CLUSTER), lowest, jnp.float32)
         for block in range(BLOCKS):
@@ -108,16 +121,20 @@
                 items[slot, rows, :], user_block, (((1,), (1,)), ((), ())),
                 preferred_element_type=jnp.float32,
             ) * INTO
-            scores[rows, :] = part
+            scores[slot, rows, :] = part
             top = jnp.maximum(top, jnp.max(part.reshape(LANES // 8, 8, CLUSTER), axis=0))
-        top = jnp.max(top, axis=0, keepdims=True)
+        return jnp.max(top, axis=0, keepdims=True)
+
+    def add_mass(slot, top):
         mass = jnp.zeros((8, CLUSTER), jnp.float32)
         for block in range(BLOCKS):
             rows = slice(block * LANES, (block + 1) * LANES)
-            terms = jnp.exp2(scores[rows, :] - top)
+            terms = jnp.exp2(scores[slot, rows, :] - top)
             mass += jnp.sum(terms.reshape(LANES // 8, 8, CLUSTER), axis=0)
         log_mass = top + jnp.log2(jnp.sum(mass, axis=0, keepdims=True))
         pack[slot : slot + 1, :] = jnp.where(filled[0, 0] > slot, log_mass, lowest)
+
+    staggered(slots, raise_top, add_mass)
 
 
 def setup_kernel(
@@ -236,14 +253,17 @@
     potential[...] = jnp.log2(counts[...]) - log_merge(packs, chosen, slots, EVERY, ROWS)
     pack[...] = notes[...]
     tops[...] = jnp.full(PACK, lowest, jnp.float32)
-    for slot in range(slots):
+
+    def raise_top(slot):
         top = jnp.full((8, CLUSTER), lowest, jnp.float32)
         for block in range(BLOCKS):
             rows = slice(block * LANES, (block + 1) * LANES)
             part = table[slot, rows, :] + wide(down_rows(potential, slot, block))
             terms[slot, rows, :] = part
             top = jnp.maximum(top, jnp.max(part.reshape(LANES // 8, 8, CLUSTER), axis=0))
-        top = jnp.max(top, axis=0, keepdims=True)
+        return jnp.max(top, axis=0, keepdims=True)
+
+    def add_mass(slot, top):
         mass = jnp.zeros((8, CLUSTER), jnp.float32)
         for block in range(BLOCKS):
             rows = slice(block * LANES, (block + 1) * LANES)
@@ -254,6 +274,8 @@
         on = active[slot : slot + 1, :] > 0.0
         pack[slot : slot + 1, :] = jnp.where(on, log_mass, lowest)
         tops[slot : slot + 1, :] = jnp.where(on, top, lowest)
+
+    staggered(slots, raise_top, add_mass)
 
 
 def row_sums(terms, factor, pack):
@@ -433,7 +455,7 @@
             [
                 small,
                 near(item_counts.shape, jnp.int32),
-                near((CLUSTER, CLUSTER)),
+                near(tall),
                 pltpu.SemaphoreType.DMA((2,)),
                 pltpu.SemaphoreType.DMA((slots, 2)),
             ],

time: 44.4 us -> 43.7 us (0.984)
  Pallas kernels: 10.5 us -> 9.79 us
    pallas_call x10, Pallas kernels: 10.5 us -> 9.79 us  [call(): pl.pallas_call(kernel, out_shape=outs, in_specs=specs or [HERE] * len(ope...]
where the time goes in v3:
time: 43.7 us; the launch traced here: 43.4 us
  starting transfers between devices  20.5 us (47%)
  waiting for transfers between devices  11.8 us (27%)
  Pallas kernels  9.79 us (22%)
  between operations  1.38 us (3%)
    ppermute x18, starting transfers between devices, exchange(): packs.append(keep(lax.ppermute(pack, axis, route)))  20.5 us
    ppermute x18, waiting for transfers between devices, exchange(): packs.append(keep(lax.ppermute(pack, axis, route)))  11.8 us
    pallas_call x10, Pallas kernels, call(): pl.pallas_call(kernel, out_shape=outs, in_specs=specs or [HERE] * len(ope...  9.79 us
  transfers between devices with their start and end apart: 18, of which 13 were waited for; matrix products, arithmetic and copies ran while one was open for 0% of the time, Pallas kernels for 6%

profile of v3, /device:TPU:0, one launch (start us, length us, event | category | flops | bytes accessed | tf_op | source)
XLA Modules:
  0.0 43.4 jit_solution(17219762699304793169)
XLA Ops:
  1.3 3.0 %shard_map.77 = (f32[8,512]{1,0:T(8,128)S(1)}, bf16[5,512,128]{2,1,0:T(8,128)(2,1)S(1)}, bf16[5,512,128]{2,1,0:T(8,128)(2,1)S(1)}) custom-call(s32[2,5]{1,0:T(2,128)} %bitcast.14, s32[1,1]{1,0:T(1,128)S(6)} %copy.8.refs_1_.filled, bf16[8192,128]{1,0:T(8,128)(2,1)} %refs_2_.1, bf16[8192,128]{1,0:T(8,128)(2,1)} %refs_3_.1, s32[64,128]{1,0:T(8,128)} %bitcast.7), custom_call_target="tpu_custom_call" | custom-call | tf_op jit(solution)/shard_map/pallas_call | solution.py:421
  4.3 5.1 %collective-permute-start.2 = (f32[8,512]{1,0:T(8,128)S(1)}, f32[8,512]{1,0:T(8,128)S(1)}, u32[]{:S(2)}, u32[]{:S(2)}) collective-permute-start(f32[8,512]{1,0:T(8,128)S(1)} %get-tuple-element.25.refs_0_), channel_id=1, source_target_pairs={{0,3},{1,2},{2,1},{3,0},{4,7},{5,6},{6,5},{7,4},{8,11},{9,10},{10,... | collective-permute-start | bytes 49160 | tf_op jit(solution)/shard_map/ppermute | solution.py:416
  9.4 0.0 collective-permute-start.1
  9.4 0.6 %collective-permute-start = (f32[8,512]{1,0:T(8,128)S(1)}, f32[8,512]{1,0:T(8,128)S(1)}, u32[]{:S(2)}, u32[]{:S(2)}) collective-permute-start(f32[8,512]{1,0:T(8,128)S(1)} %get-tuple-element.25.refs_0_), channel_id=1, source_target_pairs={{0,1},{1,0},{2,3},{3,2},{4,5},{5,4},{6,7},{7,6},{8,9},{9,8},{10,11... | collective-permute-start | bytes 49160 | tf_op jit(solution)/shard_map/ppermute | solution.py:416
  10.1 1.6 %shard_map.78 = (f32[5,512,512]{2,1,0:T(8,128)S(1)}, f32[8,512]{1,0:T(8,128)S(1)}, f32[8,512]{1,0:T(8,128)S(1)}, f32[8,128]{1,0:T(8,128)S(1)}, f32[8,128]{1,0:T(...) custom-call(s32[2,5]{1,0:T(2,128)} %bitcast.15, s32[1,1]{1,0:T(1,128)S(6)} %copy.8.refs_1_.filled, ...), custom_call_target="tpu_custom_call" | custom-call | tf_op jit(solution)/shard_map/pallas_call | solution.py:421
  11.7 0.0 collective-permute-done.2.refs_3_
  11.7 2.4 %collective-permute-done.1.refs_2_ = f32[8,512]{1,0:T(8,128)S(1)} collective-permute-done((f32[8,512]{1,0:T(8,128)S(1)}, f32[8,512]{1,0:T(8,128)S(1)}, u32[]{:S(2)}, u32[]{:S(2)}) %collective-permute-start.1) | collective-permute-done | bytes 16416 | tf_op jit(solution)/shard_map/ppermute | solution.py:416
  14.1 0.0 collective-permute-done.refs_1_
  14.1 1.3 %shard_map.79 = (f32[8,512]{1,0:T(8,128)S(1)}, f32[5,512,512]{2,1,0:T(8,128)S(1)}, f32[8,512]{1,0:T(8,128)S(1)}, f32[20,8,128]{2,1,0:T(8,128)S(1)}, f32[8,128]{1,0:T(8,128)S(1)}) custom-call(f32[8,512]{1,0:T(8,128)S(1)} %get-tuple-element.25.refs_0_, f32[8,512]{1,0:T(8,128)S(1)} %collective-permute-done.refs_1_, ...), custom_call_target="tpu_custom_call" | custom-call | tf_op jit(solution)/shard_map/pallas_call | solution.py:421
  15.4 0.1 collective-permute-start.5
  15.5 1.6 %collective-permute-start.4 = (f32[8,512]{1,0:T(8,128)S(1)}, f32[8,512]{1,0:T(8,128)S(1)}, u32[]{:S(2)}, u32[]{:S(2)}) collective-permute-start(f32[8,512]{1,0:T(8,128)S(1)} %get-tuple-element.33.refs_0_), channel_id=1, source_target_pairs={{0,8},{4,12},{8,0},{12,4},{1,9},{5,13},{9,1},{13,5},{2,10},{6,14},... | collective-permute-start | bytes 49160 | tf_op jit(solution)/shard_map/ppermute | solution.py:416
  17.0 0.3 collective-permute-start.3
  17.3 1.4 %collective-permute-done.5.refs_3_ = f32[8,512]{1,0:T(8,128)S(1)} collective-permute-done((f32[8,512]{1,0:T(8,128)S(1)}, f32[8,512]{1,0:T(8,128)S(1)}, u32[]{:S(2)}, u32[]{:S(2)}) %collective-permute-start.5) | collective-permute-done | bytes 16416 | tf_op jit(solution)/shard_map/ppermute | solution.py:416
  18.7 0.5 %collective-permute-done.4.refs_2_ = f32[8,512]{1,0:T(8,128)S(1)} collective-permute-done((f32[8,512]{1,0:T(8,128)S(1)}, f32[8,512]{1,0:T(8,128)S(1)}, u32[]{:S(2)}, u32[]{:S(2)}) %collective-permute-start.4) | collective-permute-done | bytes 16416 | tf_op jit(solution)/shard_map/ppermute | solution.py:416
  19.3 0.0 collective-permute-done.3.refs_1_
  19.3 0.5 %shard_map.80 = (f32[8,512]{1,0:T(8,128)S(1)}, f32[8,512]{1,0:T(8,128)S(1)}, f32[20,8,128]{2,1,0:T(8,128)S(1)}, f32[8,128]{1,0:T(8,128)S(1)}) custom-call(f32[8,512]{1,0:T(8,128)S(1)} %get-tuple-element.33.refs_0_, f32[8,512]{1,0:T(8,128)S(1)} %collective-permute-done.3.refs_1_, f32[8,512]{1,0:T(8,128)S(1)} %collective-permute-done.4.refs_2_, ...), custom_call_target="tpu_custom_call" | custom-call | tf_op jit(solution)/shard_map/pallas_call | solution.py:421
  19.8 1.5 %collective-permute-start.8 = (f32[8,512]{1,0:T(8,128)S(1)}, f32[8,512]{1,0:T(8,128)S(1)}, u32[]{:S(2)}, u32[]{:S(2)}) collective-permute-start(f32[8,512]{1,0:T(8,128)S(1)} %get-tuple-element.39.refs_0_), channel_id=1, source_target_pairs={{0,3},{1,2},{2,1},{3,0},{4,7},{5,6},{6,5},{7,4},{8,11},{9,10},{10,... | collective-permute-start | bytes 49160 | tf_op jit(solution)/shard_map/ppermute | solution.py:416
  21.4 0.6 %collective-permute-start.7 = (f32[8,512]{1,0:T(8,128)S(1)}, f32[8,512]{1,0:T(8,128)S(1)}, u32[]{:S(2)}, u32[]{:S(2)}) collective-permute-start(f32[8,512]{1,0:T(8,128)S(1)} %get-tuple-element.39.refs_0_), channel_id=1, source_target_pairs={{0,2},{1,3},{2,0},{3,1},{4,6},{5,7},{6,4},{7,5},{8,10},{9,11},{10,... | collective-permute-start | bytes 49160 | tf_op jit(solution)/shard_map/ppermute | solution.py:416
  22.0 2.3 %collective-permute-start.6 = (f32[8,512]{1,0:T(8,128)S(1)}, f32[8,512]{1,0:T(8,128)S(1)}, u32[]{:S(2)}, u32[]{:S(2)}) collective-permute-start(f32[8,512]{1,0:T(8,128)S(1)} %get-tuple-element.39.refs_0_), channel_id=1, source_target_pairs={{0,1},{1,0},{2,3},{3,2},{4,5},{5,4},{6,7},{7,6},{8,9},{9,8},{10,11... | collective-permute-start | bytes 49160 | tf_op jit(solution)/shard_map/ppermute | solution.py:416
  24.3 1.2 %collective-permute-done.8.refs_3_ = f32[8,512]{1,0:T(8,128)S(1)} collective-permute-done((f32[8,512]{1,0:T(8,128)S(1)}, f32[8,512]{1,0:T(8,128)S(1)}, u32[]{:S(2)}, u32[]{:S(2)}) %collective-permute-start.8) | collective-permute-done | bytes 16416 | tf_op jit(solution)/shard_map/ppermute | solution.py:416
  25.4 0.6 %collective-permute-done.7.refs_2_ = f32[8,512]{1,0:T(8,128)S(1)} collective-permute-done((f32[8,512]{1,0:T(8,128)S(1)}, f32[8,512]{1,0:T(8,128)S(1)}, u32[]{:S(2)}, u32[]{:S(2)}) %collective-permute-start.7) | collective-permute-done | bytes 16416 | tf_op jit(solution)/shard_map/ppermute | solution.py:416
  26.0 0.2 collective-permute-done.6.refs_1_
  26.2 0.5 %shard_map.81.refs_0_.refs_4_ = f32[8,512]{1,0:T(8,128)S(1)} custom-call(f32[8,512]{1,0:T(8,128)S(1)} %get-tuple-element.39.refs_0_, f32[8,512]{1,0:T(8,128)S(1)} %collective-permute-done.6.refs_1_, f32[8,512]{1,0:T(8,128)S(1)} %collective-permute-done.7.refs_2_, f32[8,512]{1,0:T(8,128)S(1)} %collective-permute-done.8.refs_3_, ...), custom_call_target="tpu_custom_call" | custom-call | tf_op jit(solution)/shard_map/pallas_call | solution.py:421
  26.7 0.1 collective-permute-start.11
  26.7 1.5 %collective-permute-start.10 = (f32[8,512]{1,0:T(8,128)S(1)}, f32[8,512]{1,0:T(8,128)S(1)}, u32[]{:S(2)}, u32[]{:S(2)}) collective-permute-start(f32[8,512]{1,0:T(8,128)S(1)} %shard_map.81.refs_0_.refs_4_), channel_id=1, source_target_pairs={{0,8},{4,12},{8,0},{12,4},{1,9},{5,13},{9,1},{13,5},{2,10},{6,14},... | collective-permute-start | bytes 49160 | tf_op jit(solution)/shard_map/ppermute | solution.py:416
  28.3 0.3 collective-permute-start.9
  28.6 1.4 %collective-permute-done.11.refs_3_.refs_7_ = f32[8,512]{1,0:T(8,128)S(1)} collective-permute-done((f32[8,512]{1,0:T(8,128)S(1)}, f32[8,512]{1,0:T(8,128)S(1)}, u32[]{:S(2)}, u32[]{:S(2)}) %collective-permute-start.11) | collective-permute-done | bytes 16416 | tf_op jit(solution)/shard_map/ppermute | solution.py:416
  30.0 0.5 %collective-permute-done.10.refs_2_.refs_6_ = f32[8,512]{1,0:T(8,128)S(1)} collective-permute-done((f32[8,512]{1,0:T(8,128)S(1)}, f32[8,512]{1,0:T(8,128)S(1)}, u32[]{:S(2)}, u32[]{:S(2)}) %collective-permute-start.10) | collective-permute-done | bytes 16416 | tf_op jit(solution)/shard_map/ppermute | solution.py:416
  30.5 0.0 collective-permute-done.9.refs_1_.refs_5_
  30.6 0.5 %shard_map.82 = (f32[8,512]{1,0:T(8,128)S(1)}, f32[8,512]{1,0:T(8,128)S(1)}) custom-call(f32[8,512]{1,0:T(8,128)S(1)} %shard_map.81.refs_0_.refs_4_, f32[8,512]{1,0:T(8,128)S(1)} %collective-permute-done.9.refs_1_.refs_5_, f32[8,512]{1,0:T(8,128)S(1)} %collective-permute-done.10.refs_2_.refs_6_, f32[8,512]{1,0:T(8,128)S(1)} %collective-permute-done.11.refs_3_.refs_7_, ...), custom_call_target="tpu_custom_call" | custom-call | tf_op jit(solution)/shard_map/pallas_call | solution.py:421
  31.0 2.5 %collective-permute-start.14 = (f32[8,512]{1,0:T(8,128)S(1)}, f32[8,512]{1,0:T(8,128)S(1)}, u32[]{:S(2)}, u32[]{:S(2)}) collective-permute-start(f32[8,512]{1,0:T(8,128)S(1)} %get-tuple-element.44.refs_4_.refs_0_), channel_id=1, source_target_pairs={{0,3},{1,2},{2,1},{3,0},{4,7},{5,6},{6,5},{7,4},{8,11},{9,10},{10,... | collective-permute-start | bytes 49160 | tf_op jit(solution)/shard_map/ppermute | solution.py:416
  33.5 0.9 %collective-permute-start.13 = (f32[8,512]{1,0:T(8,128)S(1)}, f32[8,512]{1,0:T(8,128)S(1)}, u32[]{:S(2)}, u32[]{:S(2)}) collective-permute-start(f32[8,512]{1,0:T(8,128)S(1)} %get-tuple-element.44.refs_4_.refs_0_), channel_id=1, source_target_pairs={{0,2},{1,3},{2,0},{3,1},{4,6},{5,7},{6,4},{7,5},{8,10},{9,11},{10,... | collective-permute-start | bytes 49160 | tf_op jit(solution)/shard_map/ppermute | solution.py:416
  34.4 1.1 %collective-permute-start.12 = (f32[8,512]{1,0:T(8,128)S(1)}, f32[8,512]{1,0:T(8,128)S(1)}, u32[]{:S(2)}, u32[]{:S(2)}) collective-permute-start(f32[8,512]{1,0:T(8,128)S(1)} %get-tuple-element.44.refs_4_.refs_0_), channel_id=1, source_target_pairs={{0,1},{1,0},{2,3},{3,2},{4,5},{5,4},{6,7},{7,6},{8,9},{9,8},{10,11... | collective-permute-start | bytes 49160 | tf_op jit(solution)/shard_map/ppermute | solution.py:416
  35.5 1.3 %collective-permute-done.14.refs_7_.refs_3_ = f32[8,512]{1,0:T(8,128)S(1)} collective-permute-done((f32[8,512]{1,0:T(8,128)S(1)}, f32[8,512]{1,0:T(8,128)S(1)}, u32[]{:S(2)}, u32[]{:S(2)}) %collective-permute-start.14) | collective-permute-done | bytes 16416 | tf_op jit(solution)/shard_map/ppermute | solution.py:416
  36.8 1.4 %collective-permute-done.13.refs_6_.refs_2_ = f32[8,512]{1,0:T(8,128)S(1)} collective-permute-done((f32[8,512]{1,0:T(8,128)S(1)}, f32[8,512]{1,0:T(8,128)S(1)}, u32[]{:S(2)}, u32[]{:S(2)}) %collective-permute-start.13) | collective-permute-done | bytes 16416 | tf_op jit(solution)/shard_map/ppermute | solution.py:416
  38.2 0.2 collective-permute-done.12.refs_5_.refs_1_
  38.3 0.5 %shard_map.84.refs_0_ = f32[8,512]{1,0:T(8,128)S(1)} custom-call(f32[8,512]{1,0:T(8,128)S(1)} %get-tuple-element.44.refs_4_.refs_0_, f32[8,512]{1,0:T(8,128)S(1)} %collective-permute-done.12.refs_5_.refs_1_, f32[8,512]{1,0:T(8,128)S(1)} %collective-permute-done.13.refs_6_.refs_2_, f32[8,512]{1,0:T(8,128)S(1)} %collective-permute-done.14.refs_7_.refs_3_, ...), custom_call_target="tpu_custom_call" | custom-call | tf_op jit(solution)/shard_map/pallas_call | solution.py:421
  38.8 0.1 collective-permute-start.17
  38.9 1.5 %collective-permute-start.16 = (f32[8,512]{1,0:T(8,128)S(1)}, f32[8,512]{1,0:T(8,128)S(1)}, u32[]{:S(2)}, u32[]{:S(2)}) collective-permute-start(f32[8,512]{1,0:T(8,128)S(1)} %shard_map.84.refs_0_), channel_id=1, source_target_pairs={{0,8},{4,12},{8,0},{12,4},{1,9},{5,13},{9,1},{13,5},{2,10},{6,14},... | collective-permute-start | bytes 49160 | tf_op jit(solution)/shard_map/ppermute | solution.py:416
  40.4 0.3 collective-permute-start.15
  40.8 0.0 copy-done
  40.8 0.3 shard_map.85
  41.0 0.0 copy-done.1
  41.0 0.9 %shard_map.83 = f32[64,128]{1,0:T(8,128)} custom-call(f32[8,512]{1,0:T(8,128)S(1)} %get-tuple-element.25.refs_0_, f32[8,512]{1,0:T(8,128)S(1)} %collective-permute-done.refs_1_, f32[8,512]{1,0:T(8,128)S(1)} %collective-permute-done.1.refs_2_, f32[8,512]{1,0:T(8,128)S(1)} %collective-permute-done.2.refs_3_, f32[8,512]{1,0:T(8,128)S(1)} %get-tuple-element.44.refs_4_.refs_0_, ...), custom_call_target="tpu_custom_call" | custom-call | tf_op jit(solution)/shard_map/pallas_call | solution.py:421
  41.9 0.3 collective-permute-done.17.refs_3_
  42.2 0.5 %collective-permute-done.16.refs_2_ = f32[8,512]{1,0:T(8,128)S(1)} collective-permute-done((f32[8,512]{1,0:T(8,128)S(1)}, f32[8,512]{1,0:T(8,128)S(1)}, u32[]{:S(2)}, u32[]{:S(2)}) %collective-permute-start.16) | collective-permute-done | bytes 16416 | tf_op jit(solution)/shard_map/ppermute | solution.py:416
  42.7 0.0 collective-permute-done.15.refs_1_
  42.7 0.7 %shard_map.86 = f32[64,128]{1,0:T(8,128)} custom-call(f32[8,512]{1,0:T(8,128)S(1)} %shard_map.84.refs_0_, f32[8,512]{1,0:T(8,128)S(1)} %collective-permute-done.15.refs_1_, f32[8,512]{1,0:T(8,128)S(1)} %collective-permute-done.16.refs_2_, f32[8,512]{1,0:T(8,128)S(1)} %collective-permute-done.17.refs_3_, f32[64,128]{1,0:T(8,128)S(1)} %get-tuple-element.46.refs_4_, ...), custom_call_target="tpu_custom_call" | custom-call | tf_op jit(solution)/shard_map/pallas_call | solution.py:421
  (2 shorter events, 0.0 us)
Async XLA Ops:
  4.3 7.4 %collective-permute-start.2 = (f32[8,512]{1,0:T(8,128)S(1)}, f32[8,512]{1,0:T(8,128)S(1)}, u32[]{:S(2)}, u32[]{:S(2)}) collective-permute-start(f32[8,512]{1,0:T(8,128)S(1)} %get-tuple-element.25.refs_0_), channel_id=1, source_target_pairs={{0,3},{1,2},{2,1},{3,0},{4,7},{5,6},{6,5},{7,4},{8,11},{9,10},{10,... | collective-permute-start | bytes 49160 | tf_op jit(solution)/shard_map/ppermute | solution.py:416
  9.4 4.6 %collective-permute-start.1 = (f32[8,512]{1,0:T(8,128)S(1)}, f32[8,512]{1,0:T(8,128)S(1)}, u32[]{:S(2)}, u32[]{:S(2)}) collective-permute-start(f32[8,512]{1,0:T(8,128)S(1)} %get-tuple-element.25.refs_0_), channel_id=1, source_target_pairs={{0,2},{1,3},{2,0},{3,1},{4,6},{5,7},{6,4},{7,5},{8,10},{9,11},{10,... | collective-permute-start | bytes 49160 | tf_op jit(solution)/shard_map/ppermute | solution.py:416
  9.4 4.6 %collective-permute-start = (f32[8,512]{1,0:T(8,128)S(1)}, f32[8,512]{1,0:T(8,128)S(1)}, u32[]{:S(2)}, u32[]{:S(2)}) collective-permute-start(f32[8,512]{1,0:T(8,128)S(1)} %get-tuple-element.25.refs_0_), channel_id=1, source_target_pairs={{0,1},{1,0},{2,3},{3,2},{4,5},{5,4},{6,7},{7,6},{8,9},{9,8},{10,11... | collective-permute-start | bytes 49160 | tf_op jit(solution)/shard_map/ppermute | solution.py:416
  15.4 3.4 %collective-permute-start.5 = (f32[8,512]{1,0:T(8,128)S(1)}, f32[8,512]{1,0:T(8,128)S(1)}, u32[]{:S(2)}, u32[]{:S(2)}) collective-permute-start(f32[8,512]{1,0:T(8,128)S(1)} %get-tuple-element.33.refs_0_), channel_id=1, source_target_pairs={{0,12},{4,8},{8,4},{12,0},{1,13},{5,9},{9,5},{13,1},{2,14},{6,10},... | collective-permute-start | bytes 49160 | tf_op jit(solution)/shard_map/ppermute | solution.py:416
  15.5 3.8 %collective-permute-start.4 = (f32[8,512]{1,0:T(8,128)S(1)}, f32[8,512]{1,0:T(8,128)S(1)}, u32[]{:S(2)}, u32[]{:S(2)}) collective-permute-start(f32[8,512]{1,0:T(8,128)S(1)} %get-tuple-element.33.refs_0_), channel_id=1, source_target_pairs={{0,8},{4,12},{8,0},{12,4},{1,9},{5,13},{9,1},{13,5},{2,10},{6,14},... | collective-permute-start | bytes 49160 | tf_op jit(solution)/shard_map/ppermute | solution.py:416
  17.0 2.3 %collective-permute-start.3 = (f32[8,512]{1,0:T(8,128)S(1)}, f32[8,512]{1,0:T(8,128)S(1)}, u32[]{:S(2)}, u32[]{:S(2)}) collective-permute-start(f32[8,512]{1,0:T(8,128)S(1)} %get-tuple-element.33.refs_0_), channel_id=1, source_target_pairs={{0,4},{4,0},{8,12},{12,8},{1,5},{5,1},{9,13},{13,9},{2,6},{6,2},{1... | collective-permute-start | bytes 49160 | tf_op jit(solution)/shard_map/ppermute | solution.py:416
  19.8 5.6 %collective-permute-start.8 = (f32[8,512]{1,0:T(8,128)S(1)}, f32[8,512]{1,0:T(8,128)S(1)}, u32[]{:S(2)}, u32[]{:S(2)}) collective-permute-start(f32[8,512]{1,0:T(8,128)S(1)} %get-tuple-element.39.refs_0_), channel_id=1, source_target_pairs={{0,3},{1,2},{2,1},{3,0},{4,7},{5,6},{6,5},{7,4},{8,11},{9,10},{10,... | collective-permute-start | bytes 49160 | tf_op jit(solution)/shard_map/ppermute | solution.py:416
  21.4 4.7 %collective-permute-start.7 = (f32[8,512]{1,0:T(8,128)S(1)}, f32[8,512]{1,0:T(8,128)S(1)}, u32[]{:S(2)}, u32[]{:S(2)}) collective-permute-start(f32[8,512]{1,0:T(8,128)S(1)} %get-tuple-element.39.refs_0_), channel_id=1, source_target_pairs={{0,2},{1,3},{2,0},{3,1},{4,6},{5,7},{6,4},{7,5},{8,10},{9,11},{10,... | collective-permute-start | bytes 49160 | tf_op jit(solution)/shard_map/ppermute | solution.py:416
  22.0 4.2 %collective-permute-start.6 = (f32[8,512]{1,0:T(8,128)S(1)}, f32[8,512]{1,0:T(8,128)S(1)}, u32[]{:S(2)}, u32[]{:S(2)}) collective-permute-start(f32[8,512]{1,0:T(8,128)S(1)} %get-tuple-element.39.refs_0_), channel_id=1, source_target_pairs={{0,1},{1,0},{2,3},{3,2},{4,5},{5,4},{6,7},{7,6},{8,9},{9,8},{10,11... | collective-permute-start | bytes 49160 | tf_op jit(solution)/shard_map/ppermute | solution.py:416
  26.7 3.4 %collective-permute-start.11 = (f32[8,512]{1,0:T(8,128)S(1)}, f32[8,512]{1,0:T(8,128)S(1)}, u32[]{:S(2)}, u32[]{:S(2)}) collective-permute-start(f32[8,512]{1,0:T(8,128)S(1)} %shard_map.81.refs_0_.refs_4_), channel_id=1, source_target_pairs={{0,12},{4,8},{8,4},{12,0},{1,13},{5,9},{9,5},{13,1},{2,14},{6,10},... | collective-permute-start | bytes 49160 | tf_op jit(solution)/shard_map/ppermute | solution.py:416
  26.7 3.8 %collective-permute-start.10 = (f32[8,512]{1,0:T(8,128)S(1)}, f32[8,512]{1,0:T(8,128)S(1)}, u32[]{:S(2)}, u32[]{:S(2)}) collective-permute-start(f32[8,512]{1,0:T(8,128)S(1)} %shard_map.81.refs_0_.refs_4_), channel_id=1, source_target_pairs={{0,8},{4,12},{8,0},{12,4},{1,9},{5,13},{9,1},{13,5},{2,10},{6,14},... | collective-permute-start | bytes 49160 | tf_op jit(solution)/shard_map/ppermute | solution.py:416
  28.3 2.3 %collective-permute-start.9 = (f32[8,512]{1,0:T(8,128)S(1)}, f32[8,512]{1,0:T(8,128)S(1)}, u32[]{:S(2)}, u32[]{:S(2)}) collective-permute-start(f32[8,512]{1,0:T(8,128)S(1)} %shard_map.81.refs_0_.refs_4_), channel_id=1, source_target_pairs={{0,4},{4,0},{8,12},{12,8},{1,5},{5,1},{9,13},{13,9},{2,6},{6,2},{1... | collective-permute-start | bytes 49160 | tf_op jit(solution)/shard_map/ppermute | solution.py:416
  30.5 10.2 %copy-start = (s32[8192]{0:T(1024)S(1)}, s32[8192]{0:T(1024)}, u32[]{:S(2)}) copy-start(s32[8192]{0:T(1024)} %param.9) | copy-start | bytes 98308
  30.5 10.5 %copy-start.1 = (s32[8192]{0:T(1024)S(1)}, s32[8192]{0:T(1024)}, u32[]{:S(2)}) copy-start(s32[8192]{0:T(1024)} %param.8) | copy-start | bytes 98308
  31.0 5.7 %collective-permute-start.14 = (f32[8,512]{1,0:T(8,128)S(1)}, f32[8,512]{1,0:T(8,128)S(1)}, u32[]{:S(2)}, u32[]{:S(2)}) collective-permute-start(f32[8,512]{1,0:T(8,128)S(1)} %get-tuple-element.44.refs_4_.refs_0_), channel_id=1, source_target_pairs={{0,3},{1,2},{2,1},{3,0},{4,7},{5,6},{6,5},{7,4},{8,11},{9,10},{10,... | collective-permute-start | bytes 49160 | tf_op jit(solution)/shard_map/ppermute | solution.py:416
  33.5 4.7 %collective-permute-start.13 = (f32[8,512]{1,0:T(8,128)S(1)}, f32[8,512]{1,0:T(8,128)S(1)}, u32[]{:S(2)}, u32[]{:S(2)}) collective-permute-start(f32[8,512]{1,0:T(8,128)S(1)} %get-tuple-element.44.refs_4_.refs_0_), channel_id=1, source_target_pairs={{0,2},{1,3},{2,0},{3,1},{4,6},{5,7},{6,4},{7,5},{8,10},{9,11},{10,... | collective-permute-start | bytes 49160 | tf_op jit(solution)/shard_map/ppermute | solution.py:416
  34.4 3.9 %collective-permute-start.12 = (f32[8,512]{1,0:T(8,128)S(1)}, f32[8,512]{1,0:T(8,128)S(1)}, u32[]{:S(2)}, u32[]{:S(2)}) collective-permute-start(f32[8,512]{1,0:T(8,128)S(1)} %get-tuple-element.44.refs_4_.refs_0_), channel_id=1, source_target_pairs={{0,1},{1,0},{2,3},{3,2},{4,5},{5,4},{6,7},{7,6},{8,9},{9,8},{10,11... | collective-permute-start | bytes 49160 | tf_op jit(solution)/shard_map/ppermute | solution.py:416
  38.8 3.4 %collective-permute-start.17 = (f32[8,512]{1,0:T(8,128)S(1)}, f32[8,512]{1,0:T(8,128)S(1)}, u32[]{:S(2)}, u32[]{:S(2)}) collective-permute-start(f32[8,512]{1,0:T(8,128)S(1)} %shard_map.84.refs_0_), channel_id=1, source_target_pairs={{0,12},{4,8},{8,4},{12,0},{1,13},{5,9},{9,5},{13,1},{2,14},{6,10},... | collective-permute-start | bytes 49160 | tf_op jit(solution)/shard_map/ppermute | solution.py:416
  38.9 3.8 %collective-permute-start.16 = (f32[8,512]{1,0:T(8,128)S(1)}, f32[8,512]{1,0:T(8,128)S(1)}, u32[]{:S(2)}, u32[]{:S(2)}) collective-permute-start(f32[8,512]{1,0:T(8,128)S(1)} %shard_map.84.refs_0_), channel_id=1, source_target_pairs={{0,8},{4,12},{8,0},{12,4},{1,9},{5,13},{9,1},{13,5},{2,10},{6,14},... | collective-permute-start | bytes 49160 | tf_op jit(solution)/shard_map/ppermute | solution.py:416
  40.4 2.3 %collective-permute-start.15 = (f32[8,512]{1,0:T(8,128)S(1)}, f32[8,512]{1,0:T(8,128)S(1)}, u32[]{:S(2)}, u32[]{:S(2)}) collective-permute-start(f32[8,512]{1,0:T(8,128)S(1)} %shard_map.84.refs_0_), channel_id=1, source_target_pairs={{0,4},{4,0},{8,12},{12,8},{1,5},{5,1},{9,13},{13,9},{2,6},{6,2},{1... | collective-permute-start | bytes 49160 | tf_op jit(solution)/shard_map/ppermute | solution.py:416

commit v4 on v3

--- a/solution.py
+++ b/solution.py
@@ -20,7 +20,8 @@
 HERE = pl.BlockSpec(memory_space=pltpu.VMEM)
 SCALARS = pl.BlockSpec(memory_space=pltpu.SMEM)
 FAR = pl.BlockSpec(memory_space=pltpu.HBM)
-PACK = (ROWS, CLUSTER)
+VECTORS = (ROWS, CLUSTER)
+EVERY = range(BLOCKS)
 
 
 def near(shape, dtype=jnp.float32):
@@ -35,10 +36,38 @@
     return pltpu.with_memory_space_constraint(array, pltpu.HBM)
 
 
-def note_at(slots, number):
-    row = slots + number // BLOCKS
-    lane = number % BLOCKS * LANES
-    return slice(row, row + 1), slice(lane, lane + LANES)
+def fixed_slots(groups, n_user, n_item, slots):
+    return min(groups // n_user, groups // n_item, slots)
+
+
+def pack_shape(slots, fixed):
+    rows = slots * BLOCKS + slots - fixed + 1
+    return (rows + ROWS - 1) // ROWS * ROWS, LANES
+
+
+def note(slots, number):
+    row = slots * BLOCKS + number
+    return slice(row, row + 1)
+
+
+def part_of(block):
+    return slice(block * LANES, (block + 1) * LANES)
+
+
+def put(pack, slot, values):
+    for block in EVERY:
+        row = slot * BLOCKS + block
+        pack[row : row + 1, :] = values[:, part_of(block)]
+
+
+def get(pack, slot, blocks):
+    rows = (slot * BLOCKS + block for block in blocks)
+    return jnp.concatenate([pack[row : row + 1, :] for row in rows], axis=1)
+
+
+def clear_notes(pack, slots):
+    rows = pack.shape[0] - slots * BLOCKS
+    pack[slots * BLOCKS :, :] = jnp.zeros((rows, LANES), jnp.float32)
 
 
 def wide(block):
@@ -50,13 +79,13 @@
     return jnp.broadcast_to(total, (1, LANES))
 
 
-def write_notes(pack, tiles, which, counts):
+def write_notes(pack, tiles, fixed, which, counts):
     slots = tiles.shape[1]
-    pack[slots:, :] = jnp.zeros((ROWS - slots, CLUSTER), jnp.float32)
-    for slot in range(slots):
+    clear_notes(pack, slots)
+    for slot in range(fixed, slots):
         number = jnp.full((1, LANES), tiles[which, slot], jnp.int32)
-        pack[note_at(slots, slot)] = number.astype(jnp.float32)
-    pack[note_at(slots, slots)] = total_of(counts)
+        pack[note(slots, slot - fixed), :] = number.astype(jnp.float32)
+    pack[note(slots, slots - fixed), :] = total_of(counts)
 
 
 def staggered(slots, raise_top, add_mass):
@@ -95,7 +124,7 @@
         return pair
 
     n_user, n_item = devices
-    fixed = min(groups // n_user, groups // n_item, slots)
+    fixed = fixed_slots(groups, n_user, n_item, slots)
     row, column = lax.axis_index("user"), lax.axis_index("item")
     copies = [
         fetch(slot, [lax.rem(place * fixed + slot, groups) for place in (column, row)])
@@ -105,7 +134,7 @@
         copy.wait()
     for slot in range(fixed, slots):
         copies.append(fetch(slot, [tiles[which, slot] for which in range(2)]))
-    write_notes(pack, tiles, 0, item_count[...])
+    write_notes(pack, tiles, fixed, 0, item_count[...])
     early = max(1, 3 * fixed // 4)
 
     def raise_top(slot):
@@ -132,13 +161,13 @@
             terms = jnp.exp2(scores[slot, rows, :] - top)
             mass += jnp.sum(terms.reshape(LANES // 8, 8, CLUSTER), axis=0)
         log_mass = top + jnp.log2(jnp.sum(mass, axis=0, keepdims=True))
-        pack[slot : slot + 1, :] = jnp.where(filled[0, 0] > slot, log_mass, lowest)
+        put(pack, slot, jnp.where(filled[0, 0] > slot, log_mass, lowest))
 
     staggered(slots, raise_top, add_mass)
 
 
 def setup_kernel(
-    far_tiles, filled, users, items, far_users, far_items,
+    devices, far_tiles, filled, users, items, far_users, far_items,
     table, user_here, item_here, user_ids, item_ids, notes, active,
     tiles, user_count, item_count, sems,
 ):
@@ -172,7 +201,7 @@
         ((user_count, user_here, user_ids), (item_count, item_here, item_ids))
     ):
         numbers = jnp.full((ROWS, LANES), -1, jnp.int32)
-        here[...] = jnp.ones(PACK, jnp.float32)
+        here[...] = jnp.ones(VECTORS, jnp.float32)
         for slot in range(slots):
             group = tiles[which, slot]
             numbers = jnp.where(place == slot, group, numbers)
@@ -180,48 +209,59 @@
                 here[slot : slot + 1, block * LANES : (block + 1) * LANES] = counts[
                     pl.ds(group * BLOCKS + block, 1), :
                 ].astype(jnp.float32)
-        ids[...] = numbers.astype(jnp.float32)
-    notes[...] = jnp.zeros(PACK, jnp.float32)
-    write_notes(notes, tiles, 1, user_count[...])
-
-
-def matches(packs, ids, slots):
-    return [
-        [ids == pack[note_at(slots, slot)] for slot in range(slots)] for pack in packs
-    ]
-
-
-def log_merge(packs, chosen, slots, lanes, rows):
-    width = lanes.stop - lanes.start
-    spread = wide if width == CLUSTER else (lambda mask: mask)
+        ids[...] = numbers
+    fixed = fixed_slots(user_count.shape[0] // BLOCKS, *devices, slots)
+    write_notes(notes, tiles, fixed, 1, user_count[...])
+
+
+def matches(packs, owners, ids, slots, fixed, groups):
+    chosen = []
+    for pack, owner in zip(packs, owners):
+        masks = [ids == (owner * fixed + slot) % groups for slot in range(fixed)]
+        for number in range(slots - fixed):
+            masks.append(ids == pack[note(slots, number), :].astype(jnp.int32))
+        chosen.append(masks)
+    return chosen
+
+
+def across(mask, blocks):
+    return jnp.concatenate([mask] * len(blocks), axis=1)
+
+
+def log_merge(packs, chosen, slots, blocks, rows):
+    width = len(blocks) * LANES
     top = jnp.full((rows, width), lowest, jnp.float32)
     for pack, masks in zip(packs, chosen):
         for slot in range(slots):
-            part = jnp.where(spread(masks[slot]), pack[slot : slot + 1, lanes], lowest)
+            part = jnp.where(across(masks[slot], blocks), get(pack, slot, blocks), lowest)
             top = jnp.maximum(top, part)
     mass = jnp.zeros((rows, width), jnp.float32)
     for pack, masks in zip(packs, chosen):
         for slot in range(slots):
-            part = jnp.exp2(pack[slot : slot + 1, lanes] - top)
-            mass += jnp.where(spread(masks[slot]), part, 0.0)
+            part = jnp.exp2(get(pack, slot, blocks) - top)
+            mass += jnp.where(across(masks[slot], blocks), part, 0.0)
     return top + jnp.log2(jnp.where(mass > 0.0, mass, 1.0))
 
 
-def sum_merge(packs, chosen, slots, lanes, rows):
-    width = lanes.stop - lanes.start
-    spread = wide if width == CLUSTER else (lambda mask: mask)
-    total = jnp.zeros((rows, width), jnp.float32)
+def sum_merge(packs, chosen, slots, blocks, rows):
+    total = jnp.zeros((rows, len(blocks) * LANES), jnp.float32)
     for pack, masks in zip(packs, chosen):
         for slot in range(slots):
-            total += jnp.where(spread(masks[slot]), pack[slot : slot + 1, lanes], 0.0)
+            total += jnp.where(across(masks[slot], blocks), get(pack, slot, blocks), 0.0)
     return total
 
 
-def total_in(packs, slots):
-    total = packs[0][note_at(slots, slots)]
+def total_in(packs, slots, fixed):
+    row = note(slots, slots - fixed)
+    total = packs[0][row, :]
     for pack in packs[1:]:
-        total = total + pack[note_at(slots, slots)]
+        total = total + pack[row, :]
     return total
+
+
+def owners_of(axis, devices):
+    me = lax.axis_index(axis)
+    return [partner(me, step, devices) for step in range(devices)]
 
 
 def store_masks(masks, chosen):
@@ -240,19 +280,16 @@
     return jnp.broadcast_to(row, (LANES, LANES)).T
 
 
-EVERY = slice(0, CLUSTER)
-
-
-def second_kernel(devices, *refs):
+def second_kernel(axis, devices, fixed, groups, *refs):
     packs = refs[:devices]
     table, ids, counts, notes, active, pack, terms, tops, masks, totals, potential = refs[devices:]
     slots = table.shape[0]
-    chosen = matches(packs, ids[...], slots)
+    chosen = matches(packs, owners_of(axis, devices), ids[...], slots, fixed, groups)
     store_masks(masks, chosen)
-    totals[...] = jnp.broadcast_to(total_in(packs, slots), totals.shape)
+    totals[...] = jnp.broadcast_to(total_in(packs, slots, fixed), totals.shape)
     potential[...] = jnp.log2(counts[...]) - log_merge(packs, chosen, slots, EVERY, ROWS)
     pack[...] = notes[...]
-    tops[...] = jnp.full(PACK, lowest, jnp.float32)
+    tops[...] = jnp.full(VECTORS, lowest, jnp.float32)
 
     def raise_top(slot):
         top = jnp.full((8, CLUSTER), lowest, jnp.float32)
@@ -272,7 +309,7 @@
             mass += jnp.sum(part.reshape(LANES // 8, 8, CLUSTER), axis=0)
         log_mass = top + jnp.log2(jnp.sum(mass, axis=0, keepdims=True))
         on = active[slot : slot + 1, :] > 0.0
-        pack[slot : slot + 1, :] = jnp.where(on, log_mass, lowest)
+        put(pack, slot, jnp.where(on, log_mass, lowest))
         tops[slot : slot + 1, :] = jnp.where(on, top, lowest)
 
     staggered(slots, raise_top, add_mass)
@@ -280,7 +317,7 @@
 
 def row_sums(terms, factor, pack):
     slots = terms.shape[0]
-    pack[...] = jnp.zeros(PACK, jnp.float32)
+    clear_notes(pack, slots)
     for slot in range(slots):
         for block in range(BLOCKS):
             rows = slice(block * LANES, (block + 1) * LANES)
@@ -288,28 +325,29 @@
             for other in range(1, BLOCKS):
                 lanes = slice(other * LANES, (other + 1) * LANES)
                 part += terms[slot, rows, lanes] * factor[slot : slot + 1, lanes]
-            pack[slot : slot + 1, rows] = jnp.sum(part.T, axis=0, keepdims=True)
+            row = slot * BLOCKS + block
+            pack[row : row + 1, :] = jnp.sum(part.T, axis=0, keepdims=True)
 
 
 def column_sums(terms, factor, scale, pack):
     slots = terms.shape[0]
-    pack[...] = jnp.zeros(PACK, jnp.float32)
+    clear_notes(pack, slots)
     for slot in range(slots):
         mass = jnp.zeros((8, CLUSTER), jnp.float32)
         for block in range(BLOCKS):
             rows = slice(block * LANES, (block + 1) * LANES)
             part = terms[slot, rows, :] * wide(down_rows(factor, slot, block))
             mass += jnp.sum(part.reshape(LANES // 8, 8, CLUSTER), axis=0)
-        pack[slot : slot + 1, :] = jnp.sum(mass, axis=0, keepdims=True) * scale[slot : slot + 1, :]
-
-
-def third_kernel(devices, *refs):
+        put(pack, slot, jnp.sum(mass, axis=0, keepdims=True) * scale[slot : slot + 1, :])
+
+
+def third_kernel(axis, devices, fixed, groups, *refs):
     packs = refs[:devices]
     terms, tops, ids, counts, item_total, pack, factor, masks, totals = refs[devices:]
     slots = terms.shape[0]
-    chosen = matches(packs, ids[...], slots)
+    chosen = matches(packs, owners_of(axis, devices), ids[...], slots, fixed, groups)
     store_masks(masks, chosen)
-    totals[...] = jnp.broadcast_to(total_in(packs, slots), totals.shape)
+    totals[...] = jnp.broadcast_to(total_in(packs, slots, fixed), totals.shape)
     log_share = jnp.log2(counts[...] / wide(item_total[...]))
     merged = log_merge(packs, chosen, slots, EVERY, ROWS)
     factor[...] = jnp.exp2(tops[...] + (log_share - merged))
@@ -342,27 +380,26 @@
     return [ordered.at[device] for device in range(devices)]
 
 
-def cluster_matches(packs, slots, groups):
-    numbers = lax.broadcasted_iota(jnp.int32, (groups, LANES), 0).astype(jnp.float32)
-    return matches(packs, numbers, slots)
-
-
-def user_out_kernel(axis, devices, slots, *refs):
+def cluster_matches(packs, slots, fixed, groups):
+    numbers = lax.broadcasted_iota(jnp.int32, (groups, LANES), 0)
+    return matches(packs, range(len(packs)), numbers, slots, fixed, groups)
+
+
+def user_out_kernel(axis, devices, slots, fixed, *refs):
     counts, totals, out, first_packs, last_packs = refs[2 * devices :]
     first = in_order(axis, devices, refs[:devices], first_packs)
     last = in_order(axis, devices, refs[devices : 2 * devices], last_packs)
     groups = counts.shape[0] // BLOCKS
-    chosen = cluster_matches(first, slots, groups)
+    chosen = cluster_matches(first, slots, fixed, groups)
     for block in range(BLOCKS):
-        lanes = slice(block * LANES, (block + 1) * LANES)
         here = pl.ds(block, groups, stride=BLOCKS)
         share = jnp.log2(counts[here, :].astype(jnp.float32) / totals[0:1, :])
-        merged = log_merge(first, chosen, slots, lanes, groups)
-        sums = sum_merge(last, chosen, slots, lanes, groups)
+        merged = log_merge(first, chosen, slots, [block], groups)
+        sums = sum_merge(last, chosen, slots, [block], groups)
         out[here, :] = BACK * (2.0 * share - merged - jnp.log2(sums))
 
 
-def item_base_kernel(axis, devices, slots, middles, *refs):
+def item_base_kernel(axis, devices, slots, fixed, middles, *refs):
     given = (1 + middles) * devices
     counts, item_total, user_total, out, numbers, all_packs = refs[given:]
     packs = [
@@ -370,17 +407,16 @@
         for step in range(1 + middles)
     ]
     groups = counts.shape[0] // BLOCKS
-    chosen = cluster_matches(packs[0], slots, groups)
+    chosen = cluster_matches(packs[0], slots, fixed, groups)
     for index, mask in enumerate(mask for group in chosen for mask in group):
         numbers[index] = jnp.where(mask, 1.0, 0.0)
     for block in range(BLOCKS):
-        lanes = slice(block * LANES, (block + 1) * LANES)
         here = pl.ds(block, groups, stride=BLOCKS)
         share = jnp.log2(counts[here, :].astype(jnp.float32) / item_total[0:1, :])
         base = (2 + middles) * share + jnp.log2(user_total[0:1, :])
-        base = base - log_merge(packs[0], chosen, slots, lanes, groups)
+        base = base - log_merge(packs[0], chosen, slots, [block], groups)
         for step in range(middles):
-            base = base - jnp.log2(sum_merge(packs[1 + step], chosen, slots, lanes, groups))
+            base = base - jnp.log2(sum_merge(packs[1 + step], chosen, slots, [block], groups))
         out[here, :] = base
 
 
@@ -390,9 +426,8 @@
     groups = base.shape[0] // BLOCKS
     chosen = load_masks(numbers, devices, slots)
     for block in range(BLOCKS):
-        lanes = slice(block * LANES, (block + 1) * LANES)
         here = pl.ds(block, groups, stride=BLOCKS)
-        sums = sum_merge(packs, chosen, slots, lanes, groups)
+        sums = sum_merge(packs, chosen, slots, [block], groups)
         out[here, :] = BACK * (base[here, :] - jnp.log2(sums))
 
 
@@ -437,8 +472,13 @@
     def body(user_emb, item_emb, user_count, item_count, tiles, tile_count):
         slots = tiles.shape[2]
         tall = (slots, CLUSTER, CLUSTER)
-        vectors = near(PACK)
+        groups = user_emb.shape[0] // CLUSTER
+        fixed = fixed_slots(groups, n_user, n_item, slots)
+        shape = pack_shape(slots, fixed)
+        packed = near(shape)
+        vectors = near(VECTORS)
         splat = near((ROWS, LANES))
+        numbers = near((ROWS, LANES), jnp.int32)
         user_counts = user_count.reshape(-1, LANES)
         item_counts = item_count.reshape(-1, LANES)
         gathered = near((slots, CLUSTER, user_emb.shape[1]), user_emb.dtype)
@@ -447,7 +487,7 @@
         far_tiles = jnp.transpose(tiles, (0, 1, 3, 2)).reshape(2, slots)
         pack, users, items = call(
             bind(first_kernel, (n_user, n_item)),
-            [vectors, gathered, gathered],
+            [packed, gathered, gathered],
             (
                 away(far_tiles), tile_count, away(user_emb), away(item_emb), away(item_counts),
             ),
@@ -462,8 +502,8 @@
         )
         first_packs = exchange(pack, "item", n_item)
         table, user_here, item_here, user_ids, item_ids, notes, active = call(
-            setup_kernel,
-            [near(tall), vectors, vectors, splat, splat, vectors, vectors],
+            bind(setup_kernel, (n_user, n_item)),
+            [near(tall), vectors, vectors, numbers, numbers, packed, vectors],
             (
                 away(far_tiles), tile_count, keep(users), keep(items),
                 away(user_counts), away(item_counts),
@@ -477,16 +517,16 @@
             ],
         )
         pack, terms, tops, user_masks, item_total = call(
-            bind(second_kernel, n_item),
-            [vectors, near(tall), vectors, near((n_item * slots, ROWS, LANES)), splat],
+            bind(second_kernel, "item", n_item, fixed, groups),
+            [packed, near(tall), vectors, near((n_item * slots, ROWS, LANES)), splat],
             (*first_packs, keep(table), user_ids, user_here, notes, active),
-            scratch=[near(PACK)],
+            scratch=[near(VECTORS)],
         )
         terms = keep(terms)
         second_packs = exchange(pack, "user", n_user)
         pack, factor, item_masks, user_total = call(
-            bind(third_kernel, n_user),
-            [vectors, vectors, near((n_user * slots, ROWS, LANES)), splat],
+            bind(third_kernel, "user", n_user, fixed, groups),
+            [packed, vectors, near((n_user * slots, ROWS, LANES)), splat],
             (*second_packs, terms, tops, item_ids, item_here, item_total),
         )
         item_packs = [second_packs]
@@ -494,36 +534,35 @@
             user_packs = exchange(pack, "item", n_item)
             (pack,) = call(
                 bind(user_kernel, n_item),
-                [vectors],
+                [packed],
                 (*user_packs, terms, user_masks, user_here, user_total, factor),
-                scratch=[near(PACK)],
+                scratch=[near(VECTORS)],
             )
             item_packs.append(exchange(pack, "user", n_user))
             if iteration < ITERS - 1:
                 pack, factor = call(
                     bind(item_kernel, n_user),
-                    [vectors, vectors],
+                    [packed, vectors],
                     (*item_packs[-1], terms, item_masks, item_here, item_total, factor),
                 )
         user_values = call(
-            bind(user_out_kernel, "item", n_item, slots),
+            bind(user_out_kernel, "item", n_item, slots, fixed),
             jax.ShapeDtypeStruct(user_counts.shape, jnp.float32),
             (*first_packs, *user_packs, user_counts, user_total),
-            scratch=[near((n_item, *PACK)), near((n_item, *PACK))],
+            scratch=[near((n_item, *shape)), near((n_item, *shape))],
         )
         middles = ITERS - 2
-        groups = item_counts.shape[0] // BLOCKS
-        base, numbers = call(
-            bind(item_base_kernel, "user", n_user, slots, middles),
+        base, named = call(
+            bind(item_base_kernel, "user", n_user, slots, fixed, middles),
             [near(item_counts.shape), near((n_user * slots, groups, LANES))],
             (*(pack for packs in item_packs[:-1] for pack in packs), item_counts, item_total, user_total),
-            scratch=[near((1 + middles, n_user, *PACK))],
+            scratch=[near((1 + middles, n_user, *shape))],
         )
         item_values = call(
             bind(item_out_kernel, "user", n_user, slots),
             jax.ShapeDtypeStruct(item_counts.shape, jnp.float32),
-            (*item_packs[-1], base, numbers),
-            scratch=[near((n_user, *PACK))],
+            (*item_packs[-1], base, named),
+            scratch=[near((n_user, *shape))],
         )
         return user_values.reshape(-1), item_values.reshape(-1)
 

time: 43.7 us -> 43.3 us (level)
  no operation moved by 1% of the time
where the time goes in v4:
time: 43.3 us; the launch traced here: 43.1 us
  starting transfers between devices  20.4 us (47%)
  waiting for transfers between devices  11.7 us (27%)
  Pallas kernels  9.58 us (22%)
  between operations  1.37 us (3%)
    ppermute x18, starting transfers between devices, exchange(): packs.append(keep(lax.ppermute(pack, axis, route)))  20.4 us
    ppermute x18, waiting for transfers between devices, exchange(): packs.append(keep(lax.ppermute(pack, axis, route)))  11.7 us
    pallas_call x10, Pallas kernels, call(): pl.pallas_call(kernel, out_shape=outs, in_specs=specs or [HERE] * len(ope...  9.58 us
  transfers between devices with their start and end apart: 18, of which 13 were waited for; matrix products, arithmetic and copies ran while one was open for 0% of the time, Pallas kernels for 6%

profile of v4, /device:TPU:0, one launch (start us, length us, event | category | flops | bytes accessed | tf_op | source)
XLA Modules:
  0.0 43.1 jit_solution(17259439646976066618)
XLA Ops:
  1.3 3.1 %shard_map.77 = (f32[24,128]{1,0:T(8,128)S(1)}, bf16[5,512,128]{2,1,0:T(8,128)(2,1)S(1)}, bf16[5,512,128]{2,1,0:T(8,128)(2,1)S(1)}) custom-call(s32[2,5]{1,0:T(2,128)} %bitcast.14, s32[1,1]{1,0:T(1,128)S(6)} %copy.8.refs_1_, bf16[8192,128]{1,0:T(8,128)(2,1)} %refs_2_.1, bf16[8192,128]{1,0:T(8,128)(2,1)} %refs_3_.1, s32[64,128]{1,0:T(8,128)} %bitcast.7), custom_call_target="tpu_custom_call" | custom-call | tf_op jit(solution)/shard_map/pallas_call | solution.py:456
  4.4 5.1 %collective-permute-start.2 = (f32[24,128]{1,0:T(8,128)S(1)}, f32[24,128]{1,0:T(8,128)S(1)}, u32[]{:S(2)}, u32[]{:S(2)}) collective-permute-start(f32[24,128]{1,0:T(8,128)S(1)} %get-tuple-element.25.refs_0_), channel_id=1, source_target_pairs={{0,3},{1,2},{2,1},{3,0},{4,7},{5,6},{6,5},{7,4},{8,11},{9,10},{10,... | collective-permute-start | bytes 36872 | tf_op jit(solution)/shard_map/ppermute | solution.py:451
  9.5 0.0 collective-permute-start.1
  9.5 0.6 %collective-permute-start = (f32[24,128]{1,0:T(8,128)S(1)}, f32[24,128]{1,0:T(8,128)S(1)}, u32[]{:S(2)}, u32[]{:S(2)}) collective-permute-start(f32[24,128]{1,0:T(8,128)S(1)} %get-tuple-element.25.refs_0_), channel_id=1, source_target_pairs={{0,1},{1,0},{2,3},{3,2},{4,5},{5,4},{6,7},{7,6},{8,9},{9,8},{10,11... | collective-permute-start | bytes 36872 | tf_op jit(solution)/shard_map/ppermute | solution.py:451
  10.1 1.6 %shard_map.78 = (f32[5,512,512]{2,1,0:T(8,128)S(1)}, f32[8,512]{1,0:T(8,128)S(1)}, f32[8,512]{1,0:T(8,128)S(1)}, s32[8,128]{1,0:T(8,128)S(1)}, s32[8,128]{1,0:T(...) custom-call(s32[2,5]{1,0:T(2,128)} %bitcast.15, s32[1,1]{1,0:T(1,128)S(6)} %copy.8.refs_1_, ...), custom_call_target="tpu_custom_call" | custom-call | tf_op jit(solution)/shard_map/pallas_call | solution.py:456
  11.7 0.0 collective-permute-done.2.refs_3_
  11.7 2.3 %collective-permute-done.1.refs_2_ = f32[24,128]{1,0:T(8,128)S(1)} collective-permute-done((f32[24,128]{1,0:T(8,128)S(1)}, f32[24,128]{1,0:T(8,128)S(1)}, u32[]{:S(2)}, u32[]{:S(2)}) %collective-permute-start.1) | collective-permute-done | bytes 12320 | tf_op jit(solution)/shard_map/ppermute | solution.py:451
  14.1 0.0 collective-permute-done.refs_1_
  14.1 1.3 %shard_map.79 = (f32[24,128]{1,0:T(8,128)S(1)}, f32[5,512,512]{2,1,0:T(8,128)S(1)}, f32[8,512]{1,0:T(8,128)S(1)}, f32[20,8,128]{2,1,0:T(8,128)S(1)}, f32[8,128]{1,0:T(8,128)S(1)}) custom-call(f32[24,128]{1,0:T(8,128)S(1)} %get-tuple-element.25.refs_0_, f32[24,128]{1,0:T(8,128)S(1)} %collective-permute-done.refs_1_, ...), custom_call_target="tpu_custom_call" | custom-call | tf_op jit(solution)/shard_map/pallas_call | solution.py:456
  15.3 0.1 collective-permute-start.5
  15.4 1.6 %collective-permute-start.4 = (f32[24,128]{1,0:T(8,128)S(1)}, f32[24,128]{1,0:T(8,128)S(1)}, u32[]{:S(2)}, u32[]{:S(2)}) collective-permute-start(f32[24,128]{1,0:T(8,128)S(1)} %get-tuple-element.33.refs_0_), channel_id=1, source_target_pairs={{0,8},{4,12},{8,0},{12,4},{1,9},{5,13},{9,1},{13,5},{2,10},{6,14},... | collective-permute-start | bytes 36872 | tf_op jit(solution)/shard_map/ppermute | solution.py:451
  17.0 0.3 collective-permute-start.3
  17.3 1.3 %collective-permute-done.5.refs_3_ = f32[24,128]{1,0:T(8,128)S(1)} collective-permute-done((f32[24,128]{1,0:T(8,128)S(1)}, f32[24,128]{1,0:T(8,128)S(1)}, u32[]{:S(2)}, u32[]{:S(2)}) %collective-permute-start.5) | collective-permute-done | bytes 12320 | tf_op jit(solution)/shard_map/ppermute | solution.py:451
  18.6 0.6 %collective-permute-done.4.refs_2_ = f32[24,128]{1,0:T(8,128)S(1)} collective-permute-done((f32[24,128]{1,0:T(8,128)S(1)}, f32[24,128]{1,0:T(8,128)S(1)}, u32[]{:S(2)}, u32[]{:S(2)}) %collective-permute-start.4) | collective-permute-done | bytes 12320 | tf_op jit(solution)/shard_map/ppermute | solution.py:451
  19.2 0.0 collective-permute-done.3.refs_1_
  19.2 0.6 %shard_map.80 = (f32[24,128]{1,0:T(8,128)S(1)}, f32[8,512]{1,0:T(8,128)S(1)}, f32[20,8,128]{2,1,0:T(8,128)S(1)}, f32[8,128]{1,0:T(8,128)S(1)}) custom-call(f32[24,128]{1,0:T(8,128)S(1)} %get-tuple-element.33.refs_0_, f32[24,128]{1,0:T(8,128)S(1)} %collective-permute-done.3.refs_1_, f32[24,128]{1,0:T(8,128)S(1)} %collective-permute-done.4.refs_2_, ...), custom_call_target="tpu_custom_call" | custom-call | tf_op jit(solution)/shard_map/pallas_call | solution.py:456
  19.7 1.5 %collective-permute-start.8 = (f32[24,128]{1,0:T(8,128)S(1)}, f32[24,128]{1,0:T(8,128)S(1)}, u32[]{:S(2)}, u32[]{:S(2)}) collective-permute-start(f32[24,128]{1,0:T(8,128)S(1)} %get-tuple-element.39.refs_0_), channel_id=1, source_target_pairs={{0,3},{1,2},{2,1},{3,0},{4,7},{5,6},{6,5},{7,4},{8,11},{9,10},{10,... | collective-permute-start | bytes 36872 | tf_op jit(solution)/shard_map/ppermute | solution.py:451
  21.3 0.6 %collective-permute-start.7 = (f32[24,128]{1,0:T(8,128)S(1)}, f32[24,128]{1,0:T(8,128)S(1)}, u32[]{:S(2)}, u32[]{:S(2)}) collective-permute-start(f32[24,128]{1,0:T(8,128)S(1)} %get-tuple-element.39.refs_0_), channel_id=1, source_target_pairs={{0,2},{1,3},{2,0},{3,1},{4,6},{5,7},{6,4},{7,5},{8,10},{9,11},{10,... | collective-permute-start | bytes 36872 | tf_op jit(solution)/shard_map/ppermute | solution.py:451
  21.9 2.3 %collective-permute-start.6 = (f32[24,128]{1,0:T(8,128)S(1)}, f32[24,128]{1,0:T(8,128)S(1)}, u32[]{:S(2)}, u32[]{:S(2)}) collective-permute-start(f32[24,128]{1,0:T(8,128)S(1)} %get-tuple-element.39.refs_0_), channel_id=1, source_target_pairs={{0,1},{1,0},{2,3},{3,2},{4,5},{5,4},{6,7},{7,6},{8,9},{9,8},{10,11... | collective-permute-start | bytes 36872 | tf_op jit(solution)/shard_map/ppermute | solution.py:451
  24.2 1.1 %collective-permute-done.8.refs_3_ = f32[24,128]{1,0:T(8,128)S(1)} collective-permute-done((f32[24,128]{1,0:T(8,128)S(1)}, f32[24,128]{1,0:T(8,128)S(1)}, u32[]{:S(2)}, u32[]{:S(2)}) %collective-permute-start.8) | collective-permute-done | bytes 12320 | tf_op jit(solution)/shard_map/ppermute | solution.py:451
  25.3 0.6 %collective-permute-done.7.refs_2_ = f32[24,128]{1,0:T(8,128)S(1)} collective-permute-done((f32[24,128]{1,0:T(8,128)S(1)}, f32[24,128]{1,0:T(8,128)S(1)}, u32[]{:S(2)}, u32[]{:S(2)}) %collective-permute-start.7) | collective-permute-done | bytes 12320 | tf_op jit(solution)/shard_map/ppermute | solution.py:451
  25.9 0.1 collective-permute-done.6.refs_1_
  26.0 0.5 %shard_map.81.refs_0_.refs_4_ = f32[24,128]{1,0:T(8,128)S(1)} custom-call(f32[24,128]{1,0:T(8,128)S(1)} %get-tuple-element.39.refs_0_, f32[24,128]{1,0:T(8,128)S(1)} %collective-permute-done.6.refs_1_, f32[24,128]{1,0:T(8,128)S(1)} %collective-permute-done.7.refs_2_, f32[24,128]{1,0:T(8,128)S(1)} %collective-permute-done.8.refs_3_, ...), custom_call_target="tpu_custom_call" | custom-call | tf_op jit(solution)/shard_map/pallas_call | solution.py:456
  26.5 0.1 collective-permute-start.11
  26.6 1.5 %collective-permute-start.10 = (f32[24,128]{1,0:T(8,128)S(1)}, f32[24,128]{1,0:T(8,128)S(1)}, u32[]{:S(2)}, u32[]{:S(2)}) collective-permute-start(f32[24,128]{1,0:T(8,128)S(1)} %shard_map.81.refs_0_.refs_4_), channel_id=1, source_target_pairs={{0,8},{4,12},{8,0},{12,4},{1,9},{5,13},{9,1},{13,5},{2,10},{6,14},... | collective-permute-start | bytes 36872 | tf_op jit(solution)/shard_map/ppermute | solution.py:451
  28.1 0.3 collective-permute-start.9
  28.4 1.4 %collective-permute-done.11.refs_3_.refs_7_ = f32[24,128]{1,0:T(8,128)S(1)} collective-permute-done((f32[24,128]{1,0:T(8,128)S(1)}, f32[24,128]{1,0:T(8,128)S(1)}, u32[]{:S(2)}, u32[]{:S(2)}) %collective-permute-start.11) | collective-permute-done | bytes 12320 | tf_op jit(solution)/shard_map/ppermute | solution.py:451
  29.8 0.5 %collective-permute-done.10.refs_2_.refs_6_ = f32[24,128]{1,0:T(8,128)S(1)} collective-permute-done((f32[24,128]{1,0:T(8,128)S(1)}, f32[24,128]{1,0:T(8,128)S(1)}, u32[]{:S(2)}, u32[]{:S(2)}) %collective-permute-start.10) | collective-permute-done | bytes 12320 | tf_op jit(solution)/shard_map/ppermute | solution.py:451
  30.3 0.0 collective-permute-done.9.refs_1_.refs_5_
  30.3 0.5 %shard_map.82 = (f32[24,128]{1,0:T(8,128)S(1)}, f32[8,512]{1,0:T(8,128)S(1)}) custom-call(f32[24,128]{1,0:T(8,128)S(1)} %shard_map.81.refs_0_.refs_4_, f32[24,128]{1,0:T(8,128)S(1)} %collective-permute-done.9.refs_1_.refs_5_, f32[24,128]{1,0:T(8,128)S(1)} %collective-permute-done.10.refs_2_.refs_6_, f32[24,128]{1,0:T(8,128)S(1)} %collective-permute-done.11.refs_3_.refs_7_, ...), custom_call_target="tpu_custom_call" | custom-call | tf_op jit(solution)/shard_map/pallas_call | solution.py:456
  30.8 2.5 %collective-permute-start.14 = (f32[24,128]{1,0:T(8,128)S(1)}, f32[24,128]{1,0:T(8,128)S(1)}, u32[]{:S(2)}, u32[]{:S(2)}) collective-permute-start(f32[24,128]{1,0:T(8,128)S(1)} %get-tuple-element.44.refs_4_.refs_0_), channel_id=1, source_target_pairs={{0,3},{1,2},{2,1},{3,0},{4,7},{5,6},{6,5},{7,4},{8,11},{9,10},{10,... | collective-permute-start | bytes 36872 | tf_op jit(solution)/shard_map/ppermute | solution.py:451
  33.3 0.9 %collective-permute-start.13 = (f32[24,128]{1,0:T(8,128)S(1)}, f32[24,128]{1,0:T(8,128)S(1)}, u32[]{:S(2)}, u32[]{:S(2)}) collective-permute-start(f32[24,128]{1,0:T(8,128)S(1)} %get-tuple-element.44.refs_4_.refs_0_), channel_id=1, source_target_pairs={{0,2},{1,3},{2,0},{3,1},{4,6},{5,7},{6,4},{7,5},{8,10},{9,11},{10,... | collective-permute-start | bytes 36872 | tf_op jit(solution)/shard_map/ppermute | solution.py:451
  34.3 1.0 %collective-permute-start.12 = (f32[24,128]{1,0:T(8,128)S(1)}, f32[24,128]{1,0:T(8,128)S(1)}, u32[]{:S(2)}, u32[]{:S(2)}) collective-permute-start(f32[24,128]{1,0:T(8,128)S(1)} %get-tuple-element.44.refs_4_.refs_0_), channel_id=1, source_target_pairs={{0,1},{1,0},{2,3},{3,2},{4,5},{5,4},{6,7},{7,6},{8,9},{9,8},{10,11... | collective-permute-start | bytes 36872 | tf_op jit(solution)/shard_map/ppermute | solution.py:451
  35.3 1.1 %collective-permute-done.14.refs_7_.refs_3_ = f32[24,128]{1,0:T(8,128)S(1)} collective-permute-done((f32[24,128]{1,0:T(8,128)S(1)}, f32[24,128]{1,0:T(8,128)S(1)}, u32[]{:S(2)}, u32[]{:S(2)}) %collective-permute-start.14) | collective-permute-done | bytes 12320 | tf_op jit(solution)/shard_map/ppermute | solution.py:451
  36.4 1.5 %collective-permute-done.13.refs_6_.refs_2_ = f32[24,128]{1,0:T(8,128)S(1)} collective-permute-done((f32[24,128]{1,0:T(8,128)S(1)}, f32[24,128]{1,0:T(8,128)S(1)}, u32[]{:S(2)}, u32[]{:S(2)}) %collective-permute-start.13) | collective-permute-done | bytes 12320 | tf_op jit(solution)/shard_map/ppermute | solution.py:451
  38.0 0.1 collective-permute-done.12.refs_5_.refs_1_
  38.1 0.5 %shard_map.84.refs_0_ = f32[24,128]{1,0:T(8,128)S(1)} custom-call(f32[24,128]{1,0:T(8,128)S(1)} %get-tuple-element.44.refs_4_.refs_0_, f32[24,128]{1,0:T(8,128)S(1)} %collective-permute-done.12.refs_5_.refs_1_, f32[24,128]{1,0:T(8,128)S(1)} %collective-permute-done.13.refs_6_.refs_2_, f32[24,128]{1,0:T(8,128)S(1)} %collective-permute-done.14.refs_7_.refs_3_, ...), custom_call_target="tpu_custom_call" | custom-call | tf_op jit(solution)/shard_map/pallas_call | solution.py:456
  38.6 0.1 collective-permute-start.17
  38.6 1.5 %collective-permute-start.16 = (f32[24,128]{1,0:T(8,128)S(1)}, f32[24,128]{1,0:T(8,128)S(1)}, u32[]{:S(2)}, u32[]{:S(2)}) collective-permute-start(f32[24,128]{1,0:T(8,128)S(1)} %shard_map.84.refs_0_), channel_id=1, source_target_pairs={{0,8},{4,12},{8,0},{12,4},{1,9},{5,13},{9,1},{13,5},{2,10},{6,14},... | collective-permute-start | bytes 36872 | tf_op jit(solution)/shard_map/ppermute | solution.py:451
  40.2 0.3 collective-permute-start.15
  40.5 0.0 copy-done
  40.5 0.2 shard_map.85
  40.7 0.0 copy-done.1
  40.7 0.8 %shard_map.83 = f32[64,128]{1,0:T(8,128)} custom-call(f32[24,128]{1,0:T(8,128)S(1)} %get-tuple-element.25.refs_0_, f32[24,128]{1,0:T(8,128)S(1)} %collective-permute-done.refs_1_, f32[24,128]{1,0:T(8,128)S(1)} %collective-permute-done.1.refs_2_, f32[24,128]{1,0:T(8,128)S(1)} %collective-permute-done.2.refs_3_, ...), custom_call_target="tpu_custom_call" | custom-call | tf_op jit(solution)/shard_map/pallas_call | solution.py:456
  41.5 0.4 collective-permute-done.17.refs_3_
  41.9 0.5 %collective-permute-done.16.refs_2_ = f32[24,128]{1,0:T(8,128)S(1)} collective-permute-done((f32[24,128]{1,0:T(8,128)S(1)}, f32[24,128]{1,0:T(8,128)S(1)}, u32[]{:S(2)}, u32[]{:S(2)}) %collective-permute-start.16) | collective-permute-done | bytes 12320 | tf_op jit(solution)/shard_map/ppermute | solution.py:451
  42.4 0.0 collective-permute-done.15.refs_1_
  42.4 0.7 %shard_map.86 = f32[64,128]{1,0:T(8,128)} custom-call(f32[24,128]{1,0:T(8,128)S(1)} %shard_map.84.refs_0_, f32[24,128]{1,0:T(8,128)S(1)} %collective-permute-done.15.refs_1_, f32[24,128]{1,0:T(8,128)S(1)} %collective-permute-done.16.refs_2_, f32[24,128]{1,0:T(8,128)S(1)} %collective-permute-done.17.refs_3_, f32[64,128]{1,0:T(8,128)S(1)} %get-tuple-element.46.refs_4_, ...), custom_call_target="tpu_custom_call" | custom-call | tf_op jit(solution)/shard_map/pallas_call | solution.py:456
  (2 shorter events, 0.0 us)
Async XLA Ops:
  4.4 7.4 %collective-permute-start.2 = (f32[24,128]{1,0:T(8,128)S(1)}, f32[24,128]{1,0:T(8,128)S(1)}, u32[]{:S(2)}, u32[]{:S(2)}) collective-permute-start(f32[24,128]{1,0:T(8,128)S(1)} %get-tuple-element.25.refs_0_), channel_id=1, source_target_pairs={{0,3},{1,2},{2,1},{3,0},{4,7},{5,6},{6,5},{7,4},{8,11},{9,10},{10,... | collective-permute-start | bytes 36872 | tf_op jit(solution)/shard_map/ppermute | solution.py:451
  9.5 4.6 %collective-permute-start.1 = (f32[24,128]{1,0:T(8,128)S(1)}, f32[24,128]{1,0:T(8,128)S(1)}, u32[]{:S(2)}, u32[]{:S(2)}) collective-permute-start(f32[24,128]{1,0:T(8,128)S(1)} %get-tuple-element.25.refs_0_), channel_id=1, source_target_pairs={{0,2},{1,3},{2,0},{3,1},{4,6},{5,7},{6,4},{7,5},{8,10},{9,11},{10,... | collective-permute-start | bytes 36872 | tf_op jit(solution)/shard_map/ppermute | solution.py:451
  9.5 4.6 %collective-permute-start = (f32[24,128]{1,0:T(8,128)S(1)}, f32[24,128]{1,0:T(8,128)S(1)}, u32[]{:S(2)}, u32[]{:S(2)}) collective-permute-start(f32[24,128]{1,0:T(8,128)S(1)} %get-tuple-element.25.refs_0_), channel_id=1, source_target_pairs={{0,1},{1,0},{2,3},{3,2},{4,5},{5,4},{6,7},{7,6},{8,9},{9,8},{10,11... | collective-permute-start | bytes 36872 | tf_op jit(solution)/shard_map/ppermute | solution.py:451
  15.3 3.3 %collective-permute-start.5 = (f32[24,128]{1,0:T(8,128)S(1)}, f32[24,128]{1,0:T(8,128)S(1)}, u32[]{:S(2)}, u32[]{:S(2)}) collective-permute-start(f32[24,128]{1,0:T(8,128)S(1)} %get-tuple-element.33.refs_0_), channel_id=1, source_target_pairs={{0,12},{4,8},{8,4},{12,0},{1,13},{5,9},{9,5},{13,1},{2,14},{6,10},... | collective-permute-start | bytes 36872 | tf_op jit(solution)/shard_map/ppermute | solution.py:451
  15.4 3.8 %collective-permute-start.4 = (f32[24,128]{1,0:T(8,128)S(1)}, f32[24,128]{1,0:T(8,128)S(1)}, u32[]{:S(2)}, u32[]{:S(2)}) collective-permute-start(f32[24,128]{1,0:T(8,128)S(1)} %get-tuple-element.33.refs_0_), channel_id=1, source_target_pairs={{0,8},{4,12},{8,0},{12,4},{1,9},{5,13},{9,1},{13,5},{2,10},{6,14},... | collective-permute-start | bytes 36872 | tf_op jit(solution)/shard_map/ppermute | solution.py:451
  17.0 2.2 %collective-permute-start.3 = (f32[24,128]{1,0:T(8,128)S(1)}, f32[24,128]{1,0:T(8,128)S(1)}, u32[]{:S(2)}, u32[]{:S(2)}) collective-permute-start(f32[24,128]{1,0:T(8,128)S(1)} %get-tuple-element.33.refs_0_), channel_id=1, source_target_pairs={{0,4},{4,0},{8,12},{12,8},{1,5},{5,1},{9,13},{13,9},{2,6},{6,2},{1... | collective-permute-start | bytes 36872 | tf_op jit(solution)/shard_map/ppermute | solution.py:451
  19.7 5.6 %collective-permute-start.8 = (f32[24,128]{1,0:T(8,128)S(1)}, f32[24,128]{1,0:T(8,128)S(1)}, u32[]{:S(2)}, u32[]{:S(2)}) collective-permute-start(f32[24,128]{1,0:T(8,128)S(1)} %get-tuple-element.39.refs_0_), channel_id=1, source_target_pairs={{0,3},{1,2},{2,1},{3,0},{4,7},{5,6},{6,5},{7,4},{8,11},{9,10},{10,... | collective-permute-start | bytes 36872 | tf_op jit(solution)/shard_map/ppermute | solution.py:451
  21.3 4.6 %collective-permute-start.7 = (f32[24,128]{1,0:T(8,128)S(1)}, f32[24,128]{1,0:T(8,128)S(1)}, u32[]{:S(2)}, u32[]{:S(2)}) collective-permute-start(f32[24,128]{1,0:T(8,128)S(1)} %get-tuple-element.39.refs_0_), channel_id=1, source_target_pairs={{0,2},{1,3},{2,0},{3,1},{4,6},{5,7},{6,4},{7,5},{8,10},{9,11},{10,... | collective-permute-start | bytes 36872 | tf_op jit(solution)/shard_map/ppermute | solution.py:451
  21.9 4.1 %collective-permute-start.6 = (f32[24,128]{1,0:T(8,128)S(1)}, f32[24,128]{1,0:T(8,128)S(1)}, u32[]{:S(2)}, u32[]{:S(2)}) collective-permute-start(f32[24,128]{1,0:T(8,128)S(1)} %get-tuple-element.39.refs_0_), channel_id=1, source_target_pairs={{0,1},{1,0},{2,3},{3,2},{4,5},{5,4},{6,7},{7,6},{8,9},{9,8},{10,11... | collective-permute-start | bytes 36872 | tf_op jit(solution)/shard_map/ppermute | solution.py:451
  26.5 3.3 %collective-permute-start.11 = (f32[24,128]{1,0:T(8,128)S(1)}, f32[24,128]{1,0:T(8,128)S(1)}, u32[]{:S(2)}, u32[]{:S(2)}) collective-permute-start(f32[24,128]{1,0:T(8,128)S(1)} %shard_map.81.refs_0_.refs_4_), channel_id=1, source_target_pairs={{0,12},{4,8},{8,4},{12,0},{1,13},{5,9},{9,5},{13,1},{2,14},{6,10},... | collective-permute-start | bytes 36872 | tf_op jit(solution)/shard_map/ppermute | solution.py:451
  26.6 3.8 %collective-permute-start.10 = (f32[24,128]{1,0:T(8,128)S(1)}, f32[24,128]{1,0:T(8,128)S(1)}, u32[]{:S(2)}, u32[]{:S(2)}) collective-permute-start(f32[24,128]{1,0:T(8,128)S(1)} %shard_map.81.refs_0_.refs_4_), channel_id=1, source_target_pairs={{0,8},{4,12},{8,0},{12,4},{1,9},{5,13},{9,1},{13,5},{2,10},{6,14},... | collective-permute-start | bytes 36872 | tf_op jit(solution)/shard_map/ppermute | solution.py:451
  28.1 2.2 %collective-permute-start.9 = (f32[24,128]{1,0:T(8,128)S(1)}, f32[24,128]{1,0:T(8,128)S(1)}, u32[]{:S(2)}, u32[]{:S(2)}) collective-permute-start(f32[24,128]{1,0:T(8,128)S(1)} %shard_map.81.refs_0_.refs_4_), channel_id=1, source_target_pairs={{0,4},{4,0},{8,12},{12,8},{1,5},{5,1},{9,13},{13,9},{2,6},{6,2},{1... | collective-permute-start | bytes 36872 | tf_op jit(solution)/shard_map/ppermute | solution.py:451
  30.3 10.1 %copy-start = (s32[8192]{0:T(1024)S(1)}, s32[8192]{0:T(1024)}, u32[]{:S(2)}) copy-start(s32[8192]{0:T(1024)} %param.9) | copy-start | bytes 98308
  30.3 10.3 %copy-start.1 = (s32[8192]{0:T(1024)S(1)}, s32[8192]{0:T(1024)}, u32[]{:S(2)}) copy-start(s32[8192]{0:T(1024)} %param.8) | copy-start | bytes 98308
  30.8 5.6 %collective-permute-start.14 = (f32[24,128]{1,0:T(8,128)S(1)}, f32[24,128]{1,0:T(8,128)S(1)}, u32[]{:S(2)}, u32[]{:S(2)}) collective-permute-start(f32[24,128]{1,0:T(8,128)S(1)} %get-tuple-element.44.refs_4_.refs_0_), channel_id=1, source_target_pairs={{0,3},{1,2},{2,1},{3,0},{4,7},{5,6},{6,5},{7,4},{8,11},{9,10},{10,... | collective-permute-start | bytes 36872 | tf_op jit(solution)/shard_map/ppermute | solution.py:451
  33.3 4.6 %collective-permute-start.13 = (f32[24,128]{1,0:T(8,128)S(1)}, f32[24,128]{1,0:T(8,128)S(1)}, u32[]{:S(2)}, u32[]{:S(2)}) collective-permute-start(f32[24,128]{1,0:T(8,128)S(1)} %get-tuple-element.44.refs_4_.refs_0_), channel_id=1, source_target_pairs={{0,2},{1,3},{2,0},{3,1},{4,6},{5,7},{6,4},{7,5},{8,10},{9,11},{10,... | collective-permute-start | bytes 36872 | tf_op jit(solution)/shard_map/ppermute | solution.py:451
  34.3 3.8 %collective-permute-start.12 = (f32[24,128]{1,0:T(8,128)S(1)}, f32[24,128]{1,0:T(8,128)S(1)}, u32[]{:S(2)}, u32[]{:S(2)}) collective-permute-start(f32[24,128]{1,0:T(8,128)S(1)} %get-tuple-element.44.refs_4_.refs_0_), channel_id=1, source_target_pairs={{0,1},{1,0},{2,3},{3,2},{4,5},{5,4},{6,7},{7,6},{8,9},{9,8},{10,11... | collective-permute-start | bytes 36872 | tf_op jit(solution)/shard_map/ppermute | solution.py:451
  38.6 3.3 %collective-permute-start.17 = (f32[24,128]{1,0:T(8,128)S(1)}, f32[24,128]{1,0:T(8,128)S(1)}, u32[]{:S(2)}, u32[]{:S(2)}) collective-permute-start(f32[24,128]{1,0:T(8,128)S(1)} %shard_map.84.refs_0_), channel_id=1, source_target_pairs={{0,12},{4,8},{8,4},{12,0},{1,13},{5,9},{9,5},{13,1},{2,14},{6,10},... | collective-permute-start | bytes 36872 | tf_op jit(solution)/shard_map/ppermute | solution.py:451
  38.6 3.8 %collective-permute-start.16 = (f32[24,128]{1,0:T(8,128)S(1)}, f32[24,128]{1,0:T(8,128)S(1)}, u32[]{:S(2)}, u32[]{:S(2)}) collective-permute-start(f32[24,128]{1,0:T(8,128)S(1)} %shard_map.84.refs_0_), channel_id=1, source_target_pairs={{0,8},{4,12},{8,0},{12,4},{1,9},{5,13},{9,1},{13,5},{2,10},{6,14},... | collective-permute-start | bytes 36872 | tf_op jit(solution)/shard_map/ppermute | solution.py:451
  40.2 2.2 %collective-permute-start.15 = (f32[24,128]{1,0:T(8,128)S(1)}, f32[24,128]{1,0:T(8,128)S(1)}, u32[]{:S(2)}, u32[]{:S(2)}) collective-permute-start(f32[24,128]{1,0:T(8,128)S(1)} %shard_map.84.refs_0_), channel_id=1, source_target_pairs={{0,4},{4,0},{8,12},{12,8},{1,5},{5,1},{9,13},{13,9},{2,6},{6,2},{1... | collective-permute-start | bytes 36872 | tf_op jit(solution)/shard_map/ppermute | solution.py:451

commit v5 on v4

--- a/solution.py
+++ b/solution.py
@@ -1,3 +1,4 @@
+import functools
 import math
 
 import jax
@@ -11,6 +12,7 @@
 LANES = 128
 BLOCKS = CLUSTER // LANES
 ROWS = 8
+STRIP = 32
 ITERS = 3
 entropy = 0.25
 lowest = -1e30
@@ -99,7 +101,7 @@
 
 def first_kernel(
     devices, far_tiles, filled, user_emb, item_emb, far_count, pack, users, items,
-    tiles, item_count, scores, small_sems, sems,
+    tiles, item_count, small_sems, sems,
 ):
     slots = tiles.shape[1]
     groups = user_emb.shape[0] // CLUSTER
@@ -137,33 +139,23 @@
     write_notes(pack, tiles, fixed, 0, item_count[...])
     early = max(1, 3 * fixed // 4)
 
-    def raise_top(slot):
+    for slot in range(slots):
         if slot in (0, early):
             for pair in copies[:early] if slot == 0 else copies[early:]:
                 for copy in pair:
                     copy.wait()
-        user_block = users[slot]
-        top = jnp.full((8, CLUSTER), lowest, jnp.float32)
-        for block in range(BLOCKS):
-            rows = slice(block * LANES, (block + 1) * LANES)
-            part = lax.dot_general(
-                items[slot, rows, :], user_block, (((1,), (1,)), ((), ())),
-                preferred_element_type=jnp.float32,
-            ) * INTO
-            scores[slot, rows, :] = part
-            top = jnp.maximum(top, jnp.max(part.reshape(LANES // 8, 8, CLUSTER), axis=0))
-        return jnp.max(top, axis=0, keepdims=True)
-
-    def add_mass(slot, top):
-        mass = jnp.zeros((8, CLUSTER), jnp.float32)
-        for block in range(BLOCKS):
-            rows = slice(block * LANES, (block + 1) * LANES)
-            terms = jnp.exp2(scores[slot, rows, :] - top)
-            mass += jnp.sum(terms.reshape(LANES // 8, 8, CLUSTER), axis=0)
+        scores = lax.dot_general(
+            items[slot], users[slot], (((1,), (1,)), ((), ())), preferred_element_type=jnp.float32
+        ) * INTO
+        tops, masses = [], []
+        for row in range(0, CLUSTER, STRIP):
+            part = scores[row : row + STRIP].reshape(STRIP // 8, 8, CLUSTER)
+            tops.append(jnp.max(part, axis=0))
+            masses.append(jnp.sum(jnp.exp2(part - tops[-1]), axis=0))
+        top = jnp.max(functools.reduce(jnp.maximum, tops), axis=0, keepdims=True)
+        mass = sum(mass * jnp.exp2(old - top) for mass, old in zip(masses, tops))
         log_mass = top + jnp.log2(jnp.sum(mass, axis=0, keepdims=True))
         put(pack, slot, jnp.where(filled[0, 0] > slot, log_mass, lowest))
-
-    staggered(slots, raise_top, add_mass)
 
 
 def setup_kernel(
@@ -495,7 +487,6 @@
             [
                 small,
                 near(item_counts.shape, jnp.int32),
-                near(tall),
                 pltpu.SemaphoreType.DMA((2,)),
                 pltpu.SemaphoreType.DMA((slots, 2)),
             ],

time: 43.3 us -> 43.2 us (level)
  no operation moved by 1% of the time
where the time goes in v5:
time: 43.2 us; the launch traced here: 42.9 us
  starting transfers between devices  20.5 us (47%)
  waiting for transfers between devices  11.7 us (27%)
  Pallas kernels  9.43 us (22%)
  between operations  1.37 us (3%)
    ppermute x18, starting transfers between devices, exchange(): packs.append(keep(lax.ppermute(pack, axis, route)))  20.5 us
    ppermute x18, waiting for transfers between devices, exchange(): packs.append(keep(lax.ppermute(pack, axis, route)))  11.7 us
    pallas_call x10, Pallas kernels, call(): pl.pallas_call(kernel, out_shape=outs, in_specs=specs or [HERE] * len(ope...  9.43 us
  transfers between devices with their start and end apart: 18, of which 13 were waited for; matrix products, arithmetic and copies ran while one was open for 0% of the time, Pallas kernels for 6%

profile of v5, /device:TPU:0, one launch (start us, length us, event | category | flops | bytes accessed | tf_op | source)
XLA Modules:
  0.0 42.9 jit_solution(2339443218527079065)
XLA Ops:
  1.3 2.9 %shard_map.77 = (f32[24,128]{1,0:T(8,128)S(1)}, bf16[5,512,128]{2,1,0:T(8,128)(2,1)S(1)}, bf16[5,512,128]{2,1,0:T(8,128)(2,1)S(1)}) custom-call(s32[2,5]{1,0:T(2,128)} %bitcast.14, s32[1,1]{1,0:T(1,128)S(6)} %copy.8.refs_1_, bf16[8192,128]{1,0:T(8,128)(2,1)} %refs_2_.1, bf16[8192,128]{1,0:T(8,128)(2,1)} %refs_3_.1, s32[64,128]{1,0:T(8,128)} %bitcast.7), custom_call_target="tpu_custom_call" | custom-call | tf_op jit(solution)/shard_map/pallas_call | solution.py:448
  4.2 5.1 %collective-permute-start.2 = (f32[24,128]{1,0:T(8,128)S(1)}, f32[24,128]{1,0:T(8,128)S(1)}, u32[]{:S(2)}, u32[]{:S(2)}) collective-permute-start(f32[24,128]{1,0:T(8,128)S(1)} %get-tuple-element.25.refs_0_), channel_id=1, source_target_pairs={{0,3},{1,2},{2,1},{3,0},{4,7},{5,6},{6,5},{7,4},{8,11},{9,10},{10,... | collective-permute-start | bytes 36872 | tf_op jit(solution)/shard_map/ppermute | solution.py:443
  9.3 0.0 collective-permute-start.1
  9.3 0.6 %collective-permute-start = (f32[24,128]{1,0:T(8,128)S(1)}, f32[24,128]{1,0:T(8,128)S(1)}, u32[]{:S(2)}, u32[]{:S(2)}) collective-permute-start(f32[24,128]{1,0:T(8,128)S(1)} %get-tuple-element.25.refs_0_), channel_id=1, source_target_pairs={{0,1},{1,0},{2,3},{3,2},{4,5},{5,4},{6,7},{7,6},{8,9},{9,8},{10,11... | collective-permute-start | bytes 36872 | tf_op jit(solution)/shard_map/ppermute | solution.py:443
  10.0 1.6 %shard_map.78 = (f32[5,512,512]{2,1,0:T(8,128)S(1)}, f32[8,512]{1,0:T(8,128)S(1)}, f32[8,512]{1,0:T(8,128)S(1)}, s32[8,128]{1,0:T(8,128)S(1)}, s32[8,128]{1,0:T(...) custom-call(s32[2,5]{1,0:T(2,128)} %bitcast.15, s32[1,1]{1,0:T(1,128)S(6)} %copy.8.refs_1_, ...), custom_call_target="tpu_custom_call" | custom-call | tf_op jit(solution)/shard_map/pallas_call | solution.py:448
  11.6 0.0 collective-permute-done.2.refs_3_
  11.6 2.3 %collective-permute-done.1.refs_2_ = f32[24,128]{1,0:T(8,128)S(1)} collective-permute-done((f32[24,128]{1,0:T(8,128)S(1)}, f32[24,128]{1,0:T(8,128)S(1)}, u32[]{:S(2)}, u32[]{:S(2)}) %collective-permute-start.1) | collective-permute-done | bytes 12320 | tf_op jit(solution)/shard_map/ppermute | solution.py:443
  13.9 0.0 collective-permute-done.refs_1_
  13.9 1.3 %shard_map.79 = (f32[24,128]{1,0:T(8,128)S(1)}, f32[5,512,512]{2,1,0:T(8,128)S(1)}, f32[8,512]{1,0:T(8,128)S(1)}, f32[20,8,128]{2,1,0:T(8,128)S(1)}, f32[8,128]{1,0:T(8,128)S(1)}) custom-call(f32[24,128]{1,0:T(8,128)S(1)} %get-tuple-element.25.refs_0_, f32[24,128]{1,0:T(8,128)S(1)} %collective-permute-done.refs_1_, ...), custom_call_target="tpu_custom_call" | custom-call | tf_op jit(solution)/shard_map/pallas_call | solution.py:448
  15.2 0.1 collective-permute-start.5
  15.3 1.6 %collective-permute-start.4 = (f32[24,128]{1,0:T(8,128)S(1)}, f32[24,128]{1,0:T(8,128)S(1)}, u32[]{:S(2)}, u32[]{:S(2)}) collective-permute-start(f32[24,128]{1,0:T(8,128)S(1)} %get-tuple-element.33.refs_0_), channel_id=1, source_target_pairs={{0,8},{4,12},{8,0},{12,4},{1,9},{5,13},{9,1},{13,5},{2,10},{6,14},... | collective-permute-start | bytes 36872 | tf_op jit(solution)/shard_map/ppermute | solution.py:443
  16.8 0.3 collective-permute-start.3
  17.1 1.3 %collective-permute-done.5.refs_3_ = f32[24,128]{1,0:T(8,128)S(1)} collective-permute-done((f32[24,128]{1,0:T(8,128)S(1)}, f32[24,128]{1,0:T(8,128)S(1)}, u32[]{:S(2)}, u32[]{:S(2)}) %collective-permute-start.5) | collective-permute-done | bytes 12320 | tf_op jit(solution)/shard_map/ppermute | solution.py:443
  18.5 0.6 %collective-permute-done.4.refs_2_ = f32[24,128]{1,0:T(8,128)S(1)} collective-permute-done((f32[24,128]{1,0:T(8,128)S(1)}, f32[24,128]{1,0:T(8,128)S(1)}, u32[]{:S(2)}, u32[]{:S(2)}) %collective-permute-start.4) | collective-permute-done | bytes 12320 | tf_op jit(solution)/shard_map/ppermute | solution.py:443
  19.0 0.0 collective-permute-done.3.refs_1_
  19.0 0.6 %shard_map.80 = (f32[24,128]{1,0:T(8,128)S(1)}, f32[8,512]{1,0:T(8,128)S(1)}, f32[20,8,128]{2,1,0:T(8,128)S(1)}, f32[8,128]{1,0:T(8,128)S(1)}) custom-call(f32[24,128]{1,0:T(8,128)S(1)} %get-tuple-element.33.refs_0_, f32[24,128]{1,0:T(8,128)S(1)} %collective-permute-done.3.refs_1_, f32[24,128]{1,0:T(8,128)S(1)} %collective-permute-done.4.refs_2_, ...), custom_call_target="tpu_custom_call" | custom-call | tf_op jit(solution)/shard_map/pallas_call | solution.py:448
  19.6 1.5 %collective-permute-start.8 = (f32[24,128]{1,0:T(8,128)S(1)}, f32[24,128]{1,0:T(8,128)S(1)}, u32[]{:S(2)}, u32[]{:S(2)}) collective-permute-start(f32[24,128]{1,0:T(8,128)S(1)} %get-tuple-element.39.refs_0_), channel_id=1, source_target_pairs={{0,3},{1,2},{2,1},{3,0},{4,7},{5,6},{6,5},{7,4},{8,11},{9,10},{10,... | collective-permute-start | bytes 36872 | tf_op jit(solution)/shard_map/ppermute | solution.py:443
  21.1 0.6 %collective-permute-start.7 = (f32[24,128]{1,0:T(8,128)S(1)}, f32[24,128]{1,0:T(8,128)S(1)}, u32[]{:S(2)}, u32[]{:S(2)}) collective-permute-start(f32[24,128]{1,0:T(8,128)S(1)} %get-tuple-element.39.refs_0_), channel_id=1, source_target_pairs={{0,2},{1,3},{2,0},{3,1},{4,6},{5,7},{6,4},{7,5},{8,10},{9,11},{10,... | collective-permute-start | bytes 36872 | tf_op jit(solution)/shard_map/ppermute | solution.py:443
  21.8 2.3 %collective-permute-start.6 = (f32[24,128]{1,0:T(8,128)S(1)}, f32[24,128]{1,0:T(8,128)S(1)}, u32[]{:S(2)}, u32[]{:S(2)}) collective-permute-start(f32[24,128]{1,0:T(8,128)S(1)} %get-tuple-element.39.refs_0_), channel_id=1, source_target_pairs={{0,1},{1,0},{2,3},{3,2},{4,5},{5,4},{6,7},{7,6},{8,9},{9,8},{10,11... | collective-permute-start | bytes 36872 | tf_op jit(solution)/shard_map/ppermute | solution.py:443
  24.1 1.1 %collective-permute-done.8.refs_3_ = f32[24,128]{1,0:T(8,128)S(1)} collective-permute-done((f32[24,128]{1,0:T(8,128)S(1)}, f32[24,128]{1,0:T(8,128)S(1)}, u32[]{:S(2)}, u32[]{:S(2)}) %collective-permute-start.8) | collective-permute-done | bytes 12320 | tf_op jit(solution)/shard_map/ppermute | solution.py:443
  25.2 0.6 %collective-permute-done.7.refs_2_ = f32[24,128]{1,0:T(8,128)S(1)} collective-permute-done((f32[24,128]{1,0:T(8,128)S(1)}, f32[24,128]{1,0:T(8,128)S(1)}, u32[]{:S(2)}, u32[]{:S(2)}) %collective-permute-start.7) | collective-permute-done | bytes 12320 | tf_op jit(solution)/shard_map/ppermute | solution.py:443
  25.7 0.1 collective-permute-done.6.refs_1_
  25.9 0.5 %shard_map.81.refs_0_.refs_4_ = f32[24,128]{1,0:T(8,128)S(1)} custom-call(f32[24,128]{1,0:T(8,128)S(1)} %get-tuple-element.39.refs_0_, f32[24,128]{1,0:T(8,128)S(1)} %collective-permute-done.6.refs_1_, f32[24,128]{1,0:T(8,128)S(1)} %collective-permute-done.7.refs_2_, f32[24,128]{1,0:T(8,128)S(1)} %collective-permute-done.8.refs_3_, ...), custom_call_target="tpu_custom_call" | custom-call | tf_op jit(solution)/shard_map/pallas_call | solution.py:448
  26.3 0.1 collective-permute-start.11
  26.4 1.5 %collective-permute-start.10 = (f32[24,128]{1,0:T(8,128)S(1)}, f32[24,128]{1,0:T(8,128)S(1)}, u32[]{:S(2)}, u32[]{:S(2)}) collective-permute-start(f32[24,128]{1,0:T(8,128)S(1)} %shard_map.81.refs_0_.refs_4_), channel_id=1, source_target_pairs={{0,8},{4,12},{8,0},{12,4},{1,9},{5,13},{9,1},{13,5},{2,10},{6,14},... | collective-permute-start | bytes 36872 | tf_op jit(solution)/shard_map/ppermute | solution.py:443
  28.0 0.3 collective-permute-start.9
  28.3 1.4 %collective-permute-done.11.refs_3_.refs_7_ = f32[24,128]{1,0:T(8,128)S(1)} collective-permute-done((f32[24,128]{1,0:T(8,128)S(1)}, f32[24,128]{1,0:T(8,128)S(1)}, u32[]{:S(2)}, u32[]{:S(2)}) %collective-permute-start.11) | collective-permute-done | bytes 12320 | tf_op jit(solution)/shard_map/ppermute | solution.py:443
  29.6 0.6 %collective-permute-done.10.refs_2_.refs_6_ = f32[24,128]{1,0:T(8,128)S(1)} collective-permute-done((f32[24,128]{1,0:T(8,128)S(1)}, f32[24,128]{1,0:T(8,128)S(1)}, u32[]{:S(2)}, u32[]{:S(2)}) %collective-permute-start.10) | collective-permute-done | bytes 12320 | tf_op jit(solution)/shard_map/ppermute | solution.py:443
  30.2 0.0 collective-permute-done.9.refs_1_.refs_5_
  30.2 0.5 %shard_map.82 = (f32[24,128]{1,0:T(8,128)S(1)}, f32[8,512]{1,0:T(8,128)S(1)}) custom-call(f32[24,128]{1,0:T(8,128)S(1)} %shard_map.81.refs_0_.refs_4_, f32[24,128]{1,0:T(8,128)S(1)} %collective-permute-done.9.refs_1_.refs_5_, f32[24,128]{1,0:T(8,128)S(1)} %collective-permute-done.10.refs_2_.refs_6_, f32[24,128]{1,0:T(8,128)S(1)} %collective-permute-done.11.refs_3_.refs_7_, ...), custom_call_target="tpu_custom_call" | custom-call | tf_op jit(solution)/shard_map/pallas_call | solution.py:448
  30.7 2.5 %collective-permute-start.14 = (f32[24,128]{1,0:T(8,128)S(1)}, f32[24,128]{1,0:T(8,128)S(1)}, u32[]{:S(2)}, u32[]{:S(2)}) collective-permute-start(f32[24,128]{1,0:T(8,128)S(1)} %get-tuple-element.44.refs_4_.refs_0_), channel_id=1, source_target_pairs={{0,3},{1,2},{2,1},{3,0},{4,7},{5,6},{6,5},{7,4},{8,11},{9,10},{10,... | collective-permute-start | bytes 36872 | tf_op jit(solution)/shard_map/ppermute | solution.py:443
  33.2 0.9 %collective-permute-start.13 = (f32[24,128]{1,0:T(8,128)S(1)}, f32[24,128]{1,0:T(8,128)S(1)}, u32[]{:S(2)}, u32[]{:S(2)}) collective-permute-start(f32[24,128]{1,0:T(8,128)S(1)} %get-tuple-element.44.refs_4_.refs_0_), channel_id=1, source_target_pairs={{0,2},{1,3},{2,0},{3,1},{4,6},{5,7},{6,4},{7,5},{8,10},{9,11},{10,... | collective-permute-start | bytes 36872 | tf_op jit(solution)/shard_map/ppermute | solution.py:443
  34.1 1.0 %collective-permute-start.12 = (f32[24,128]{1,0:T(8,128)S(1)}, f32[24,128]{1,0:T(8,128)S(1)}, u32[]{:S(2)}, u32[]{:S(2)}) collective-permute-start(f32[24,128]{1,0:T(8,128)S(1)} %get-tuple-element.44.refs_4_.refs_0_), channel_id=1, source_target_pairs={{0,1},{1,0},{2,3},{3,2},{4,5},{5,4},{6,7},{7,6},{8,9},{9,8},{10,11... | collective-permute-start | bytes 36872 | tf_op jit(solution)/shard_map/ppermute | solution.py:443
  35.1 1.1 %collective-permute-done.14.refs_7_.refs_3_ = f32[24,128]{1,0:T(8,128)S(1)} collective-permute-done((f32[24,128]{1,0:T(8,128)S(1)}, f32[24,128]{1,0:T(8,128)S(1)}, u32[]{:S(2)}, u32[]{:S(2)}) %collective-permute-start.14) | collective-permute-done | bytes 12320 | tf_op jit(solution)/shard_map/ppermute | solution.py:443
  36.3 1.5 %collective-permute-done.13.refs_6_.refs_2_ = f32[24,128]{1,0:T(8,128)S(1)} collective-permute-done((f32[24,128]{1,0:T(8,128)S(1)}, f32[24,128]{1,0:T(8,128)S(1)}, u32[]{:S(2)}, u32[]{:S(2)}) %collective-permute-start.13) | collective-permute-done | bytes 12320 | tf_op jit(solution)/shard_map/ppermute | solution.py:443
  37.8 0.1 collective-permute-done.12.refs_5_.refs_1_
  37.9 0.5 %shard_map.84.refs_0_ = f32[24,128]{1,0:T(8,128)S(1)} custom-call(f32[24,128]{1,0:T(8,128)S(1)} %get-tuple-element.44.refs_4_.refs_0_, f32[24,128]{1,0:T(8,128)S(1)} %collective-permute-done.12.refs_5_.refs_1_, f32[24,128]{1,0:T(8,128)S(1)} %collective-permute-done.13.refs_6_.refs_2_, f32[24,128]{1,0:T(8,128)S(1)} %collective-permute-done.14.refs_7_.refs_3_, ...), custom_call_target="tpu_custom_call" | custom-call | tf_op jit(solution)/shard_map/pallas_call | solution.py:448
  38.4 0.1 collective-permute-start.17
  38.5 1.5 %collective-permute-start.16 = (f32[24,128]{1,0:T(8,128)S(1)}, f32[24,128]{1,0:T(8,128)S(1)}, u32[]{:S(2)}, u32[]{:S(2)}) collective-permute-start(f32[24,128]{1,0:T(8,128)S(1)} %shard_map.84.refs_0_), channel_id=1, source_target_pairs={{0,8},{4,12},{8,0},{12,4},{1,9},{5,13},{9,1},{13,5},{2,10},{6,14},... | collective-permute-start | bytes 36872 | tf_op jit(solution)/shard_map/ppermute | solution.py:443
  40.0 0.3 collective-permute-start.15
  40.3 0.0 copy-done
  40.3 0.2 shard_map.85
  40.5 0.0 copy-done.1
  40.5 0.8 %shard_map.83 = f32[64,128]{1,0:T(8,128)} custom-call(f32[24,128]{1,0:T(8,128)S(1)} %get-tuple-element.25.refs_0_, f32[24,128]{1,0:T(8,128)S(1)} %collective-permute-done.refs_1_, f32[24,128]{1,0:T(8,128)S(1)} %collective-permute-done.1.refs_2_, f32[24,128]{1,0:T(8,128)S(1)} %collective-permute-done.2.refs_3_, ...), custom_call_target="tpu_custom_call" | custom-call | tf_op jit(solution)/shard_map/pallas_call | solution.py:448
  41.3 0.4 collective-permute-done.17.refs_3_
  41.7 0.5 %collective-permute-done.16.refs_2_ = f32[24,128]{1,0:T(8,128)S(1)} collective-permute-done((f32[24,128]{1,0:T(8,128)S(1)}, f32[24,128]{1,0:T(8,128)S(1)}, u32[]{:S(2)}, u32[]{:S(2)}) %collective-permute-start.16) | collective-permute-done | bytes 12320 | tf_op jit(solution)/shard_map/ppermute | solution.py:443
  42.2 0.0 collective-permute-done.15.refs_1_
  42.2 0.7 %shard_map.86 = f32[64,128]{1,0:T(8,128)} custom-call(f32[24,128]{1,0:T(8,128)S(1)} %shard_map.84.refs_0_, f32[24,128]{1,0:T(8,128)S(1)} %collective-permute-done.15.refs_1_, f32[24,128]{1,0:T(8,128)S(1)} %collective-permute-done.16.refs_2_, f32[24,128]{1,0:T(8,128)S(1)} %collective-permute-done.17.refs_3_, f32[64,128]{1,0:T(8,128)S(1)} %get-tuple-element.46.refs_4_, ...), custom_call_target="tpu_custom_call" | custom-call | tf_op jit(solution)/shard_map/pallas_call | solution.py:448
  (2 shorter events, 0.0 us)
Async XLA Ops:
  4.2 7.4 %collective-permute-start.2 = (f32[24,128]{1,0:T(8,128)S(1)}, f32[24,128]{1,0:T(8,128)S(1)}, u32[]{:S(2)}, u32[]{:S(2)}) collective-permute-start(f32[24,128]{1,0:T(8,128)S(1)} %get-tuple-element.25.refs_0_), channel_id=1, source_target_pairs={{0,3},{1,2},{2,1},{3,0},{4,7},{5,6},{6,5},{7,4},{8,11},{9,10},{10,... | collective-permute-start | bytes 36872 | tf_op jit(solution)/shard_map/ppermute | solution.py:443
  9.3 4.6 %collective-permute-start.1 = (f32[24,128]{1,0:T(8,128)S(1)}, f32[24,128]{1,0:T(8,128)S(1)}, u32[]{:S(2)}, u32[]{:S(2)}) collective-permute-start(f32[24,128]{1,0:T(8,128)S(1)} %get-tuple-element.25.refs_0_), channel_id=1, source_target_pairs={{0,2},{1,3},{2,0},{3,1},{4,6},{5,7},{6,4},{7,5},{8,10},{9,11},{10,... | collective-permute-start | bytes 36872 | tf_op jit(solution)/shard_map/ppermute | solution.py:443
  9.3 4.6 %collective-permute-start = (f32[24,128]{1,0:T(8,128)S(1)}, f32[24,128]{1,0:T(8,128)S(1)}, u32[]{:S(2)}, u32[]{:S(2)}) collective-permute-start(f32[24,128]{1,0:T(8,128)S(1)} %get-tuple-element.25.refs_0_), channel_id=1, source_target_pairs={{0,1},{1,0},{2,3},{3,2},{4,5},{5,4},{6,7},{7,6},{8,9},{9,8},{10,11... | collective-permute-start | bytes 36872 | tf_op jit(solution)/shard_map/ppermute | solution.py:443
  15.2 3.3 %collective-permute-start.5 = (f32[24,128]{1,0:T(8,128)S(1)}, f32[24,128]{1,0:T(8,128)S(1)}, u32[]{:S(2)}, u32[]{:S(2)}) collective-permute-start(f32[24,128]{1,0:T(8,128)S(1)} %get-tuple-element.33.refs_0_), channel_id=1, source_target_pairs={{0,12},{4,8},{8,4},{12,0},{1,13},{5,9},{9,5},{13,1},{2,14},{6,10},... | collective-permute-start | bytes 36872 | tf_op jit(solution)/shard_map/ppermute | solution.py:443
  15.3 3.8 %collective-permute-start.4 = (f32[24,128]{1,0:T(8,128)S(1)}, f32[24,128]{1,0:T(8,128)S(1)}, u32[]{:S(2)}, u32[]{:S(2)}) collective-permute-start(f32[24,128]{1,0:T(8,128)S(1)} %get-tuple-element.33.refs_0_), channel_id=1, source_target_pairs={{0,8},{4,12},{8,0},{12,4},{1,9},{5,13},{9,1},{13,5},{2,10},{6,14},... | collective-permute-start | bytes 36872 | tf_op jit(solution)/shard_map/ppermute | solution.py:443
  16.8 2.2 %collective-permute-start.3 = (f32[24,128]{1,0:T(8,128)S(1)}, f32[24,128]{1,0:T(8,128)S(1)}, u32[]{:S(2)}, u32[]{:S(2)}) collective-permute-start(f32[24,128]{1,0:T(8,128)S(1)} %get-tuple-element.33.refs_0_), channel_id=1, source_target_pairs={{0,4},{4,0},{8,12},{12,8},{1,5},{5,1},{9,13},{13,9},{2,6},{6,2},{1... | collective-permute-start | bytes 36872 | tf_op jit(solution)/shard_map/ppermute | solution.py:443
  19.6 5.6 %collective-permute-start.8 = (f32[24,128]{1,0:T(8,128)S(1)}, f32[24,128]{1,0:T(8,128)S(1)}, u32[]{:S(2)}, u32[]{:S(2)}) collective-permute-start(f32[24,128]{1,0:T(8,128)S(1)} %get-tuple-element.39.refs_0_), channel_id=1, source_target_pairs={{0,3},{1,2},{2,1},{3,0},{4,7},{5,6},{6,5},{7,4},{8,11},{9,10},{10,... | collective-permute-start | bytes 36872 | tf_op jit(solution)/shard_map/ppermute | solution.py:443
  21.1 4.6 %collective-permute-start.7 = (f32[24,128]{1,0:T(8,128)S(1)}, f32[24,128]{1,0:T(8,128)S(1)}, u32[]{:S(2)}, u32[]{:S(2)}) collective-permute-start(f32[24,128]{1,0:T(8,128)S(1)} %get-tuple-element.39.refs_0_), channel_id=1, source_target_pairs={{0,2},{1,3},{2,0},{3,1},{4,6},{5,7},{6,4},{7,5},{8,10},{9,11},{10,... | collective-permute-start | bytes 36872 | tf_op jit(solution)/shard_map/ppermute | solution.py:443
  21.8 4.1 %collective-permute-start.6 = (f32[24,128]{1,0:T(8,128)S(1)}, f32[24,128]{1,0:T(8,128)S(1)}, u32[]{:S(2)}, u32[]{:S(2)}) collective-permute-start(f32[24,128]{1,0:T(8,128)S(1)} %get-tuple-element.39.refs_0_), channel_id=1, source_target_pairs={{0,1},{1,0},{2,3},{3,2},{4,5},{5,4},{6,7},{7,6},{8,9},{9,8},{10,11... | collective-permute-start | bytes 36872 | tf_op jit(solution)/shard_map/ppermute | solution.py:443
  26.3 3.3 %collective-permute-start.11 = (f32[24,128]{1,0:T(8,128)S(1)}, f32[24,128]{1,0:T(8,128)S(1)}, u32[]{:S(2)}, u32[]{:S(2)}) collective-permute-start(f32[24,128]{1,0:T(8,128)S(1)} %shard_map.81.refs_0_.refs_4_), channel_id=1, source_target_pairs={{0,12},{4,8},{8,4},{12,0},{1,13},{5,9},{9,5},{13,1},{2,14},{6,10},... | collective-permute-start | bytes 36872 | tf_op jit(solution)/shard_map/ppermute | solution.py:443
  26.4 3.8 %collective-permute-start.10 = (f32[24,128]{1,0:T(8,128)S(1)}, f32[24,128]{1,0:T(8,128)S(1)}, u32[]{:S(2)}, u32[]{:S(2)}) collective-permute-start(f32[24,128]{1,0:T(8,128)S(1)} %shard_map.81.refs_0_.refs_4_), channel_id=1, source_target_pairs={{0,8},{4,12},{8,0},{12,4},{1,9},{5,13},{9,1},{13,5},{2,10},{6,14},... | collective-permute-start | bytes 36872 | tf_op jit(solution)/shard_map/ppermute | solution.py:443
  28.0 2.2 %collective-permute-start.9 = (f32[24,128]{1,0:T(8,128)S(1)}, f32[24,128]{1,0:T(8,128)S(1)}, u32[]{:S(2)}, u32[]{:S(2)}) collective-permute-start(f32[24,128]{1,0:T(8,128)S(1)} %shard_map.81.refs_0_.refs_4_), channel_id=1, source_target_pairs={{0,4},{4,0},{8,12},{12,8},{1,5},{5,1},{9,13},{13,9},{2,6},{6,2},{1... | collective-permute-start | bytes 36872 | tf_op jit(solution)/shard_map/ppermute | solution.py:443
  30.2 10.2 %copy-start = (s32[8192]{0:T(1024)S(1)}, s32[8192]{0:T(1024)}, u32[]{:S(2)}) copy-start(s32[8192]{0:T(1024)} %param.9) | copy-start | bytes 98308
  30.2 10.3 %copy-start.1 = (s32[8192]{0:T(1024)S(1)}, s32[8192]{0:T(1024)}, u32[]{:S(2)}) copy-start(s32[8192]{0:T(1024)} %param.8) | copy-start | bytes 98308
  30.7 5.6 %collective-permute-start.14 = (f32[24,128]{1,0:T(8,128)S(1)}, f32[24,128]{1,0:T(8,128)S(1)}, u32[]{:S(2)}, u32[]{:S(2)}) collective-permute-start(f32[24,128]{1,0:T(8,128)S(1)} %get-tuple-element.44.refs_4_.refs_0_), channel_id=1, source_target_pairs={{0,3},{1,2},{2,1},{3,0},{4,7},{5,6},{6,5},{7,4},{8,11},{9,10},{10,... | collective-permute-start | bytes 36872 | tf_op jit(solution)/shard_map/ppermute | solution.py:443
  33.2 4.6 %collective-permute-start.13 = (f32[24,128]{1,0:T(8,128)S(1)}, f32[24,128]{1,0:T(8,128)S(1)}, u32[]{:S(2)}, u32[]{:S(2)}) collective-permute-start(f32[24,128]{1,0:T(8,128)S(1)} %get-tuple-element.44.refs_4_.refs_0_), channel_id=1, source_target_pairs={{0,2},{1,3},{2,0},{3,1},{4,6},{5,7},{6,4},{7,5},{8,10},{9,11},{10,... | collective-permute-start | bytes 36872 | tf_op jit(solution)/shard_map/ppermute | solution.py:443
  34.1 3.8 %collective-permute-start.12 = (f32[24,128]{1,0:T(8,128)S(1)}, f32[24,128]{1,0:T(8,128)S(1)}, u32[]{:S(2)}, u32[]{:S(2)}) collective-permute-start(f32[24,128]{1,0:T(8,128)S(1)} %get-tuple-element.44.refs_4_.refs_0_), channel_id=1, source_target_pairs={{0,1},{1,0},{2,3},{3,2},{4,5},{5,4},{6,7},{7,6},{8,9},{9,8},{10,11... | collective-permute-start | bytes 36872 | tf_op jit(solution)/shard_map/ppermute | solution.py:443
  38.4 3.3 %collective-permute-start.17 = (f32[24,128]{1,0:T(8,128)S(1)}, f32[24,128]{1,0:T(8,128)S(1)}, u32[]{:S(2)}, u32[]{:S(2)}) collective-permute-start(f32[24,128]{1,0:T(8,128)S(1)} %shard_map.84.refs_0_), channel_id=1, source_target_pairs={{0,12},{4,8},{8,4},{12,0},{1,13},{5,9},{9,5},{13,1},{2,14},{6,10},... | collective-permute-start | bytes 36872 | tf_op jit(solution)/shard_map/ppermute | solution.py:443
  38.5 3.8 %collective-permute-start.16 = (f32[24,128]{1,0:T(8,128)S(1)}, f32[24,128]{1,0:T(8,128)S(1)}, u32[]{:S(2)}, u32[]{:S(2)}) collective-permute-start(f32[24,128]{1,0:T(8,128)S(1)} %shard_map.84.refs_0_), channel_id=1, source_target_pairs={{0,8},{4,12},{8,0},{12,4},{1,9},{5,13},{9,1},{13,5},{2,10},{6,14},... | collective-permute-start | bytes 36872 | tf_op jit(solution)/shard_map/ppermute | solution.py:443
  40.0 2.2 %collective-permute-start.15 = (f32[24,128]{1,0:T(8,128)S(1)}, f32[24,128]{1,0:T(8,128)S(1)}, u32[]{:S(2)}, u32[]{:S(2)}) collective-permute-start(f32[24,128]{1,0:T(8,128)S(1)} %shard_map.84.refs_0_), channel_id=1, source_target_pairs={{0,4},{4,0},{8,12},{12,8},{1,5},{5,1},{9,13},{13,9},{2,6},{6,2},{1... | collective-permute-start | bytes 36872 | tf_op jit(solution)/shard_map/ppermute | solution.py:443

commit v6 on v5

--- a/solution.py
+++ b/solution.py
@@ -160,7 +160,7 @@
 
 def setup_kernel(
     devices, far_tiles, filled, users, items, far_users, far_items,
-    table, user_here, item_here, user_ids, item_ids, notes, active,
+    table, user_here, item_here, user_ids, item_ids, notes, active, user_log, item_log,
     tiles, user_count, item_count, sems,
 ):
     slots = tiles.shape[1]
@@ -202,6 +202,7 @@
                     pl.ds(group * BLOCKS + block, 1), :
                 ].astype(jnp.float32)
         ids[...] = numbers
+        (user_log, item_log)[which][...] = jnp.log2(here[...])
     fixed = fixed_slots(user_count.shape[0] // BLOCKS, *devices, slots)
     write_notes(notes, tiles, fixed, 1, user_count[...])
 
@@ -274,12 +275,12 @@
 
 def second_kernel(axis, devices, fixed, groups, *refs):
     packs = refs[:devices]
-    table, ids, counts, notes, active, pack, terms, tops, masks, totals, potential = refs[devices:]
+    table, ids, log_counts, notes, active, pack, terms, tops, masks, totals, potential = refs[devices:]
     slots = table.shape[0]
     chosen = matches(packs, owners_of(axis, devices), ids[...], slots, fixed, groups)
     store_masks(masks, chosen)
     totals[...] = jnp.broadcast_to(total_in(packs, slots, fixed), totals.shape)
-    potential[...] = jnp.log2(counts[...]) - log_merge(packs, chosen, slots, EVERY, ROWS)
+    potential[...] = log_counts[...] - log_merge(packs, chosen, slots, EVERY, ROWS)
     pack[...] = notes[...]
     tops[...] = jnp.full(VECTORS, lowest, jnp.float32)
 
@@ -335,12 +336,12 @@
 
 def third_kernel(axis, devices, fixed, groups, *refs):
     packs = refs[:devices]
-    terms, tops, ids, counts, item_total, pack, factor, masks, totals = refs[devices:]
+    terms, tops, ids, log_counts, item_total, pack, factor, masks, totals = refs[devices:]
     slots = terms.shape[0]
     chosen = matches(packs, owners_of(axis, devices), ids[...], slots, fixed, groups)
     store_masks(masks, chosen)
     totals[...] = jnp.broadcast_to(total_in(packs, slots, fixed), totals.shape)
-    log_share = jnp.log2(counts[...] / wide(item_total[...]))
+    log_share = log_counts[...] - wide(jnp.log2(item_total[...]))
     merged = log_merge(packs, chosen, slots, EVERY, ROWS)
     factor[...] = jnp.exp2(tops[...] + (log_share - merged))
     row_sums(terms, factor, pack)
@@ -492,9 +493,9 @@
             ],
         )
         first_packs = exchange(pack, "item", n_item)
-        table, user_here, item_here, user_ids, item_ids, notes, active = call(
+        table, user_here, item_here, user_ids, item_ids, notes, active, user_log, item_log = call(
             bind(setup_kernel, (n_user, n_item)),
-            [near(tall), vectors, vectors, numbers, numbers, packed, vectors],
+            [near(tall), vectors, vectors, numbers, numbers, packed, vectors, vectors, vectors],
             (
                 away(far_tiles), tile_count, keep(users), keep(items),
                 away(user_counts), away(item_counts),
@@ -510,7 +511,7 @@
         pack, terms, tops, user_masks, item_total = call(
             bind(second_kernel, "item", n_item, fixed, groups),
             [packed, near(tall), vectors, near((n_item * slots, ROWS, LANES)), splat],
-            (*first_packs, keep(table), user_ids, user_here, notes, active),
+            (*first_packs, keep(table), user_ids, user_log, notes, active),
             scratch=[near(VECTORS)],
         )
         terms = keep(terms)
@@ -518,7 +519,7 @@
         pack, factor, item_masks, user_total = call(
             bind(third_kernel, "user", n_user, fixed, groups),
             [packed, vectors, near((n_user * slots, ROWS, LANES)), splat],
-            (*second_packs, terms, tops, item_ids, item_here, item_total),
+            (*second_packs, terms, tops, item_ids, item_log, item_total),
         )
         item_packs = [second_packs]
         for iteration in range(1, ITERS):

time: 43.2 us -> 43.1 us (level)
  Pallas kernels: 9.43 us -> 8.82 us
  waiting for transfers between devices: 11.7 us -> 12.3 us
    ppermute x18, waiting for transfers between devices: 11.7 us -> 12.3 us  [exchange(): packs.append(keep(lax.ppermute(pack, axis, route)))]
    pallas_call x10, Pallas kernels: 9.43 us -> 8.82 us  [call(): pl.pallas_call(kernel, out_shape=outs, in_specs=specs or [HERE] * len(ope...]
  transfers between devices with their start and end apart: 18 -> 18, of which waited for: 13 -> 13; matrix products, arithmetic and copies ran while one was open for 0% -> 0% of each run, Pallas kernels for 6% -> 5%
where the time goes in v6:
time: 43.1 us; the launch traced here: 43 us
  starting transfers between devices  20.5 us (48%)
  waiting for transfers between devices  12.3 us (29%)
  Pallas kernels  8.82 us (20%)
  between operations  1.36 us (3%)
    ppermute x18, starting transfers between devices, exchange(): packs.append(keep(lax.ppermute(pack, axis, route)))  20.5 us
    ppermute x18, waiting for transfers between devices, exchange(): packs.append(keep(lax.ppermute(pack, axis, route)))  12.3 us
    pallas_call x10, Pallas kernels, call(): pl.pallas_call(kernel, out_shape=outs, in_specs=specs or [HERE] * len(ope...  8.82 us
  transfers between devices with their start and end apart: 18, of which 13 were waited for; matrix products, arithmetic and copies ran while one was open for 0% of the time, Pallas kernels for 5%

profile of v6, /device:TPU:0, one launch (start us, length us, event | category | flops | bytes accessed | tf_op | source)
XLA Modules:
  0.0 43.0 jit_solution(4129975569107005003)
XLA Ops:
  1.3 2.9 %shard_map.77 = (f32[24,128]{1,0:T(8,128)S(1)}, bf16[5,512,128]{2,1,0:T(8,128)(2,1)S(1)}, bf16[5,512,128]{2,1,0:T(8,128)(2,1)S(1)}) custom-call(s32[2,5]{1,0:T(2,128)} %bitcast.14, s32[1,1]{1,0:T(1,128)S(6)} %copy.8.refs_1_, bf16[8192,128]{1,0:T(8,128)(2,1)} %refs_2_.1, bf16[8192,128]{1,0:T(8,128)(2,1)} %refs_3_.1, s32[64,128]{1,0:T(8,128)} %bitcast.7), custom_call_target="tpu_custom_call" | custom-call | tf_op jit(solution)/shard_map/pallas_call | solution.py:449
  4.2 5.1 %collective-permute-start.2 = (f32[24,128]{1,0:T(8,128)S(1)}, f32[24,128]{1,0:T(8,128)S(1)}, u32[]{:S(2)}, u32[]{:S(2)}) collective-permute-start(f32[24,128]{1,0:T(8,128)S(1)} %get-tuple-element.27.refs_0_), channel_id=1, source_target_pairs={{0,3},{1,2},{2,1},{3,0},{4,7},{5,6},{6,5},{7,4},{8,11},{9,10},{10,... | collective-permute-start | bytes 36872 | tf_op jit(solution)/shard_map/ppermute | solution.py:444
  9.3 0.0 collective-permute-start.1
  9.3 0.6 %collective-permute-start = (f32[24,128]{1,0:T(8,128)S(1)}, f32[24,128]{1,0:T(8,128)S(1)}, u32[]{:S(2)}, u32[]{:S(2)}) collective-permute-start(f32[24,128]{1,0:T(8,128)S(1)} %get-tuple-element.27.refs_0_), channel_id=1, source_target_pairs={{0,1},{1,0},{2,3},{3,2},{4,5},{5,4},{6,7},{7,6},{8,9},{9,8},{10,11... | collective-permute-start | bytes 36872 | tf_op jit(solution)/shard_map/ppermute | solution.py:444
  10.0 1.0 %shard_map.78 = (f32[5,512,512]{2,1,0:T(8,128)S(1)}, f32[8,512]{1,0:T(8,128)S(1)}, f32[8,512]{1,0:T(8,128)S(1)}, s32[8,128]{1,0:T(8,128)S(1)}, s32[8,128]{1,0:T(...) custom-call(s32[2,5]{1,0:T(2,128)} %bitcast.15, ...), custom_call_target="tpu_custom_call" | custom-call | tf_op jit(solution)/shard_map/pallas_call | solution.py:449
  11.0 0.0 collective-permute-done.2.refs_3_
  11.0 2.9 %collective-permute-done.1.refs_2_ = f32[24,128]{1,0:T(8,128)S(1)} collective-permute-done((f32[24,128]{1,0:T(8,128)S(1)}, f32[24,128]{1,0:T(8,128)S(1)}, u32[]{:S(2)}, u32[]{:S(2)}) %collective-permute-start.1) | collective-permute-done | bytes 12320 | tf_op jit(solution)/shard_map/ppermute | solution.py:444
  13.9 0.0 collective-permute-done.refs_1_
  13.9 1.3 %shard_map.79 = (f32[24,128]{1,0:T(8,128)S(1)}, f32[5,512,512]{2,1,0:T(8,128)S(1)}, f32[8,512]{1,0:T(8,128)S(1)}, f32[20,8,128]{2,1,0:T(8,128)S(1)}, f32[8,128]{1,0:T(8,128)S(1)}) custom-call(f32[24,128]{1,0:T(8,128)S(1)} %get-tuple-element.27.refs_0_, f32[24,128]{1,0:T(8,128)S(1)} %collective-permute-done.refs_1_, ...), custom_call_target="tpu_custom_call" | custom-call | tf_op jit(solution)/shard_map/pallas_call | solution.py:449
  15.2 0.1 collective-permute-start.5
  15.3 1.6 %collective-permute-start.4 = (f32[24,128]{1,0:T(8,128)S(1)}, f32[24,128]{1,0:T(8,128)S(1)}, u32[]{:S(2)}, u32[]{:S(2)}) collective-permute-start(f32[24,128]{1,0:T(8,128)S(1)} %get-tuple-element.35.refs_0_), channel_id=1, source_target_pairs={{0,8},{4,12},{8,0},{12,4},{1,9},{5,13},{9,1},{13,5},{2,10},{6,14},... | collective-permute-start | bytes 36872 | tf_op jit(solution)/shard_map/ppermute | solution.py:444
  16.8 0.3 collective-permute-start.3
  17.1 1.3 %collective-permute-done.5.refs_3_ = f32[24,128]{1,0:T(8,128)S(1)} collective-permute-done((f32[24,128]{1,0:T(8,128)S(1)}, f32[24,128]{1,0:T(8,128)S(1)}, u32[]{:S(2)}, u32[]{:S(2)}) %collective-permute-start.5) | collective-permute-done | bytes 12320 | tf_op jit(solution)/shard_map/ppermute | solution.py:444
  18.5 0.6 %collective-permute-done.4.refs_2_ = f32[24,128]{1,0:T(8,128)S(1)} collective-permute-done((f32[24,128]{1,0:T(8,128)S(1)}, f32[24,128]{1,0:T(8,128)S(1)}, u32[]{:S(2)}, u32[]{:S(2)}) %collective-permute-start.4) | collective-permute-done | bytes 12320 | tf_op jit(solution)/shard_map/ppermute | solution.py:444
  19.0 0.0 collective-permute-done.3.refs_1_
  19.0 0.6 %shard_map.80 = (f32[24,128]{1,0:T(8,128)S(1)}, f32[8,512]{1,0:T(8,128)S(1)}, f32[20,8,128]{2,1,0:T(8,128)S(1)}, f32[8,128]{1,0:T(8,128)S(1)}) custom-call(f32[24,128]{1,0:T(8,128)S(1)} %get-tuple-element.35.refs_0_, f32[24,128]{1,0:T(8,128)S(1)} %collective-permute-done.3.refs_1_, f32[24,128]{1,0:T(8,128)S(1)} %collective-permute-done.4.refs_2_, ...), custom_call_target="tpu_custom_call" | custom-call | tf_op jit(solution)/shard_map/pallas_call | solution.py:449
  19.6 1.5 %collective-permute-start.8 = (f32[24,128]{1,0:T(8,128)S(1)}, f32[24,128]{1,0:T(8,128)S(1)}, u32[]{:S(2)}, u32[]{:S(2)}) collective-permute-start(f32[24,128]{1,0:T(8,128)S(1)} %get-tuple-element.41.refs_0_), channel_id=1, source_target_pairs={{0,3},{1,2},{2,1},{3,0},{4,7},{5,6},{6,5},{7,4},{8,11},{9,10},{10,... | collective-permute-start | bytes 36872 | tf_op jit(solution)/shard_map/ppermute | solution.py:444
  21.1 0.6 %collective-permute-start.7 = (f32[24,128]{1,0:T(8,128)S(1)}, f32[24,128]{1,0:T(8,128)S(1)}, u32[]{:S(2)}, u32[]{:S(2)}) collective-permute-start(f32[24,128]{1,0:T(8,128)S(1)} %get-tuple-element.41.refs_0_), channel_id=1, source_target_pairs={{0,2},{1,3},{2,0},{3,1},{4,6},{5,7},{6,4},{7,5},{8,10},{9,11},{10,... | collective-permute-start | bytes 36872 | tf_op jit(solution)/shard_map/ppermute | solution.py:444
  21.8 2.3 %collective-permute-start.6 = (f32[24,128]{1,0:T(8,128)S(1)}, f32[24,128]{1,0:T(8,128)S(1)}, u32[]{:S(2)}, u32[]{:S(2)}) collective-permute-start(f32[24,128]{1,0:T(8,128)S(1)} %get-tuple-element.41.refs_0_), channel_id=1, source_target_pairs={{0,1},{1,0},{2,3},{3,2},{4,5},{5,4},{6,7},{7,6},{8,9},{9,8},{10,11... | collective-permute-start | bytes 36872 | tf_op jit(solution)/shard_map/ppermute | solution.py:444
  24.1 1.1 %collective-permute-done.8.refs_3_ = f32[24,128]{1,0:T(8,128)S(1)} collective-permute-done((f32[24,128]{1,0:T(8,128)S(1)}, f32[24,128]{1,0:T(8,128)S(1)}, u32[]{:S(2)}, u32[]{:S(2)}) %collective-permute-start.8) | collective-permute-done | bytes 12320 | tf_op jit(solution)/shard_map/ppermute | solution.py:444
  25.2 0.6 %collective-permute-done.7.refs_2_ = f32[24,128]{1,0:T(8,128)S(1)} collective-permute-done((f32[24,128]{1,0:T(8,128)S(1)}, f32[24,128]{1,0:T(8,128)S(1)}, u32[]{:S(2)}, u32[]{:S(2)}) %collective-permute-start.7) | collective-permute-done | bytes 12320 | tf_op jit(solution)/shard_map/ppermute | solution.py:444
  25.7 0.1 collective-permute-done.6.refs_1_
  25.9 0.5 %shard_map.81.refs_0_.refs_4_ = f32[24,128]{1,0:T(8,128)S(1)} custom-call(f32[24,128]{1,0:T(8,128)S(1)} %get-tuple-element.41.refs_0_, f32[24,128]{1,0:T(8,128)S(1)} %collective-permute-done.6.refs_1_, f32[24,128]{1,0:T(8,128)S(1)} %collective-permute-done.7.refs_2_, f32[24,128]{1,0:T(8,128)S(1)} %collective-permute-done.8.refs_3_, ...), custom_call_target="tpu_custom_call" | custom-call | tf_op jit(solution)/shard_map/pallas_call | solution.py:449
  26.3 0.1 collective-permute-start.11
  26.4 1.5 %collective-permute-start.10 = (f32[24,128]{1,0:T(8,128)S(1)}, f32[24,128]{1,0:T(8,128)S(1)}, u32[]{:S(2)}, u32[]{:S(2)}) collective-permute-start(f32[24,128]{1,0:T(8,128)S(1)} %shard_map.81.refs_0_.refs_4_), channel_id=1, source_target_pairs={{0,8},{4,12},{8,0},{12,4},{1,9},{5,13},{9,1},{13,5},{2,10},{6,14},... | collective-permute-start | bytes 36872 | tf_op jit(solution)/shard_map/ppermute | solution.py:444
  28.0 0.3 collective-permute-start.9
  28.3 1.4 %collective-permute-done.11.refs_3_.refs_7_ = f32[24,128]{1,0:T(8,128)S(1)} collective-permute-done((f32[24,128]{1,0:T(8,128)S(1)}, f32[24,128]{1,0:T(8,128)S(1)}, u32[]{:S(2)}, u32[]{:S(2)}) %collective-permute-start.11) | collective-permute-done | bytes 12320 | tf_op jit(solution)/shard_map/ppermute | solution.py:444
  29.6 0.6 %collective-permute-done.10.refs_2_.refs_6_ = f32[24,128]{1,0:T(8,128)S(1)} collective-permute-done((f32[24,128]{1,0:T(8,128)S(1)}, f32[24,128]{1,0:T(8,128)S(1)}, u32[]{:S(2)}, u32[]{:S(2)}) %collective-permute-start.10) | collective-permute-done | bytes 12320 | tf_op jit(solution)/shard_map/ppermute | solution.py:444
  30.2 0.0 collective-permute-done.9.refs_1_.refs_5_
  30.2 0.5 %shard_map.82 = (f32[24,128]{1,0:T(8,128)S(1)}, f32[8,512]{1,0:T(8,128)S(1)}) custom-call(f32[24,128]{1,0:T(8,128)S(1)} %shard_map.81.refs_0_.refs_4_, f32[24,128]{1,0:T(8,128)S(1)} %collective-permute-done.9.refs_1_.refs_5_, f32[24,128]{1,0:T(8,128)S(1)} %collective-permute-done.10.refs_2_.refs_6_, f32[24,128]{1,0:T(8,128)S(1)} %collective-permute-done.11.refs_3_.refs_7_, ...), custom_call_target="tpu_custom_call" | custom-call | tf_op jit(solution)/shard_map/pallas_call | solution.py:449
  30.7 2.5 %collective-permute-start.14 = (f32[24,128]{1,0:T(8,128)S(1)}, f32[24,128]{1,0:T(8,128)S(1)}, u32[]{:S(2)}, u32[]{:S(2)}) collective-permute-start(f32[24,128]{1,0:T(8,128)S(1)} %get-tuple-element.48.refs_4_.refs_0_), channel_id=1, source_target_pairs={{0,3},{1,2},{2,1},{3,0},{4,7},{5,6},{6,5},{7,4},{8,11},{9,10},{10,... | collective-permute-start | bytes 36872 | tf_op jit(solution)/shard_map/ppermute | solution.py:444
  33.2 0.9 %collective-permute-start.13 = (f32[24,128]{1,0:T(8,128)S(1)}, f32[24,128]{1,0:T(8,128)S(1)}, u32[]{:S(2)}, u32[]{:S(2)}) collective-permute-start(f32[24,128]{1,0:T(8,128)S(1)} %get-tuple-element.48.refs_4_.refs_0_), channel_id=1, source_target_pairs={{0,2},{1,3},{2,0},{3,1},{4,6},{5,7},{6,4},{7,5},{8,10},{9,11},{10,... | collective-permute-start | bytes 36872 | tf_op jit(solution)/shard_map/ppermute | solution.py:444
  34.1 1.0 %collective-permute-start.12 = (f32[24,128]{1,0:T(8,128)S(1)}, f32[24,128]{1,0:T(8,128)S(1)}, u32[]{:S(2)}, u32[]{:S(2)}) collective-permute-start(f32[24,128]{1,0:T(8,128)S(1)} %get-tuple-element.48.refs_4_.refs_0_), channel_id=1, source_target_pairs={{0,1},{1,0},{2,3},{3,2},{4,5},{5,4},{6,7},{7,6},{8,9},{9,8},{10,11... | collective-permute-start | bytes 36872 | tf_op jit(solution)/shard_map/ppermute | solution.py:444
  35.1 1.1 %collective-permute-done.14.refs_7_.refs_3_ = f32[24,128]{1,0:T(8,128)S(1)} collective-permute-done((f32[24,128]{1,0:T(8,128)S(1)}, f32[24,128]{1,0:T(8,128)S(1)}, u32[]{:S(2)}, u32[]{:S(2)}) %collective-permute-start.14) | collective-permute-done | bytes 12320 | tf_op jit(solution)/shard_map/ppermute | solution.py:444
  36.3 1.5 %collective-permute-done.13.refs_6_.refs_2_ = f32[24,128]{1,0:T(8,128)S(1)} collective-permute-done((f32[24,128]{1,0:T(8,128)S(1)}, f32[24,128]{1,0:T(8,128)S(1)}, u32[]{:S(2)}, u32[]{:S(2)}) %collective-permute-start.13) | collective-permute-done | bytes 12320 | tf_op jit(solution)/shard_map/ppermute | solution.py:444
  37.8 0.1 collective-permute-done.12.refs_5_.refs_1_
  37.9 0.5 %shard_map.84.refs_0_ = f32[24,128]{1,0:T(8,128)S(1)} custom-call(f32[24,128]{1,0:T(8,128)S(1)} %get-tuple-element.48.refs_4_.refs_0_, f32[24,128]{1,0:T(8,128)S(1)} %collective-permute-done.12.refs_5_.refs_1_, f32[24,128]{1,0:T(8,128)S(1)} %collective-permute-done.13.refs_6_.refs_2_, f32[24,128]{1,0:T(8,128)S(1)} %collective-permute-done.14.refs_7_.refs_3_, ...), custom_call_target="tpu_custom_call" | custom-call | tf_op jit(solution)/shard_map/pallas_call | solution.py:449
  38.4 0.1 collective-permute-start.17
  38.5 1.5 %collective-permute-start.16 = (f32[24,128]{1,0:T(8,128)S(1)}, f32[24,128]{1,0:T(8,128)S(1)}, u32[]{:S(2)}, u32[]{:S(2)}) collective-permute-start(f32[24,128]{1,0:T(8,128)S(1)} %shard_map.84.refs_0_), channel_id=1, source_target_pairs={{0,8},{4,12},{8,0},{12,4},{1,9},{5,13},{9,1},{13,5},{2,10},{6,14},... | collective-permute-start | bytes 36872 | tf_op jit(solution)/shard_map/ppermute | solution.py:444
  40.0 0.3 collective-permute-start.15
  40.3 0.0 copy-done
  40.3 0.2 shard_map.85
  40.5 0.0 copy-done.1
  40.5 0.8 %shard_map.83 = f32[64,128]{1,0:T(8,128)} custom-call(f32[24,128]{1,0:T(8,128)S(1)} %get-tuple-element.27.refs_0_, f32[24,128]{1,0:T(8,128)S(1)} %collective-permute-done.refs_1_, f32[24,128]{1,0:T(8,128)S(1)} %collective-permute-done.1.refs_2_, f32[24,128]{1,0:T(8,128)S(1)} %collective-permute-done.2.refs_3_, ...), custom_call_target="tpu_custom_call" | custom-call | tf_op jit(solution)/shard_map/pallas_call | solution.py:449
  41.3 0.4 collective-permute-done.17.refs_3_
  41.7 0.5 %collective-permute-done.16.refs_2_ = f32[24,128]{1,0:T(8,128)S(1)} collective-permute-done((f32[24,128]{1,0:T(8,128)S(1)}, f32[24,128]{1,0:T(8,128)S(1)}, u32[]{:S(2)}, u32[]{:S(2)}) %collective-permute-start.16) | collective-permute-done | bytes 12320 | tf_op jit(solution)/shard_map/ppermute | solution.py:444
  42.3 0.0 collective-permute-done.15.refs_1_
  42.3 0.7 %shard_map.86 = f32[64,128]{1,0:T(8,128)} custom-call(f32[24,128]{1,0:T(8,128)S(1)} %shard_map.84.refs_0_, f32[24,128]{1,0:T(8,128)S(1)} %collective-permute-done.15.refs_1_, f32[24,128]{1,0:T(8,128)S(1)} %collective-permute-done.16.refs_2_, f32[24,128]{1,0:T(8,128)S(1)} %collective-permute-done.17.refs_3_, f32[64,128]{1,0:T(8,128)S(1)} %get-tuple-element.50.refs_4_, ...), custom_call_target="tpu_custom_call" | custom-call | tf_op jit(solution)/shard_map/pallas_call | solution.py:449
  (2 shorter events, 0.0 us)
Async XLA Ops:
  4.2 6.8 %collective-permute-start.2 = (f32[24,128]{1,0:T(8,128)S(1)}, f32[24,128]{1,0:T(8,128)S(1)}, u32[]{:S(2)}, u32[]{:S(2)}) collective-permute-start(f32[24,128]{1,0:T(8,128)S(1)} %get-tuple-element.27.refs_0_), channel_id=1, source_target_pairs={{0,3},{1,2},{2,1},{3,0},{4,7},{5,6},{6,5},{7,4},{8,11},{9,10},{10,... | collective-permute-start | bytes 36872 | tf_op jit(solution)/shard_map/ppermute | solution.py:444
  9.3 4.6 %collective-permute-start.1 = (f32[24,128]{1,0:T(8,128)S(1)}, f32[24,128]{1,0:T(8,128)S(1)}, u32[]{:S(2)}, u32[]{:S(2)}) collective-permute-start(f32[24,128]{1,0:T(8,128)S(1)} %get-tuple-element.27.refs_0_), channel_id=1, source_target_pairs={{0,2},{1,3},{2,0},{3,1},{4,6},{5,7},{6,4},{7,5},{8,10},{9,11},{10,... | collective-permute-start | bytes 36872 | tf_op jit(solution)/shard_map/ppermute | solution.py:444
  9.3 4.6 %collective-permute-start = (f32[24,128]{1,0:T(8,128)S(1)}, f32[24,128]{1,0:T(8,128)S(1)}, u32[]{:S(2)}, u32[]{:S(2)}) collective-permute-start(f32[24,128]{1,0:T(8,128)S(1)} %get-tuple-element.27.refs_0_), channel_id=1, source_target_pairs={{0,1},{1,0},{2,3},{3,2},{4,5},{5,4},{6,7},{7,6},{8,9},{9,8},{10,11... | collective-permute-start | bytes 36872 | tf_op jit(solution)/shard_map/ppermute | solution.py:444
  15.2 3.3 %collective-permute-start.5 = (f32[24,128]{1,0:T(8,128)S(1)}, f32[24,128]{1,0:T(8,128)S(1)}, u32[]{:S(2)}, u32[]{:S(2)}) collective-permute-start(f32[24,128]{1,0:T(8,128)S(1)} %get-tuple-element.35.refs_0_), channel_id=1, source_target_pairs={{0,12},{4,8},{8,4},{12,0},{1,13},{5,9},{9,5},{13,1},{2,14},{6,10},... | collective-permute-start | bytes 36872 | tf_op jit(solution)/shard_map/ppermute | solution.py:444
  15.3 3.8 %collective-permute-start.4 = (f32[24,128]{1,0:T(8,128)S(1)}, f32[24,128]{1,0:T(8,128)S(1)}, u32[]{:S(2)}, u32[]{:S(2)}) collective-permute-start(f32[24,128]{1,0:T(8,128)S(1)} %get-tuple-element.35.refs_0_), channel_id=1, source_target_pairs={{0,8},{4,12},{8,0},{12,4},{1,9},{5,13},{9,1},{13,5},{2,10},{6,14},... | collective-permute-start | bytes 36872 | tf_op jit(solution)/shard_map/ppermute | solution.py:444
  16.8 2.2 %collective-permute-start.3 = (f32[24,128]{1,0:T(8,128)S(1)}, f32[24,128]{1,0:T(8,128)S(1)}, u32[]{:S(2)}, u32[]{:S(2)}) collective-permute-start(f32[24,128]{1,0:T(8,128)S(1)} %get-tuple-element.35.refs_0_), channel_id=1, source_target_pairs={{0,4},{4,0},{8,12},{12,8},{1,5},{5,1},{9,13},{13,9},{2,6},{6,2},{1... | collective-permute-start | bytes 36872 | tf_op jit(solution)/shard_map/ppermute | solution.py:444
  19.6 5.6 %collective-permute-start.8 = (f32[24,128]{1,0:T(8,128)S(1)}, f32[24,128]{1,0:T(8,128)S(1)}, u32[]{:S(2)}, u32[]{:S(2)}) collective-permute-start(f32[24,128]{1,0:T(8,128)S(1)} %get-tuple-element.41.refs_0_), channel_id=1, source_target_pairs={{0,3},{1,2},{2,1},{3,0},{4,7},{5,6},{6,5},{7,4},{8,11},{9,10},{10,... | collective-permute-start | bytes 36872 | tf_op jit(solution)/shard_map/ppermute | solution.py:444
  21.1 4.6 %collective-permute-start.7 = (f32[24,128]{1,0:T(8,128)S(1)}, f32[24,128]{1,0:T(8,128)S(1)}, u32[]{:S(2)}, u32[]{:S(2)}) collective-permute-start(f32[24,128]{1,0:T(8,128)S(1)} %get-tuple-element.41.refs_0_), channel_id=1, source_target_pairs={{0,2},{1,3},{2,0},{3,1},{4,6},{5,7},{6,4},{7,5},{8,10},{9,11},{10,... | collective-permute-start | bytes 36872 | tf_op jit(solution)/shard_map/ppermute | solution.py:444
  21.8 4.1 %collective-permute-start.6 = (f32[24,128]{1,0:T(8,128)S(1)}, f32[24,128]{1,0:T(8,128)S(1)}, u32[]{:S(2)}, u32[]{:S(2)}) collective-permute-start(f32[24,128]{1,0:T(8,128)S(1)} %get-tuple-element.41.refs_0_), channel_id=1, source_target_pairs={{0,1},{1,0},{2,3},{3,2},{4,5},{5,4},{6,7},{7,6},{8,9},{9,8},{10,11... | collective-permute-start | bytes 36872 | tf_op jit(solution)/shard_map/ppermute | solution.py:444
  26.3 3.3 %collective-permute-start.11 = (f32[24,128]{1,0:T(8,128)S(1)}, f32[24,128]{1,0:T(8,128)S(1)}, u32[]{:S(2)}, u32[]{:S(2)}) collective-permute-start(f32[24,128]{1,0:T(8,128)S(1)} %shard_map.81.refs_0_.refs_4_), channel_id=1, source_target_pairs={{0,12},{4,8},{8,4},{12,0},{1,13},{5,9},{9,5},{13,1},{2,14},{6,10},... | collective-permute-start | bytes 36872 | tf_op jit(solution)/shard_map/ppermute | solution.py:444
  26.4 3.8 %collective-permute-start.10 = (f32[24,128]{1,0:T(8,128)S(1)}, f32[24,128]{1,0:T(8,128)S(1)}, u32[]{:S(2)}, u32[]{:S(2)}) collective-permute-start(f32[24,128]{1,0:T(8,128)S(1)} %shard_map.81.refs_0_.refs_4_), channel_id=1, source_target_pairs={{0,8},{4,12},{8,0},{12,4},{1,9},{5,13},{9,1},{13,5},{2,10},{6,14},... | collective-permute-start | bytes 36872 | tf_op jit(solution)/shard_map/ppermute | solution.py:444
  28.0 2.2 %collective-permute-start.9 = (f32[24,128]{1,0:T(8,128)S(1)}, f32[24,128]{1,0:T(8,128)S(1)}, u32[]{:S(2)}, u32[]{:S(2)}) collective-permute-start(f32[24,128]{1,0:T(8,128)S(1)} %shard_map.81.refs_0_.refs_4_), channel_id=1, source_target_pairs={{0,4},{4,0},{8,12},{12,8},{1,5},{5,1},{9,13},{13,9},{2,6},{6,2},{1... | collective-permute-start | bytes 36872 | tf_op jit(solution)/shard_map/ppermute | solution.py:444
  30.2 10.2 %copy-start = (s32[8192]{0:T(1024)S(1)}, s32[8192]{0:T(1024)}, u32[]{:S(2)}) copy-start(s32[8192]{0:T(1024)} %param.9) | copy-start | bytes 98308
  30.2 10.3 %copy-start.1 = (s32[8192]{0:T(1024)S(1)}, s32[8192]{0:T(1024)}, u32[]{:S(2)}) copy-start(s32[8192]{0:T(1024)} %param.8) | copy-start | bytes 98308
  30.7 5.6 %collective-permute-start.14 = (f32[24,128]{1,0:T(8,128)S(1)}, f32[24,128]{1,0:T(8,128)S(1)}, u32[]{:S(2)}, u32[]{:S(2)}) collective-permute-start(f32[24,128]{1,0:T(8,128)S(1)} %get-tuple-element.48.refs_4_.refs_0_), channel_id=1, source_target_pairs={{0,3},{1,2},{2,1},{3,0},{4,7},{5,6},{6,5},{7,4},{8,11},{9,10},{10,... | collective-permute-start | bytes 36872 | tf_op jit(solution)/shard_map/ppermute | solution.py:444
  33.2 4.6 %collective-permute-start.13 = (f32[24,128]{1,0:T(8,128)S(1)}, f32[24,128]{1,0:T(8,128)S(1)}, u32[]{:S(2)}, u32[]{:S(2)}) collective-permute-start(f32[24,128]{1,0:T(8,128)S(1)} %get-tuple-element.48.refs_4_.refs_0_), channel_id=1, source_target_pairs={{0,2},{1,3},{2,0},{3,1},{4,6},{5,7},{6,4},{7,5},{8,10},{9,11},{10,... | collective-permute-start | bytes 36872 | tf_op jit(solution)/shard_map/ppermute | solution.py:444
  34.1 3.8 %collective-permute-start.12 = (f32[24,128]{1,0:T(8,128)S(1)}, f32[24,128]{1,0:T(8,128)S(1)}, u32[]{:S(2)}, u32[]{:S(2)}) collective-permute-start(f32[24,128]{1,0:T(8,128)S(1)} %get-tuple-element.48.refs_4_.refs_0_), channel_id=1, source_target_pairs={{0,1},{1,0},{2,3},{3,2},{4,5},{5,4},{6,7},{7,6},{8,9},{9,8},{10,11... | collective-permute-start | bytes 36872 | tf_op jit(solution)/shard_map/ppermute | solution.py:444
  38.4 3.3 %collective-permute-start.17 = (f32[24,128]{1,0:T(8,128)S(1)}, f32[24,128]{1,0:T(8,128)S(1)}, u32[]{:S(2)}, u32[]{:S(2)}) collective-permute-start(f32[24,128]{1,0:T(8,128)S(1)} %shard_map.84.refs_0_), channel_id=1, source_target_pairs={{0,12},{4,8},{8,4},{12,0},{1,13},{5,9},{9,5},{13,1},{2,14},{6,10},... | collective-permute-start | bytes 36872 | tf_op jit(solution)/shard_map/ppermute | solution.py:444
  38.5 3.8 %collective-permute-start.16 = (f32[24,128]{1,0:T(8,128)S(1)}, f32[24,128]{1,0:T(8,128)S(1)}, u32[]{:S(2)}, u32[]{:S(2)}) collective-permute-start(f32[24,128]{1,0:T(8,128)S(1)} %shard_map.84.refs_0_), channel_id=1, source_target_pairs={{0,8},{4,12},{8,0},{12,4},{1,9},{5,13},{9,1},{13,5},{2,10},{6,14},... | collective-permute-start | bytes 36872 | tf_op jit(solution)/shard_map/ppermute | solution.py:444
  40.0 2.2 %collective-permute-start.15 = (f32[24,128]{1,0:T(8,128)S(1)}, f32[24,128]{1,0:T(8,128)S(1)}, u32[]{:S(2)}, u32[]{:S(2)}) collective-permute-start(f32[24,128]{1,0:T(8,128)S(1)} %shard_map.84.refs_0_), channel_id=1, source_target_pairs={{0,4},{4,0},{8,12},{12,8},{1,5},{5,1},{9,13},{13,9},{2,6},{6,2},{1... | collective-permute-start | bytes 36872 | tf_op jit(solution)/shard_map/ppermute | solution.py:444

commit v7 on v6

--- a/solution.py
+++ b/solution.py
@@ -414,8 +414,15 @@
 
 
 def item_out_kernel(axis, devices, slots, *refs):
-    base, numbers, out, packs_here = refs[devices:]
-    packs = in_order(axis, devices, refs[:devices], packs_here)
+    base, numbers, out = refs[devices:]
+    given = [pack[...] for pack in refs[:devices]]
+    owners = owners_of(axis, devices)
+    packs = []
+    for device in range(devices):
+        chosen = given[0]
+        for step in range(1, devices):
+            chosen = jnp.where(owners[step] == device, given[step], chosen)
+        packs.append(chosen)
     groups = base.shape[0] // BLOCKS
     chosen = load_masks(numbers, devices, slots)
     for block in range(BLOCKS):
@@ -554,7 +561,6 @@
             bind(item_out_kernel, "user", n_user, slots),
             jax.ShapeDtypeStruct(item_counts.shape, jnp.float32),
             (*item_packs[-1], base, named),
-            scratch=[near((n_user, *shape))],
         )
         return user_values.reshape(-1), item_values.reshape(-1)
 

time: 43.1 us -> 43.1 us (level)
  no operation moved by 1% of the time
where the time goes in v7:
time: 43.1 us; the launch traced here: 43 us
  starting transfers between devices  20.5 us (48%)
  waiting for transfers between devices  12.3 us (29%)
  Pallas kernels  8.84 us (21%)
  between operations  1.36 us (3%)
    ppermute x18, starting transfers between devices, exchange(): packs.append(keep(lax.ppermute(pack, axis, route)))  20.5 us
    ppermute x18, waiting for transfers between devices, exchange(): packs.append(keep(lax.ppermute(pack, axis, route)))  12.3 us
    pallas_call x10, Pallas kernels, call(): pl.pallas_call(kernel, out_shape=outs, in_specs=specs or [HERE] * len(ope...  8.84 us
  transfers between devices with their start and end apart: 18, of which 13 were waited for; matrix products, arithmetic and copies ran while one was open for 0% of the time, Pallas kernels for 5%

profile of v7, /device:TPU:0, one launch (start us, length us, event | category | flops | bytes accessed | tf_op | source)
XLA Modules:
  0.0 43.0 jit_solution(236066451477901126)
XLA Ops:
  1.3 2.9 %shard_map.77 = (f32[24,128]{1,0:T(8,128)S(1)}, bf16[5,512,128]{2,1,0:T(8,128)(2,1)S(1)}, bf16[5,512,128]{2,1,0:T(8,128)(2,1)S(1)}) custom-call(s32[2,5]{1,0:T(2,128)} %bitcast.14, s32[1,1]{1,0:T(1,128)S(6)} %copy.8.refs_1_, bf16[8192,128]{1,0:T(8,128)(2,1)} %refs_2_.1, bf16[8192,128]{1,0:T(8,128)(2,1)} %refs_3_.1, s32[64,128]{1,0:T(8,128)} %bitcast.7), custom_call_target="tpu_custom_call" | custom-call | tf_op jit(solution)/shard_map/pallas_call | solution.py:456
  4.2 5.1 %collective-permute-start.2 = (f32[24,128]{1,0:T(8,128)S(1)}, f32[24,128]{1,0:T(8,128)S(1)}, u32[]{:S(2)}, u32[]{:S(2)}) collective-permute-start(f32[24,128]{1,0:T(8,128)S(1)} %get-tuple-element.27.refs_0_), channel_id=1, source_target_pairs={{0,3},{1,2},{2,1},{3,0},{4,7},{5,6},{6,5},{7,4},{8,11},{9,10},{10,... | collective-permute-start | bytes 36872 | tf_op jit(solution)/shard_map/ppermute | solution.py:451
  9.3 0.0 collective-permute-start.1
  9.3 0.6 %collective-permute-start = (f32[24,128]{1,0:T(8,128)S(1)}, f32[24,128]{1,0:T(8,128)S(1)}, u32[]{:S(2)}, u32[]{:S(2)}) collective-permute-start(f32[24,128]{1,0:T(8,128)S(1)} %get-tuple-element.27.refs_0_), channel_id=1, source_target_pairs={{0,1},{1,0},{2,3},{3,2},{4,5},{5,4},{6,7},{7,6},{8,9},{9,8},{10,11... | collective-permute-start | bytes 36872 | tf_op jit(solution)/shard_map/ppermute | solution.py:451
  10.0 1.0 %shard_map.78 = (f32[5,512,512]{2,1,0:T(8,128)S(1)}, f32[8,512]{1,0:T(8,128)S(1)}, f32[8,512]{1,0:T(8,128)S(1)}, s32[8,128]{1,0:T(8,128)S(1)}, s32[8,128]{1,0:T(...) custom-call(s32[2,5]{1,0:T(2,128)} %bitcast.15, ...), custom_call_target="tpu_custom_call" | custom-call | tf_op jit(solution)/shard_map/pallas_call | solution.py:456
  11.0 0.0 collective-permute-done.2.refs_3_
  11.0 2.9 %collective-permute-done.1.refs_2_ = f32[24,128]{1,0:T(8,128)S(1)} collective-permute-done((f32[24,128]{1,0:T(8,128)S(1)}, f32[24,128]{1,0:T(8,128)S(1)}, u32[]{:S(2)}, u32[]{:S(2)}) %collective-permute-start.1) | collective-permute-done | bytes 12320 | tf_op jit(solution)/shard_map/ppermute | solution.py:451
  13.9 0.0 collective-permute-done.refs_1_
  13.9 1.3 %shard_map.79 = (f32[24,128]{1,0:T(8,128)S(1)}, f32[5,512,512]{2,1,0:T(8,128)S(1)}, f32[8,512]{1,0:T(8,128)S(1)}, f32[20,8,128]{2,1,0:T(8,128)S(1)}, f32[8,128]{1,0:T(8,128)S(1)}) custom-call(f32[24,128]{1,0:T(8,128)S(1)} %get-tuple-element.27.refs_0_, f32[24,128]{1,0:T(8,128)S(1)} %collective-permute-done.refs_1_, ...), custom_call_target="tpu_custom_call" | custom-call | tf_op jit(solution)/shard_map/pallas_call | solution.py:456
  15.2 0.1 collective-permute-start.5
  15.3 1.6 %collective-permute-start.4 = (f32[24,128]{1,0:T(8,128)S(1)}, f32[24,128]{1,0:T(8,128)S(1)}, u32[]{:S(2)}, u32[]{:S(2)}) collective-permute-start(f32[24,128]{1,0:T(8,128)S(1)} %get-tuple-element.35.refs_0_), channel_id=1, source_target_pairs={{0,8},{4,12},{8,0},{12,4},{1,9},{5,13},{9,1},{13,5},{2,10},{6,14},... | collective-permute-start | bytes 36872 | tf_op jit(solution)/shard_map/ppermute | solution.py:451
  16.8 0.3 collective-permute-start.3
  17.1 1.3 %collective-permute-done.5.refs_3_ = f32[24,128]{1,0:T(8,128)S(1)} collective-permute-done((f32[24,128]{1,0:T(8,128)S(1)}, f32[24,128]{1,0:T(8,128)S(1)}, u32[]{:S(2)}, u32[]{:S(2)}) %collective-permute-start.5) | collective-permute-done | bytes 12320 | tf_op jit(solution)/shard_map/ppermute | solution.py:451
  18.5 0.6 %collective-permute-done.4.refs_2_ = f32[24,128]{1,0:T(8,128)S(1)} collective-permute-done((f32[24,128]{1,0:T(8,128)S(1)}, f32[24,128]{1,0:T(8,128)S(1)}, u32[]{:S(2)}, u32[]{:S(2)}) %collective-permute-start.4) | collective-permute-done | bytes 12320 | tf_op jit(solution)/shard_map/ppermute | solution.py:451
  19.0 0.0 collective-permute-done.3.refs_1_
  19.0 0.6 %shard_map.80 = (f32[24,128]{1,0:T(8,128)S(1)}, f32[8,512]{1,0:T(8,128)S(1)}, f32[20,8,128]{2,1,0:T(8,128)S(1)}, f32[8,128]{1,0:T(8,128)S(1)}) custom-call(f32[24,128]{1,0:T(8,128)S(1)} %get-tuple-element.35.refs_0_, f32[24,128]{1,0:T(8,128)S(1)} %collective-permute-done.3.refs_1_, f32[24,128]{1,0:T(8,128)S(1)} %collective-permute-done.4.refs_2_, ...), custom_call_target="tpu_custom_call" | custom-call | tf_op jit(solution)/shard_map/pallas_call | solution.py:456
  19.6 1.5 %collective-permute-start.8 = (f32[24,128]{1,0:T(8,128)S(1)}, f32[24,128]{1,0:T(8,128)S(1)}, u32[]{:S(2)}, u32[]{:S(2)}) collective-permute-start(f32[24,128]{1,0:T(8,128)S(1)} %get-tuple-element.41.refs_0_), channel_id=1, source_target_pairs={{0,3},{1,2},{2,1},{3,0},{4,7},{5,6},{6,5},{7,4},{8,11},{9,10},{10,... | collective-permute-start | bytes 36872 | tf_op jit(solution)/shard_map/ppermute | solution.py:451
  21.1 0.6 %collective-permute-start.7 = (f32[24,128]{1,0:T(8,128)S(1)}, f32[24,128]{1,0:T(8,128)S(1)}, u32[]{:S(2)}, u32[]{:S(2)}) collective-permute-start(f32[24,128]{1,0:T(8,128)S(1)} %get-tuple-element.41.refs_0_), channel_id=1, source_target_pairs={{0,2},{1,3},{2,0},{3,1},{4,6},{5,7},{6,4},{7,5},{8,10},{9,11},{10,... | collective-permute-start | bytes 36872 | tf_op jit(solution)/shard_map/ppermute | solution.py:451
  21.8 2.3 %collective-permute-start.6 = (f32[24,128]{1,0:T(8,128)S(1)}, f32[24,128]{1,0:T(8,128)S(1)}, u32[]{:S(2)}, u32[]{:S(2)}) collective-permute-start(f32[24,128]{1,0:T(8,128)S(1)} %get-tuple-element.41.refs_0_), channel_id=1, source_target_pairs={{0,1},{1,0},{2,3},{3,2},{4,5},{5,4},{6,7},{7,6},{8,9},{9,8},{10,11... | collective-permute-start | bytes 36872 | tf_op jit(solution)/shard_map/ppermute | solution.py:451
  24.1 1.1 %collective-permute-done.8.refs_3_ = f32[24,128]{1,0:T(8,128)S(1)} collective-permute-done((f32[24,128]{1,0:T(8,128)S(1)}, f32[24,128]{1,0:T(8,128)S(1)}, u32[]{:S(2)}, u32[]{:S(2)}) %collective-permute-start.8) | collective-permute-done | bytes 12320 | tf_op jit(solution)/shard_map/ppermute | solution.py:451
  25.2 0.6 %collective-permute-done.7.refs_2_ = f32[24,128]{1,0:T(8,128)S(1)} collective-permute-done((f32[24,128]{1,0:T(8,128)S(1)}, f32[24,128]{1,0:T(8,128)S(1)}, u32[]{:S(2)}, u32[]{:S(2)}) %collective-permute-start.7) | collective-permute-done | bytes 12320 | tf_op jit(solution)/shard_map/ppermute | solution.py:451
  25.7 0.1 collective-permute-done.6.refs_1_
  25.9 0.5 %shard_map.81.refs_0_.refs_4_ = f32[24,128]{1,0:T(8,128)S(1)} custom-call(f32[24,128]{1,0:T(8,128)S(1)} %get-tuple-element.41.refs_0_, f32[24,128]{1,0:T(8,128)S(1)} %collective-permute-done.6.refs_1_, f32[24,128]{1,0:T(8,128)S(1)} %collective-permute-done.7.refs_2_, f32[24,128]{1,0:T(8,128)S(1)} %collective-permute-done.8.refs_3_, ...), custom_call_target="tpu_custom_call" | custom-call | tf_op jit(solution)/shard_map/pallas_call | solution.py:456
  26.3 0.1 collective-permute-start.11
  26.4 1.5 %collective-permute-start.10 = (f32[24,128]{1,0:T(8,128)S(1)}, f32[24,128]{1,0:T(8,128)S(1)}, u32[]{:S(2)}, u32[]{:S(2)}) collective-permute-start(f32[24,128]{1,0:T(8,128)S(1)} %shard_map.81.refs_0_.refs_4_), channel_id=1, source_target_pairs={{0,8},{4,12},{8,0},{12,4},{1,9},{5,13},{9,1},{13,5},{2,10},{6,14},... | collective-permute-start | bytes 36872 | tf_op jit(solution)/shard_map/ppermute | solution.py:451
  28.0 0.3 collective-permute-start.9
  28.3 1.4 %collective-permute-done.11.refs_3_.refs_7_ = f32[24,128]{1,0:T(8,128)S(1)} collective-permute-done((f32[24,128]{1,0:T(8,128)S(1)}, f32[24,128]{1,0:T(8,128)S(1)}, u32[]{:S(2)}, u32[]{:S(2)}) %collective-permute-start.11) | collective-permute-done | bytes 12320 | tf_op jit(solution)/shard_map/ppermute | solution.py:451
  29.6 0.6 %collective-permute-done.10.refs_2_.refs_6_ = f32[24,128]{1,0:T(8,128)S(1)} collective-permute-done((f32[24,128]{1,0:T(8,128)S(1)}, f32[24,128]{1,0:T(8,128)S(1)}, u32[]{:S(2)}, u32[]{:S(2)}) %collective-permute-start.10) | collective-permute-done | bytes 12320 | tf_op jit(solution)/shard_map/ppermute | solution.py:451
  30.2 0.0 collective-permute-done.9.refs_1_.refs_5_
  30.2 0.5 %shard_map.82 = (f32[24,128]{1,0:T(8,128)S(1)}, f32[8,512]{1,0:T(8,128)S(1)}) custom-call(f32[24,128]{1,0:T(8,128)S(1)} %shard_map.81.refs_0_.refs_4_, f32[24,128]{1,0:T(8,128)S(1)} %collective-permute-done.9.refs_1_.refs_5_, f32[24,128]{1,0:T(8,128)S(1)} %collective-permute-done.10.refs_2_.refs_6_, f32[24,128]{1,0:T(8,128)S(1)} %collective-permute-done.11.refs_3_.refs_7_, ...), custom_call_target="tpu_custom_call" | custom-call | tf_op jit(solution)/shard_map/pallas_call | solution.py:456
  30.7 2.5 %collective-permute-start.14 = (f32[24,128]{1,0:T(8,128)S(1)}, f32[24,128]{1,0:T(8,128)S(1)}, u32[]{:S(2)}, u32[]{:S(2)}) collective-permute-start(f32[24,128]{1,0:T(8,128)S(1)} %get-tuple-element.48.refs_4_.refs_0_), channel_id=1, source_target_pairs={{0,3},{1,2},{2,1},{3,0},{4,7},{5,6},{6,5},{7,4},{8,11},{9,10},{10,... | collective-permute-start | bytes 36872 | tf_op jit(solution)/shard_map/ppermute | solution.py:451
  33.2 0.9 %collective-permute-start.13 = (f32[24,128]{1,0:T(8,128)S(1)}, f32[24,128]{1,0:T(8,128)S(1)}, u32[]{:S(2)}, u32[]{:S(2)}) collective-permute-start(f32[24,128]{1,0:T(8,128)S(1)} %get-tuple-element.48.refs_4_.refs_0_), channel_id=1, source_target_pairs={{0,2},{1,3},{2,0},{3,1},{4,6},{5,7},{6,4},{7,5},{8,10},{9,11},{10,... | collective-permute-start | bytes 36872 | tf_op jit(solution)/shard_map/ppermute | solution.py:451
  34.1 1.0 %collective-permute-start.12 = (f32[24,128]{1,0:T(8,128)S(1)}, f32[24,128]{1,0:T(8,128)S(1)}, u32[]{:S(2)}, u32[]{:S(2)}) collective-permute-start(f32[24,128]{1,0:T(8,128)S(1)} %get-tuple-element.48.refs_4_.refs_0_), channel_id=1, source_target_pairs={{0,1},{1,0},{2,3},{3,2},{4,5},{5,4},{6,7},{7,6},{8,9},{9,8},{10,11... | collective-permute-start | bytes 36872 | tf_op jit(solution)/shard_map/ppermute | solution.py:451
  35.1 1.1 %collective-permute-done.14.refs_7_.refs_3_ = f32[24,128]{1,0:T(8,128)S(1)} collective-permute-done((f32[24,128]{1,0:T(8,128)S(1)}, f32[24,128]{1,0:T(8,128)S(1)}, u32[]{:S(2)}, u32[]{:S(2)}) %collective-permute-start.14) | collective-permute-done | bytes 12320 | tf_op jit(solution)/shard_map/ppermute | solution.py:451
  36.3 1.5 %collective-permute-done.13.refs_6_.refs_2_ = f32[24,128]{1,0:T(8,128)S(1)} collective-permute-done((f32[24,128]{1,0:T(8,128)S(1)}, f32[24,128]{1,0:T(8,128)S(1)}, u32[]{:S(2)}, u32[]{:S(2)}) %collective-permute-start.13) | collective-permute-done | bytes 12320 | tf_op jit(solution)/shard_map/ppermute | solution.py:451
  37.8 0.1 collective-permute-done.12.refs_5_.refs_1_
  37.9 0.5 %shard_map.84.refs_0_ = f32[24,128]{1,0:T(8,128)S(1)} custom-call(f32[24,128]{1,0:T(8,128)S(1)} %get-tuple-element.48.refs_4_.refs_0_, f32[24,128]{1,0:T(8,128)S(1)} %collective-permute-done.12.refs_5_.refs_1_, f32[24,128]{1,0:T(8,128)S(1)} %collective-permute-done.13.refs_6_.refs_2_, f32[24,128]{1,0:T(8,128)S(1)} %collective-permute-done.14.refs_7_.refs_3_, ...), custom_call_target="tpu_custom_call" | custom-call | tf_op jit(solution)/shard_map/pallas_call | solution.py:456
  38.4 0.1 collective-permute-start.17
  38.5 1.5 %collective-permute-start.16 = (f32[24,128]{1,0:T(8,128)S(1)}, f32[24,128]{1,0:T(8,128)S(1)}, u32[]{:S(2)}, u32[]{:S(2)}) collective-permute-start(f32[24,128]{1,0:T(8,128)S(1)} %shard_map.84.refs_0_), channel_id=1, source_target_pairs={{0,8},{4,12},{8,0},{12,4},{1,9},{5,13},{9,1},{13,5},{2,10},{6,14},... | collective-permute-start | bytes 36872 | tf_op jit(solution)/shard_map/ppermute | solution.py:451
  40.0 0.3 collective-permute-start.15
  40.3 0.0 copy-done
  40.3 0.2 shard_map.85
  40.5 0.0 copy-done.1
  40.5 0.8 %shard_map.83 = f32[64,128]{1,0:T(8,128)} custom-call(f32[24,128]{1,0:T(8,128)S(1)} %get-tuple-element.27.refs_0_, f32[24,128]{1,0:T(8,128)S(1)} %collective-permute-done.refs_1_, f32[24,128]{1,0:T(8,128)S(1)} %collective-permute-done.1.refs_2_, f32[24,128]{1,0:T(8,128)S(1)} %collective-permute-done.2.refs_3_, ...), custom_call_target="tpu_custom_call" | custom-call | tf_op jit(solution)/shard_map/pallas_call | solution.py:456
  41.3 0.4 collective-permute-done.17.refs_3_
  41.7 0.5 %collective-permute-done.16.refs_2_ = f32[24,128]{1,0:T(8,128)S(1)} collective-permute-done((f32[24,128]{1,0:T(8,128)S(1)}, f32[24,128]{1,0:T(8,128)S(1)}, u32[]{:S(2)}, u32[]{:S(2)}) %collective-permute-start.16) | collective-permute-done | bytes 12320 | tf_op jit(solution)/shard_map/ppermute | solution.py:451
  42.3 0.0 collective-permute-done.15.refs_1_
  42.3 0.7 %shard_map.86 = f32[64,128]{1,0:T(8,128)} custom-call(f32[24,128]{1,0:T(8,128)S(1)} %shard_map.84.refs_0_, f32[24,128]{1,0:T(8,128)S(1)} %collective-permute-done.15.refs_1_, f32[24,128]{1,0:T(8,128)S(1)} %collective-permute-done.16.refs_2_, f32[24,128]{1,0:T(8,128)S(1)} %collective-permute-done.17.refs_3_, f32[64,128]{1,0:T(8,128)S(1)} %get-tuple-element.50.refs_4_, ...), custom_call_target="tpu_custom_call" | custom-call | tf_op jit(solution)/shard_map/pallas_call | solution.py:456
  (2 shorter events, 0.0 us)
Async XLA Ops:
  4.2 6.8 %collective-permute-start.2 = (f32[24,128]{1,0:T(8,128)S(1)}, f32[24,128]{1,0:T(8,128)S(1)}, u32[]{:S(2)}, u32[]{:S(2)}) collective-permute-start(f32[24,128]{1,0:T(8,128)S(1)} %get-tuple-element.27.refs_0_), channel_id=1, source_target_pairs={{0,3},{1,2},{2,1},{3,0},{4,7},{5,6},{6,5},{7,4},{8,11},{9,10},{10,... | collective-permute-start | bytes 36872 | tf_op jit(solution)/shard_map/ppermute | solution.py:451
  9.3 4.6 %collective-permute-start.1 = (f32[24,128]{1,0:T(8,128)S(1)}, f32[24,128]{1,0:T(8,128)S(1)}, u32[]{:S(2)}, u32[]{:S(2)}) collective-permute-start(f32[24,128]{1,0:T(8,128)S(1)} %get-tuple-element.27.refs_0_), channel_id=1, source_target_pairs={{0,2},{1,3},{2,0},{3,1},{4,6},{5,7},{6,4},{7,5},{8,10},{9,11},{10,... | collective-permute-start | bytes 36872 | tf_op jit(solution)/shard_map/ppermute | solution.py:451
  9.3 4.6 %collective-permute-start = (f32[24,128]{1,0:T(8,128)S(1)}, f32[24,128]{1,0:T(8,128)S(1)}, u32[]{:S(2)}, u32[]{:S(2)}) collective-permute-start(f32[24,128]{1,0:T(8,128)S(1)} %get-tuple-element.27.refs_0_), channel_id=1, source_target_pairs={{0,1},{1,0},{2,3},{3,2},{4,5},{5,4},{6,7},{7,6},{8,9},{9,8},{10,11... | collective-permute-start | bytes 36872 | tf_op jit(solution)/shard_map/ppermute | solution.py:451
  15.2 3.3 %collective-permute-start.5 = (f32[24,128]{1,0:T(8,128)S(1)}, f32[24,128]{1,0:T(8,128)S(1)}, u32[]{:S(2)}, u32[]{:S(2)}) collective-permute-start(f32[24,128]{1,0:T(8,128)S(1)} %get-tuple-element.35.refs_0_), channel_id=1, source_target_pairs={{0,12},{4,8},{8,4},{12,0},{1,13},{5,9},{9,5},{13,1},{2,14},{6,10},... | collective-permute-start | bytes 36872 | tf_op jit(solution)/shard_map/ppermute | solution.py:451
  15.3 3.8 %collective-permute-start.4 = (f32[24,128]{1,0:T(8,128)S(1)}, f32[24,128]{1,0:T(8,128)S(1)}, u32[]{:S(2)}, u32[]{:S(2)}) collective-permute-start(f32[24,128]{1,0:T(8,128)S(1)} %get-tuple-element.35.refs_0_), channel_id=1, source_target_pairs={{0,8},{4,12},{8,0},{12,4},{1,9},{5,13},{9,1},{13,5},{2,10},{6,14},... | collective-permute-start | bytes 36872 | tf_op jit(solution)/shard_map/ppermute | solution.py:451
  16.8 2.2 %collective-permute-start.3 = (f32[24,128]{1,0:T(8,128)S(1)}, f32[24,128]{1,0:T(8,128)S(1)}, u32[]{:S(2)}, u32[]{:S(2)}) collective-permute-start(f32[24,128]{1,0:T(8,128)S(1)} %get-tuple-element.35.refs_0_), channel_id=1, source_target_pairs={{0,4},{4,0},{8,12},{12,8},{1,5},{5,1},{9,13},{13,9},{2,6},{6,2},{1... | collective-permute-start | bytes 36872 | tf_op jit(solution)/shard_map/ppermute | solution.py:451
  19.6 5.6 %collective-permute-start.8 = (f32[24,128]{1,0:T(8,128)S(1)}, f32[24,128]{1,0:T(8,128)S(1)}, u32[]{:S(2)}, u32[]{:S(2)}) collective-permute-start(f32[24,128]{1,0:T(8,128)S(1)} %get-tuple-element.41.refs_0_), channel_id=1, source_target_pairs={{0,3},{1,2},{2,1},{3,0},{4,7},{5,6},{6,5},{7,4},{8,11},{9,10},{10,... | collective-permute-start | bytes 36872 | tf_op jit(solution)/shard_map/ppermute | solution.py:451
  21.1 4.6 %collective-permute-start.7 = (f32[24,128]{1,0:T(8,128)S(1)}, f32[24,128]{1,0:T(8,128)S(1)}, u32[]{:S(2)}, u32[]{:S(2)}) collective-permute-start(f32[24,128]{1,0:T(8,128)S(1)} %get-tuple-element.41.refs_0_), channel_id=1, source_target_pairs={{0,2},{1,3},{2,0},{3,1},{4,6},{5,7},{6,4},{7,5},{8,10},{9,11},{10,... | collective-permute-start | bytes 36872 | tf_op jit(solution)/shard_map/ppermute | solution.py:451
  21.8 4.1 %collective-permute-start.6 = (f32[24,128]{1,0:T(8,128)S(1)}, f32[24,128]{1,0:T(8,128)S(1)}, u32[]{:S(2)}, u32[]{:S(2)}) collective-permute-start(f32[24,128]{1,0:T(8,128)S(1)} %get-tuple-element.41.refs_0_), channel_id=1, source_target_pairs={{0,1},{1,0},{2,3},{3,2},{4,5},{5,4},{6,7},{7,6},{8,9},{9,8},{10,11... | collective-permute-start | bytes 36872 | tf_op jit(solution)/shard_map/ppermute | solution.py:451
  26.3 3.3 %collective-permute-start.11 = (f32[24,128]{1,0:T(8,128)S(1)}, f32[24,128]{1,0:T(8,128)S(1)}, u32[]{:S(2)}, u32[]{:S(2)}) collective-permute-start(f32[24,128]{1,0:T(8,128)S(1)} %shard_map.81.refs_0_.refs_4_), channel_id=1, source_target_pairs={{0,12},{4,8},{8,4},{12,0},{1,13},{5,9},{9,5},{13,1},{2,14},{6,10},... | collective-permute-start | bytes 36872 | tf_op jit(solution)/shard_map/ppermute | solution.py:451
  26.4 3.8 %collective-permute-start.10 = (f32[24,128]{1,0:T(8,128)S(1)}, f32[24,128]{1,0:T(8,128)S(1)}, u32[]{:S(2)}, u32[]{:S(2)}) collective-permute-start(f32[24,128]{1,0:T(8,128)S(1)} %shard_map.81.refs_0_.refs_4_), channel_id=1, source_target_pairs={{0,8},{4,12},{8,0},{12,4},{1,9},{5,13},{9,1},{13,5},{2,10},{6,14},... | collective-permute-start | bytes 36872 | tf_op jit(solution)/shard_map/ppermute | solution.py:451
  28.0 2.2 %collective-permute-start.9 = (f32[24,128]{1,0:T(8,128)S(1)}, f32[24,128]{1,0:T(8,128)S(1)}, u32[]{:S(2)}, u32[]{:S(2)}) collective-permute-start(f32[24,128]{1,0:T(8,128)S(1)} %shard_map.81.refs_0_.refs_4_), channel_id=1, source_target_pairs={{0,4},{4,0},{8,12},{12,8},{1,5},{5,1},{9,13},{13,9},{2,6},{6,2},{1... | collective-permute-start | bytes 36872 | tf_op jit(solution)/shard_map/ppermute | solution.py:451
  30.2 10.2 %copy-start = (s32[8192]{0:T(1024)S(1)}, s32[8192]{0:T(1024)}, u32[]{:S(2)}) copy-start(s32[8192]{0:T(1024)} %param.9) | copy-start | bytes 98308
  30.2 10.3 %copy-start.1 = (s32[8192]{0:T(1024)S(1)}, s32[8192]{0:T(1024)}, u32[]{:S(2)}) copy-start(s32[8192]{0:T(1024)} %param.8) | copy-start | bytes 98308
  30.7 5.6 %collective-permute-start.14 = (f32[24,128]{1,0:T(8,128)S(1)}, f32[24,128]{1,0:T(8,128)S(1)}, u32[]{:S(2)}, u32[]{:S(2)}) collective-permute-start(f32[24,128]{1,0:T(8,128)S(1)} %get-tuple-element.48.refs_4_.refs_0_), channel_id=1, source_target_pairs={{0,3},{1,2},{2,1},{3,0},{4,7},{5,6},{6,5},{7,4},{8,11},{9,10},{10,... | collective-permute-start | bytes 36872 | tf_op jit(solution)/shard_map/ppermute | solution.py:451
  33.2 4.6 %collective-permute-start.13 = (f32[24,128]{1,0:T(8,128)S(1)}, f32[24,128]{1,0:T(8,128)S(1)}, u32[]{:S(2)}, u32[]{:S(2)}) collective-permute-start(f32[24,128]{1,0:T(8,128)S(1)} %get-tuple-element.48.refs_4_.refs_0_), channel_id=1, source_target_pairs={{0,2},{1,3},{2,0},{3,1},{4,6},{5,7},{6,4},{7,5},{8,10},{9,11},{10,... | collective-permute-start | bytes 36872 | tf_op jit(solution)/shard_map/ppermute | solution.py:451
  34.1 3.8 %collective-permute-start.12 = (f32[24,128]{1,0:T(8,128)S(1)}, f32[24,128]{1,0:T(8,128)S(1)}, u32[]{:S(2)}, u32[]{:S(2)}) collective-permute-start(f32[24,128]{1,0:T(8,128)S(1)} %get-tuple-element.48.refs_4_.refs_0_), channel_id=1, source_target_pairs={{0,1},{1,0},{2,3},{3,2},{4,5},{5,4},{6,7},{7,6},{8,9},{9,8},{10,11... | collective-permute-start | bytes 36872 | tf_op jit(solution)/shard_map/ppermute | solution.py:451
  38.4 3.3 %collective-permute-start.17 = (f32[24,128]{1,0:T(8,128)S(1)}, f32[24,128]{1,0:T(8,128)S(1)}, u32[]{:S(2)}, u32[]{:S(2)}) collective-permute-start(f32[24,128]{1,0:T(8,128)S(1)} %shard_map.84.refs_0_), channel_id=1, source_target_pairs={{0,12},{4,8},{8,4},{12,0},{1,13},{5,9},{9,5},{13,1},{2,14},{6,10},... | collective-permute-start | bytes 36872 | tf_op jit(solution)/shard_map/ppermute | solution.py:451
  38.5 3.8 %collective-permute-start.16 = (f32[24,128]{1,0:T(8,128)S(1)}, f32[24,128]{1,0:T(8,128)S(1)}, u32[]{:S(2)}, u32[]{:S(2)}) collective-permute-start(f32[24,128]{1,0:T(8,128)S(1)} %shard_map.84.refs_0_), channel_id=1, source_target_pairs={{0,8},{4,12},{8,0},{12,4},{1,9},{5,13},{9,1},{13,5},{2,10},{6,14},... | collective-permute-start | bytes 36872 | tf_op jit(solution)/shard_map/ppermute | solution.py:451
  40.0 2.2 %collective-permute-start.15 = (f32[24,128]{1,0:T(8,128)S(1)}, f32[24,128]{1,0:T(8,128)S(1)}, u32[]{:S(2)}, u32[]{:S(2)}) collective-permute-start(f32[24,128]{1,0:T(8,128)S(1)} %shard_map.84.refs_0_), channel_id=1, source_target_pairs={{0,4},{4,0},{8,12},{12,8},{1,5},{5,1},{9,13},{13,9},{2,6},{6,2},{1... | collective-permute-start | bytes 36872 | tf_op jit(solution)/shard_map/ppermute | solution.py:451
